TPU v7x, 32 devices: a whole 2x2x4 slice. The times are simulated.
32 devices in a mesh: shot: 8 (over z, x), freq: 4 (over y, core).
Axes of the slice: x: 2, y: 2, z: 4, core: 2. Of those that a mesh axis runs over, the one named last changes fastest.
Arguments:
- data: bfloat16 [4, 2, 1024, 8192], P('freq', None, 'shot'), may hold values from -6 to 6
- primaries: bfloat16 [4, 2, 1024, 640], P('freq', None, 'shot'), may hold values from -0.15625 to 0.15625
- wavelet: float32 [4, 2], P('freq'), may hold values from 2 to 8
- cover_ids: int32 [1024, 8], P('shot'), may hold values from 0 to 15, all different within a row
- cover_counts: int32 [1024], P('shot'), may hold values from 1 to 8
Outputs:
- misfit: bfloat16 [4, 2, 1024, 8192], P('freq', None, 'shot')
- grad_primaries: float32 [4, 2, 1024, 640], P('freq', None, 'shot')
- wavelet_grad: float32 [128], replicated
Inputs may be any that keep to these rules, and one draw needn't show every extreme that they name: `cover_ids`: the entries of a shot's list are different coverage blocks.
All inputs are finite; a program needn't handle non-finite values.
Results may differ from a plain program's by a relative error of at most 0.0013.
Values may be sent and summed in bfloat16 or wider, within the bound.
No kernel may reach another device: no remote copies, remote signals or barrier semaphores. Data moves between devices by JAX's collectives and lax.ppermute only.
A program may use at most 128 MiB of HBM per device.

v0:
```python
import math

import jax
import jax.numpy as jnp
from jax import lax
from jax.sharding import PartitionSpec as P

RB = 512
NT = 128


def passed_along(block, axis, distance):
    devices = range(lax.axis_size(axis))
    route = [(i - distance, i) for i in devices if i - distance in devices]
    return lax.ppermute(block, axis, route)


def on_device(data, primaries, wavelet, cover_ids, cover_counts):
    own_rows = data[0]
    rows_dev = own_rows.shape[1]
    width = own_rows.shape[2]
    band_width = primaries.shape[3]
    reach_blocks = (band_width // rows_dev - 1) // 2
    shot_count = lax.axis_size("shot") * rows_dev
    stride_cols = width // shot_count
    position = lax.axis_index("shot")
    freq_index = lax.axis_index("freq")
    lower_rows = [
        passed_along(own_rows, "shot", distance) for distance in range(reach_blocks, 0, -1)
    ]
    upper_rows = [
        passed_along(own_rows, "shot", -distance) for distance in range(1, reach_blocks + 1)
    ]
    nearby = jnp.concatenate(lower_rows + [own_rows] + upper_rows, axis=1)
    first_row = (position - reach_blocks) * rows_dev
    shot_ids = first_row + jnp.arange(band_width, dtype=jnp.int32)
    columns = jnp.arange(width, dtype=jnp.int32)
    direct_hit = columns[None, :] == shot_ids[:, None] * stride_cols
    wave_re = wavelet[0, 0]
    wave_im = wavelet[0, 1]
    operand = jnp.stack(
        [
            jnp.where(direct_hit, wave_re, 0.0) - nearby[0].astype(jnp.float32),
            jnp.where(direct_hit, wave_im, 0.0) - nearby[1].astype(jnp.float32),
        ]
    ).astype(jnp.bfloat16)
    response = primaries[0]
    response_pair = jnp.stack(
        [jnp.stack([response[0], -response[1]]), jnp.stack([response[1], response[0]])]
    )
    predicted = jnp.einsum(
        "gcik,ckj->gij", response_pair, operand, preferred_element_type=jnp.float32
    )
    block_ids = jnp.arange(width // RB, dtype=jnp.int32)
    listed = jnp.arange(cover_ids.shape[1], dtype=jnp.int32)[None, :] < cover_counts[:, None]
    covered = jnp.any(
        (cover_ids[:, :, None] == block_ids[None, None, :]) & listed[:, :, None], axis=1
    )
    receiver_mask = jnp.repeat(covered.astype(jnp.float32), RB, axis=1)
    misfit = (receiver_mask[None] * (own_rows.astype(jnp.float32) - predicted)).astype(jnp.bfloat16)
    misfit_pair = jnp.stack([misfit, jnp.stack([misfit[1], -misfit[0]])])
    gradient = -jnp.einsum(
        "gcij,ckj->gik", misfit_pair, operand, preferred_element_type=jnp.float32
    )
    sources = jnp.pad(
        misfit[:, :, ::stride_cols],
        ((0, 0), (0, 0), (reach_blocks * rows_dev, reach_blocks * rows_dev)),
    )
    sources = lax.dynamic_slice_in_dim(sources, position * rows_dev, band_width, 2).astype(
        jnp.float32
    )
    response_wide = response.astype(jnp.float32)
    corr_re = -jnp.sum(response_wide[0] * sources[0] + response_wide[1] * sources[1])
    corr_im = -jnp.sum(response_wide[0] * sources[1] - response_wide[1] * sources[0])
    times = jnp.arange(NT, dtype=jnp.int32).astype(jnp.float32)
    phase = 2.0 * math.pi * (freq_index + 1).astype(jnp.float32) * times / NT
    scale = 1.0 / math.sqrt(shot_count * band_width)
    total_re, total_im = lax.psum((corr_re, corr_im), "shot")
    series = total_re * jnp.cos(phase) - total_im * jnp.sin(phase)
    wavelet_grad = lax.psum(series, "freq") * scale
    return (misfit[None], gradient[None], wavelet_grad)


def solution(mesh):
    in_specs = (
        P("freq", None, "shot", None),
        P("freq", None, "shot", None),
        P("freq", None),
        P("shot", None),
        P("shot"),
    )
    out_specs = (P("freq", None, "shot", None), P("freq", None, "shot", None), P())
    return jax.shard_map(
        on_device, mesh=mesh, in_specs=in_specs, out_specs=out_specs, check_vma=False
    )
```

profile of v0, /device:TPU:0, one launch (start us, length us, event | category | flops | bytes accessed | tf_op | source)
XLA Modules:
  0.0 290.7 jit_solution(10244098641319696753)
XLA Ops:
  0.6 6.9 %collective-permute-start = (bf16[2,128,8192]{2,1,0:T(8,128)(2,1)}, bf16[2,128,8192]{2,1,0:T(8,128)(2,1)}, u32[]{:S(2)}, u32[]{:S(2)}) collective-permute-start(bf16[2,128,8192]{2,1,0:T(8,128)(2,1)} %bitcast.71), channel_id=1, source_target_pairs={{0,8},{4,12},{8,16},{12,20},{16,24},{20,28},{1,9},{5,13},{9,17},{1... | collective-permute-start | bytes 12582920 | tf_op jit(solution)/shard_map/ppermute | solution.py:15
  7.5 5.4 %collective-permute-start.1 = (bf16[2,128,8192]{2,1,0:T(8,128)(2,1)}, bf16[2,128,8192]{2,1,0:T(8,128)(2,1)}, u32[]{:S(2)}, u32[]{:S(2)}) collective-permute-start(bf16[2,128,8192]{2,1,0:T(8,128)(2,1)} %bitcast.72), channel_id=1, source_target_pairs={{0,4},{4,8},{8,12},{12,16},{16,20},{20,24},{24,28},{1,5},{5,9},{9,... | collective-permute-start | bytes 12582920 | tf_op jit(solution)/shard_map/ppermute | solution.py:15
  12.9 1.3 collective-permute-start.2
  14.1 1.3 collective-permute-start.3
  15.5 1.4 fusion.28
  16.8 0.7 iota_compare_fusion.2
  17.5 0.7 fusion.23
  18.2 1.6 fusion.26
  19.8 1.7 slice_bitcast_fusion.2
  21.5 1.0 convert_element_type.38
  22.5 0.1 copy.9
  22.6 0.3 broadcast_in_dim.28
  23.0 5.4 %copy.12 = f32[16,8,16,512]{3,1,2,0:T(8,128)} copy(f32[16,8,16,512]{3,2,1,0:T(8,128)S(1)} %bitcast.68) | data formatting | bytes 8388608
  28.3 0.0 copy-start
  28.3 2.2 maximum_bitcast_fusion.18
  30.5 65.2 %collective-permute-done = bf16[2,128,8192]{2,1,0:T(8,128)(2,1)} collective-permute-done((bf16[2,128,8192]{2,1,0:T(8,128)(2,1)}, bf16[2,128,8192]{2,1,0:T(8,128)(2,1)}, u32[]{:S(2)}, u32[]{:S(2)}) %collective-permute-start) | collective-permute-done | bytes 4194336 | tf_op jit(solution)/shard_map/ppermute | solution.py:15
  95.7 2.5 constant_dynamic-update-slice_fusion.4
  98.2 92.5 %collective-permute-done.1 = bf16[2,128,8192]{2,1,0:T(8,128)(2,1)} collective-permute-done((bf16[2,128,8192]{2,1,0:T(8,128)(2,1)}, bf16[2,128,8192]{2,1,0:T(8,128)(2,1)}, u32[]{:S(2)}, u32[]{:S(2)}) %collective-permute-start.1) | collective-permute-done | bytes 4194336 | tf_op jit(solution)/shard_map/ppermute | solution.py:15
  190.6 2.5 constant_dynamic-update-slice_fusion.3
  193.1 0.0 copy-done
  193.1 0.3 constant_dynamic-update-slice_fusion.2
  193.4 0.0 collective-permute-done.2
  193.4 2.5 constant_dynamic-update-slice_fusion.1
  195.8 0.0 collective-permute-done.3
  195.9 2.5 constant_dynamic-update-slice_fusion
  198.3 11.6 %subtract_convert_fusion.1 = (bf16[1,640,8192]{2,1,0:T(8,128)(2,1)}, bf16[1,640,8192]{2,1,0:T(8,128)(2,1)}) fusion(bf16[2,640,8192]{2,1,0:T(8,128)(2,1)S(1)} %constant_dynamic-update-slice_fusion, f32[]{:T(128)} %bitcast.5, s32[640]{0:T(1024)S(1)} %add_multiply_fusion, f32[]{:T(128)} %bitcast.6), kind=kLoop, calls=%fused_computation.2 | loop fusion | flops 47185920 | bytes 41945608 | tf_op jit(solution)/shard_map/convert
  209.9 13.6 %fusion.5 = bf16[2,128,8192]{2,1,0:T(8,128)(2,1)} fusion(bf16[1,640,8192]{2,1,0:T(8,128)(2,1)} %get-tuple-element.8, bf16[1,640,8192]{2,1,0:T(8,128)(2,1)} %get-tuple-element.7, f32[128,8192]{1,0:T(8,128)} %bitcast.75, bf16[1,2,128,640]{3,2,1,0:T(8,128)(2,1)} %get-tuple-element.14, bf16[1,2,128,640]{3,2,1,0:T(8,128)(2,1)} %get-tuple-element.13, ...), kind=kOutput, calls=%fused_computation.9 | convolution fusion | flops 5387911168 | bytes 34209792 | tf_op jit(solution)/shard_map/gcik,ckj->gij/dot_general | solution.py:51
  223.6 19.1 %slice.66 = bf16[2,128,1024]{2,1,0:T(8,128)(2,1)S(1)} slice(bf16[2,128,8192]{2,1,0:T(8,128)(2,1)} %fusion.5), slice={[0:2:1], [0:128:1], [0:8192:8]} | slice | bytes 1048576 | tf_op jit(solution)/shard_map/slice | solution.py:66
  242.7 0.1 fusion.21
  242.8 0.7 add_reduce_fusion
  244.8 3.8 %fusion.27 = (bf16[1,128,8192]{2,1,0:T(8,128)(2,1)S(1)}, bf16[1,128,8192]{2,1,0:T(8,128)(2,1)}) fusion(bf16[2,128,8192]{2,1,0:T(8,128)(2,1)} %fusion.5), kind=kLoop, calls=%fused_computation.46 | loop fusion | flops 1048576 | bytes 8388608 | tf_op jit(solution)/shard_map/slice | solution.py:61
  248.6 20.1 %all-reduce.1 = (f32[]{:T(128)}, f32[]{:T(128)}) all-reduce(f32[]{:T(128)S(6)} %neg.27, f32[]{:T(128)S(6)} %neg.26), channel_id=1, replica_groups=mesh['shot'=8,'freq'=4] {'shot'}, use_global_device_ids=true, to_apply=%region_4.5 | all-reduce | flops 2 | bytes 16 | tf_op jit(solution)/shard_map/psum | solution.py:78
  268.7 1.3 multiply_subtract_fusion
  270.1 5.7 %psum.23 = f32[128]{0:T(128)S(1)} all-reduce(f32[128]{0:T(128)S(1)} %multiply_subtract_fusion), channel_id=1, replica_groups=mesh['shot'=8,'freq'=4] {'freq'}, use_global_device_ids=true, to_apply=%region_5.6 | all-reduce | flops 128 | bytes 1024 | tf_op jit(solution)/shard_map/psum | solution.py:80
  275.7 0.5 broadcast_multiply_fusion
  276.3 2.0 maximum_bitcast_fusion.11
  278.2 12.5 %fusion.15 = f32[1,2,128,640]{3,2,1,0:T(8,128)} fusion(bf16[1,640,8192]{2,1,0:T(8,128)(2,1)} %get-tuple-element.8, bf16[1,640,8192]{2,1,0:T(8,128)(2,1)} %get-tuple-element.7, bf16[1,2,128,8192]{3,2,1,0:T(8,128)(2,1)S(1)} %maximum_bitcast_fusion.11, bf16[1,2,128,8192]{3,2,1,0:T(8,128)(2,1)} %bitcast.69), kind=kOutput, calls=%fused_computation.17 | convolution fusion | flops 5383553024 | bytes 30015488 | tf_op jit(solution)/shard_map/gcij,ckj->gik/dot_general | solution.py:62
  (2 shorter events, 0.0 us)
Async XLA Ops:
  0.6 95.1 %collective-permute-start = (bf16[2,128,8192]{2,1,0:T(8,128)(2,1)}, bf16[2,128,8192]{2,1,0:T(8,128)(2,1)}, u32[]{:S(2)}, u32[]{:S(2)}) collective-permute-start(bf16[2,128,8192]{2,1,0:T(8,128)(2,1)} %bitcast.71), channel_id=1, source_target_pairs={{0,8},{4,12},{8,16},{12,20},{16,24},{20,28},{1,9},{5,13},{9,17},{1... | collective-permute-start | bytes 12582920 | tf_op jit(solution)/shard_map/ppermute | solution.py:15
  7.5 183.1 %collective-permute-start.1 = (bf16[2,128,8192]{2,1,0:T(8,128)(2,1)}, bf16[2,128,8192]{2,1,0:T(8,128)(2,1)}, u32[]{:S(2)}, u32[]{:S(2)}) collective-permute-start(bf16[2,128,8192]{2,1,0:T(8,128)(2,1)} %bitcast.72), channel_id=1, source_target_pairs={{0,4},{4,8},{8,12},{12,16},{16,20},{20,24},{24,28},{1,5},{5,9},{9,... | collective-permute-start | bytes 12582920 | tf_op jit(solution)/shard_map/ppermute | solution.py:15
  12.9 180.5 %collective-permute-start.2 = (bf16[2,128,8192]{2,1,0:T(8,128)(2,1)}, bf16[2,128,8192]{2,1,0:T(8,128)(2,1)}, u32[]{:S(2)}, u32[]{:S(2)}) collective-permute-start(bf16[2,128,8192]{2,1,0:T(8,128)(2,1)} %bitcast.73), channel_id=1, source_target_pairs={{4,0},{8,4},{12,8},{16,12},{20,16},{24,20},{28,24},{5,1},{9,5},{13... | collective-permute-start | bytes 12582920 | tf_op jit(solution)/shard_map/ppermute | solution.py:15
  14.1 181.7 %collective-permute-start.3 = (bf16[2,128,8192]{2,1,0:T(8,128)(2,1)}, bf16[2,128,8192]{2,1,0:T(8,128)(2,1)}, u32[]{:S(2)}, u32[]{:S(2)}) collective-permute-start(bf16[2,128,8192]{2,1,0:T(8,128)(2,1)} %bitcast.74), channel_id=1, source_target_pairs={{8,0},{12,4},{16,8},{20,12},{24,16},{28,20},{9,1},{13,5},{17,9},{2... | collective-permute-start | bytes 12582920 | tf_op jit(solution)/shard_map/ppermute | solution.py:15
  28.3 164.7 %copy-start = (bf16[1,2,128,8192]{3,2,1,0:T(8,128)(2,1)S(1)}, bf16[1,2,128,8192]{3,2,1,0:T(8,128)(2,1)}, u32[]{:S(2)}) copy-start(bf16[1,2,128,8192]{3,2,1,0:T(8,128)(2,1)} %param.5) | copy-start | bytes 12582916
where the time goes:
time: 291 us
  waiting for transfers between devices  158 us (54%)
  local copies, waits for them, and re-layouts  38.1 us (13%)
  other arithmetic  26.3 us (9%)
  matrix products  26.1 us (9%)
  blocking collectives  25.8 us (9%)
  starting transfers between devices  14.8 us (5%)
    ppermute x4, waiting for transfers between devices, passed_along(): return lax.ppermute(block, axis, route)  158 us
    psum x1, blocking collectives, on_device(): total_re, total_im = lax.psum((corr_re, corr_im), 'shot')  20.1 us
    slice x1, local copies, waits for them, and re-layouts, on_device(): misfit[:, :, ::stride_cols]  19.1 us
    ppermute x4, starting transfers between devices, passed_along(): return lax.ppermute(block, axis, route)  14.8 us
    dot_general x1, matrix products, on_device(): jnp.einsum('gcik,ckj->gij', response_pair, operand, preferred_element_typ...  13.6 us
    unnamed x7, local copies, waits for them, and re-layouts  13 us
    dot_general x1, matrix products, on_device(): jnp.einsum('gcij,ckj->gik', misfit_pair, operand, preferred_element_type=...  12.5 us
    another operation x1, other arithmetic  11.6 us
  transfers between devices with their start and end apart: 4, of which 2 were waited for; matrix products, arithmetic and copies ran while one was open for 8% of the time, Pallas kernels for 0%

commit v1 on v0

v1 whole, which is shorter than its diff:
```python
import functools
import math

import jax
import jax.numpy as jnp
from jax import lax
from jax.experimental import pallas as pl
from jax.experimental.pallas import tpu as pltpu
from jax.sharding import PartitionSpec as P

RB = 512
NT = 128
VMEM = 48 * 1024 * 1024
PARTS = (2, 4, 4, 4, 2)
LOW, LOW_X, OWN, MATE, HIGH, HIGH_X = range(6)


def split_kernel(half, cuts, info, whole, *refs):
    outs, sems = refs[:-1], refs[-1]
    side = info[0]
    copies = []
    for n, (off, size) in enumerate(cuts):
        for which in range(2):
            start = (side if which == 0 else 1 - side) * half + off
            copies.append(
                pltpu.make_async_copy(
                    whole.at[:, :, pl.ds(pl.multiple_of(start, 128), size)],
                    outs[2 * n + which],
                    sems.at[2 * n + which],
                )
            )
    for copy in copies:
        copy.start()
    for copy in copies:
        copy.wait()


def split(info, whole, half, cuts):
    rows = whole.shape[1]
    shapes = [
        jax.ShapeDtypeStruct((2, rows, size), whole.dtype) for _, size in cuts for _ in range(2)
    ]
    outs = pl.pallas_call(
        functools.partial(split_kernel, half, cuts),
        out_shape=shapes,
        in_specs=[pl.BlockSpec(memory_space=pltpu.SMEM), pl.BlockSpec(memory_space=pl.ANY)],
        out_specs=[pl.BlockSpec(memory_space=pl.ANY)] * len(shapes),
        scratch_shapes=[pltpu.SemaphoreType.DMA((len(shapes),))],
        cost_estimate=pl.CostEstimate(
            flops=0, bytes_accessed=sum(8 * rows * size * 2 for _, size in cuts), transcendentals=0
        ),
        name="split_columns",
    )(info, whole)
    return [(outs[2 * n], outs[2 * n + 1]) for n in range(len(cuts))]


def place_kernel(half, off, size, info, whole_in, part, whole, sem):
    del whole_in
    start = (1 - info[0]) * half + off
    copy = pltpu.make_async_copy(
        part, whole.at[:, :, pl.ds(pl.multiple_of(start, 128), size)], sem
    )
    copy.start()
    copy.wait()


def place(info, whole, part, half, off):
    size = part.shape[2]
    return pl.pallas_call(
        functools.partial(place_kernel, half, off, size),
        out_shape=jax.ShapeDtypeStruct(whole.shape, whole.dtype),
        in_specs=[pl.BlockSpec(memory_space=pltpu.SMEM)] + [pl.BlockSpec(memory_space=pl.ANY)] * 2,
        out_specs=pl.BlockSpec(memory_space=pl.ANY),
        scratch_shapes=[pltpu.SemaphoreType.DMA],
        input_output_aliases={1: 0},
        cost_estimate=pl.CostEstimate(
            flops=0, bytes_accessed=2 * part.size * 2, transcendentals=0
        ),
        name="place_columns",
    )(info, whole, part)


def chunk_kernel(conf, *refs):
    rows, tile, steps, stride, off, half, layout, first = conf
    refs = list(refs)
    info, wave, resp, ids = (refs.pop(0) for _ in range(4))
    count = max(ref for ref, _ in layout) + 1
    tiles = [refs.pop(0) for _ in range(count)]
    if not first:
        _, grad_in, corr_in = (refs.pop(0) for _ in range(3))
    out_own, out_mate, grad_out, corr_out, ys, sums = refs
    step = pl.program_id(0)
    side, pos = info[0], info[1]
    mate = pos + 1 - 2 * side
    width2 = 2 * rows
    col0 = side * half + off + step * tile
    blocks = (pos - 2, mate - 2, pos, mate, pos + 2, mate + 2)

    @pl.when(step == 0)
    def _():
        sums[...] = jnp.zeros_like(sums)
        corr_out[...] = jnp.zeros_like(corr_out) if first else corr_in[...]

    def record(slot):
        ref, part = layout[slot]
        value = tiles[ref][...] if part is None else tiles[ref][part]
        return value.reshape(width2, tile)

    def hits(slot):
        shots = blocks[slot] * rows + lax.broadcasted_iota(jnp.int32, (rows, tile), 0)
        cols = col0 + lax.broadcasted_iota(jnp.int32, (rows, tile), 1)
        return shots * stride == cols

    def meets(slot):
        low = blocks[slot] * rows * stride
        return (low < col0 + tile) & (low + rows * stride > col0)

    for slot in range(6):
        ys[pl.ds(slot * width2, width2), :] = record(slot)

        @pl.when(meets(slot))
        def _(slot=slot):
            hit = hits(slot)
            for c in range(2):
                at = pl.ds(slot * width2 + c * rows, rows)
                direct = jnp.where(hit, wave[c], 0.0)
                ys[at, :] = (ys[at, :].astype(jnp.float32) - direct).astype(jnp.bfloat16)

    y = ys[...]
    fit = jnp.dot(resp[...], y, preferred_element_type=jnp.float32)
    lists = ids[...]
    entry = lax.broadcasted_iota(jnp.int32, lists.shape, 1)
    count_col = lists[:, -1:]
    recorded = (lists == col0 // RB) & (entry < count_col) & (entry < lists.shape[1] - 1)
    covered = jnp.max(jnp.where(recorded, 1.0, 0.0), axis=1, keepdims=True)
    out = []
    for which, slot in ((0, OWN), (1, MATE)):
        mask = covered[which * rows : (which + 1) * rows]
        mask = jnp.concatenate([mask, mask], axis=0)
        value = record(slot).astype(jnp.float32) + fit[which * width2 : (which + 1) * width2]
        out.append((mask * value).astype(jnp.bfloat16))
    out_own[...] = out[0].reshape(out_own.shape)
    out_mate[...] = out[1].reshape(out_mate.shape)
    misfit = jnp.concatenate(out, axis=0)
    across = (((1,), (1,)), ((), ()))
    sums[...] += lax.dot_general(misfit, y, across, preferred_element_type=jnp.float32)

    for slot in range(6):

        @pl.when(meets(slot))
        def _(slot=slot):
            one = jnp.where(hits(slot), 1.0, 0.0).astype(jnp.bfloat16)
            at_shots = lax.dot_general(misfit, one, across, preferred_element_type=jnp.float32)
            for c in range(2):
                x = resp[:, pl.ds(slot * width2 + c * rows, rows)].astype(jnp.float32)
                terms = (x * at_shots).reshape(-1, 8, rows)
                corr_out[c] -= jnp.sum(terms, axis=0)

    @pl.when(step == steps - 1)
    def _():
        even = side == 0
        for which in range(2):
            re = pl.ds(which * width2, rows)
            im = pl.ds(which * width2 + rows, rows)

            def part(slot):
                a = pl.ds(slot * width2, rows)
                b = pl.ds(slot * width2 + rows, rows)
                return (sums[re, a] + sums[im, b], sums[im, a] - sums[re, b])

            if which == 0:
                order = (LOW, (LOW_X, MATE), OWN, (MATE, HIGH_X), HIGH)
            else:
                order = (LOW_X, (OWN, LOW), MATE, (HIGH, OWN), HIGH_X)
            for k, slot in enumerate(order):
                at = pl.ds(k * rows, rows)
                if isinstance(slot, tuple):
                    value = [
                        jnp.where(even, p, q) for p, q in zip(part(slot[0]), part(slot[1]))
                    ]
                else:
                    value = part(slot)
                for c in range(2):
                    if first:
                        grad_out[which, c, :, at] = value[c]
                    else:
                        grad_out[which, c, :, at] = grad_in[which, c, :, at] + value[c]


def chunk(info, wave, resp, ids, arrays, layout, carry, off, size, half, width, stride, rows, band):
    tile = min(size, RB)
    steps = size // tile
    first = carry is None
    conf = (rows, tile, steps, stride, off, half, layout, first)
    whole_block = pl.BlockSpec(
        (2, rows, tile), lambda i, info: (0, 0, (info[0] * half + off) // tile + i)
    )
    grad_shape = (2, 2, rows, band)
    corr_shape = (2, 8, rows)

    def full(shape):
        return pl.BlockSpec(shape, lambda i, info: (0,) * len(shape))

    in_specs = [pl.BlockSpec(memory_space=pltpu.SMEM), full(resp.shape), full(ids.shape)]
    for a in arrays:
        if a.ndim == 3:
            in_specs.append(pl.BlockSpec((2, rows, tile), lambda i, info: (0, 0, i)))
        else:
            in_specs.append(pl.BlockSpec((2, 2, rows, tile), lambda i, info: (0, 0, 0, i)))
    args = [info, wave, resp, ids, *arrays]
    aliases = {}
    if not first:
        aliases = {len(args): 0, len(args) + 1: 2, len(args) + 2: 3}
        args += list(carry)
        in_specs += [pl.BlockSpec(memory_space=pl.ANY), full(grad_shape), full(corr_shape)]
    macs = 2 * resp.shape[0] * resp.shape[1] * size
    return pl.pallas_call(
        functools.partial(chunk_kernel, conf),
        out_shape=[
            jax.ShapeDtypeStruct((2, rows, width), jnp.bfloat16),
            jax.ShapeDtypeStruct((2, rows, size), jnp.bfloat16),
            jax.ShapeDtypeStruct(grad_shape, jnp.float32),
            jax.ShapeDtypeStruct(corr_shape, jnp.float32),
        ],
        grid_spec=pltpu.PrefetchScalarGridSpec(
            num_scalar_prefetch=1,
            grid=(steps,),
            in_specs=in_specs,
            out_specs=[
                whole_block,
                pl.BlockSpec((2, rows, tile), lambda i, info: (0, 0, i)),
                full(grad_shape),
                full(corr_shape),
            ],
            scratch_shapes=[
                pltpu.VMEM((12 * rows, tile), jnp.bfloat16),
                pltpu.VMEM((4 * rows, 12 * rows), jnp.float32),
            ],
        ),
        input_output_aliases=aliases,
        compiler_params=pltpu.CompilerParams(vmem_limit_bytes=VMEM),
        cost_estimate=pl.CostEstimate(
            flops=2 * macs, bytes_accessed=16 * rows * size * 2 + 5 * 10**6, transcendentals=0
        ),
        name="residual_chunk",
    )(*args)


def responses(own, mate, side, rows):
    even = side == 0

    def piece(a, k):
        return a[:, :, k * rows : (k + 1) * rows]

    none = jnp.zeros_like(piece(own, 0))
    o = [piece(own, k) for k in range(5)]
    m = [piece(mate, k) for k in range(5)]
    table = [
        [o[0], jnp.where(even, o[1], none), o[2], jnp.where(even, o[3], o[1]), o[4],
         jnp.where(even, none, o[3])],
        [jnp.where(even, none, m[1]), m[0], jnp.where(even, m[1], m[3]), m[2],
         jnp.where(even, m[3], none), m[4]],
    ]
    lines = []
    for line in table:
        lines.append(jnp.concatenate([v for p in line for v in (p[0], -p[1])], axis=1))
        lines.append(jnp.concatenate([v for p in line for v in (p[1], p[0])], axis=1))
    return jnp.concatenate(lines, axis=0)


def on_device(data, primaries, wavelet, cover_ids, cover_counts):
    record = data[0]
    _, rows, width = record.shape
    band = primaries.shape[3]
    devices = lax.axis_size("shot")
    shot_count = devices * rows
    stride = width // shot_count
    half = width // 2
    position = lax.axis_index("shot").astype(jnp.int32)
    freq_index = lax.axis_index("freq")
    side = position % 2
    info = jnp.stack([side, position])
    unit = half // sum(PARTS)
    cuts, off = [], 0
    for part in PARTS:
        cuts.append((off, part * unit))
        off += part * unit

    swap = [(i, i ^ 1) for i in range(devices)]
    up = [(i, i + 2) for i in range(devices - 2)]
    down = [(i + 2, i) for i in range(devices - 2)]

    def send(a, route):
        return lax.ppermute(a, "shot", route)

    pieces = split(info, record, half, cuts[:1]) + split(info, record, half, cuts[1:])
    response = primaries[0]
    lists = jnp.concatenate([cover_ids, cover_counts[:, None]], axis=1)
    resp = responses(response, send(response, swap), side, rows)
    ids = jnp.concatenate([lists, send(lists, swap)], axis=0)
    wave = wavelet[0]

    carry = None
    for n, (off, size) in enumerate(cuts):
        mine, other = pieces[n]
        theirs = send(other, swap)
        if n == 0:
            arrays = [
                mine, theirs, send(mine, up), send(theirs, up), send(mine, down), send(theirs, down)
            ]
            layout = ((2, None), (3, None), (0, None), (1, None), (4, None), (5, None))
        else:
            both = jnp.stack([mine, theirs])
            arrays = [both, send(both, up), send(both, down)]
            layout = ((1, 0), (1, 1), (0, 0), (0, 1), (2, 0), (2, 1))
        whole, back, grad, corr = chunk(
            info, wave, resp, ids, arrays, layout, carry,
            off, size, half, width, stride, rows, band,
        )
        whole = place(info, whole, send(back, swap), half, off)
        carry = (whole, grad, corr)

    gradient = grad[0] + send(grad[1], swap)
    total_re, total_im = jnp.sum(corr[0]), jnp.sum(corr[1])
    times = jnp.arange(NT, dtype=jnp.int32).astype(jnp.float32)
    phase = 2.0 * math.pi * (freq_index + 1).astype(jnp.float32) * times / NT
    scale = 1.0 / math.sqrt(shot_count * band)
    series = total_re * jnp.cos(phase) - total_im * jnp.sin(phase)
    wavelet_grad = lax.psum(series, ("shot", "freq")) * scale
    return (whole[None], gradient[None], wavelet_grad)


def solution(mesh):
    in_specs = (
        P("freq", None, "shot", None),
        P("freq", None, "shot", None),
        P("freq", None),
        P("shot", None),
        P("shot"),
    )
    out_specs = (P("freq", None, "shot", None), P("freq", None, "shot", None), P())
    return jax.shard_map(
        on_device, mesh=mesh, in_specs=in_specs, out_specs=out_specs, check_vma=False
    )
```

time: 291 us -> 392 us (1.35)
  Pallas kernels: 0 us -> 239 us
  waiting for transfers between devices: 158 us -> 48.6 us
  local copies, waits for them, and re-layouts: 38.1 us -> 5.77 us
  starting transfers between devices: 14.8 us -> 45 us
  matrix products: 26.1 us -> 0 us
  other arithmetic: 26.3 us -> 9.81 us
  blocking collectives: 25.8 us -> 41.8 us
    pallas_call x0 -> x12, Pallas kernels: none -> 239 us  [the longest x2 131 us: split(): pl.pallas_call(functools.partial(split_kernel, half, cuts), out_shape=sha...]
    ppermute x4 -> x25, waiting for transfers between devices: 158 us -> 48.6 us  [send(): return lax.ppermute(a, 'shot', route)]
    ppermute x4 -> x25, starting transfers between devices: 14.8 us -> 45 us  [send(): return lax.ppermute(a, 'shot', route)]
    dot_general x2 -> x0, matrix products: 26.1 us -> none  [the longest x1 13.6 us: on_device(): jnp.einsum('gcik,ckj->gij', response_pair, operand, preferred_element_typ...]
    slice x2 -> x0, local copies, waits for them, and re-layouts: 20.5 us -> none  [the longest x1 19.1 us: on_device(): misfit[:, :, ::stride_cols]]
    psum x2 -> x1, blocking collectives: 25.8 us -> 41.8 us  [on_device(): wavelet_grad = lax.psum(series, ('shot', 'freq')) * scale]
    another operation x3 -> x5, other arithmetic: 15.8 us -> 5.91 us  [the longest x4 5.33 us: on_device(): both = jnp.stack([mine, theirs])]
    unnamed x7 -> x76, local copies, waits for them, and re-layouts: 13 us -> 5.58 us
  transfers between devices with their start and end apart: 4 -> 25, of which waited for: 2 -> 6; matrix products, arithmetic and copies ran while one was open for 8% -> 2% of each run, Pallas kernels for 0% -> 55%
where the time goes in v1:
time: 392 us; the launch traced here: 391 us
  Pallas kernels  239 us (61%)
  waiting for transfers between devices  48.6 us (12%)
  starting transfers between devices  45 us (11%)
  blocking collectives  41.8 us (11%)
  other arithmetic  9.81 us (3%)
  local copies, waits for them, and re-layouts  5.77 us (1%)
    pallas_call x2, Pallas kernels, split(): pl.pallas_call(functools.partial(split_kernel, half, cuts), out_shape=sha...  131 us
    pallas_call x5, Pallas kernels, place(): pl.pallas_call(functools.partial(place_kernel, half, off, size), out_shap...  72.9 us
    ppermute x25, waiting for transfers between devices, send(): return lax.ppermute(a, 'shot', route)  48.6 us
    ppermute x25, starting transfers between devices, send(): return lax.ppermute(a, 'shot', route)  45 us
    psum x1, blocking collectives, on_device(): wavelet_grad = lax.psum(series, ('shot', 'freq')) * scale  41.8 us
    pallas_call x5, Pallas kernels, chunk(): pl.pallas_call(functools.partial(chunk_kernel, conf), out_shape=[jax.Shap...  35.4 us
  transfers between devices with their start and end apart: 25, of which 6 were waited for; matrix products, arithmetic and copies ran while one was open for 2% of the time, Pallas kernels for 55%

profile of v1, /device:TPU:0, one launch (start us, length us, event | category | flops | bytes accessed | tf_op | source)
XLA Modules:
  0.0 391.3 jit_solution(6434916131497779298)
XLA Ops:
  1.3 17.7 %split_columns.3 = (bf16[2,128,512]{2,1,0:T(8,128)(2,1)}, bf16[2,128,512]{2,1,0:T(8,128)(2,1)}) custom-call(s32[2]{0:T(128)} %pad_add_fusion.2.info.refs_0_, bf16[2,128,8192]{2,1,0:T(8,128)(2,1)} %bitcast.173), custom_call_target="tpu_custom_call" | custom-call | bytes 1048576 | tf_op jit(solution)/shard_map/split_columns/pallas_call | solution.py:43
  18.9 4.9 %collective-permute-start.15 = (bf16[2,128,512]{2,1,0:T(8,128)(2,1)}, bf16[2,128,512]{2,1,0:T(8,128)(2,1)S(1)}, u32[]{:S(2)}, u32[]{:S(2)}) collective-permute-start(bf16[2,128,512]{2,1,0:T(8,128)(2,1)} %get-tuple-element.41.refs_4_), channel_id=1, source_target_pairs={{0,8},{4,12},{8,16},{12,20},{16,24},{20,28},{1,9},{5,13},{9,17},{1... | collective-permute-start | bytes 786440 | tf_op jit(solution)/shard_map/ppermute | solution.py:294
  23.9 1.3 collective-permute-start.17
  25.2 1.6 collective-permute-start
  27.3 1.6 collective-permute-start.1
  29.3 113.0 %split_columns.2 = (bf16[2,128,1024]{2,1,0:T(8,128)(2,1)}, bf16[2,128,1024]{2,1,0:T(8,128)(2,1)}, bf16[2,128,1024]{2,1,0:T(8,128)(2,1)}, bf16[2,128,1024]{2,1,0:...) custom-call(s32[2]{0:T(128)} %pad_add_fusion.2.info.refs_0_, ...), custom_call_target="tpu_custom_call" | custom-call | bytes 7340032 | tf_op jit(solution)/shard_map/split_columns/pallas_call | solution.py:43
  143.5 11.7 %collective-permute-done.11 = bf16[2,128,1024]{2,1,0:T(8,128)(2,1)S(1)} collective-permute-done((bf16[2,128,1024]{2,1,0:T(8,128)(2,1)}, bf16[2,128,1024]{2,1,0:T(8,128)(2,1)S(1)}, u32[]{:S(2)}, u32[]{:S(2)}) %collective-permute-start.11) | collective-permute-done | bytes 524320 | tf_op jit(solution)/shard_map/ppermute | solution.py:294
  155.1 2.1 pad_maximum_fusion.3.refs_4_
  157.2 5.2 %collective-permute-start.12 = (bf16[2,2,128,1024]{3,2,1,0:T(8,128)(2,1)}, bf16[2,2,128,1024]{3,2,1,0:T(8,128)(2,1)}, u32[]{:S(2)}, u32[]{:S(2)}) collective-permute-start(bf16[2,2,128,1024]{3,2,1,0:T(8,128)(2,1)} %pad_maximum_fusion.3.refs_4_), channel_id=1, source_target_pairs={{0,8},{4,12},{8,16},{12,20},{16,24},{20,28},{1,9},{5,13},{9,17},{1... | collective-permute-start | bytes 3145736 | tf_op jit(solution)/shard_map/ppermute | solution.py:294
  162.5 1.3 collective-permute-start.13
  164.4 4.6 %collective-permute-start.16 = (bf16[2,128,512]{2,1,0:T(8,128)(2,1)S(1)}, bf16[2,128,512]{2,1,0:T(8,128)(2,1)S(1)}, u32[]{:S(2)}, u32[]{:S(2)}) collective-permute-start(bf16[2,128,512]{2,1,0:T(8,128)(2,1)S(1)} %collective-permute-done.14.refs_5_), channel_id=1, source_target_pairs={{0,8},{4,12},{8,16},{12,20},{16,24},{20,28},{1,9},{5,13},{9,17},{1... | collective-permute-start | bytes 786440 | tf_op jit(solution)/shard_map/ppermute | solution.py:294
  169.0 0.7 copy-done.9
  169.7 1.3 collective-permute-start.18
  171.8 15.6 %collective-permute-done.16.refs_7_ = bf16[2,128,512]{2,1,0:T(8,128)(2,1)S(1)} collective-permute-done((bf16[2,128,512]{2,1,0:T(8,128)(2,1)S(1)}, bf16[2,128,512]{2,1,0:T(8,128)(2,1)S(1)}, u32[]{:S(2)}, u32[]{:S(2)}) %collective-permute-start.16) | collective-permute-done | bytes 262176 | tf_op jit(solution)/shard_map/ppermute | solution.py:294
  187.4 5.1 %collective-permute-done.18.refs_9_ = bf16[2,128,512]{2,1,0:T(8,128)(2,1)S(1)} collective-permute-done((bf16[2,128,512]{2,1,0:T(8,128)(2,1)S(1)}, bf16[2,128,512]{2,1,0:T(8,128)(2,1)S(1)}, u32[]{:S(2)}, u32[]{:S(2)}) %collective-permute-start.18) | collective-permute-done | bytes 262176 | tf_op jit(solution)/shard_map/ppermute | solution.py:294
  192.5 4.3 %residual_chunk.5 = (bf16[2,128,8192]{2,1,0:T(8,128)(2,1)}, bf16[2,128,512]{2,1,0:T(8,128)(2,1)S(1)}, f32[2,2,128,640]{3,2,1,0:T(8,128)S(1)}, f32[2,8,128]{2,1,0:T(8,128)S(1)}) custom-call(s32[2]{0:T(128)S(1)} %copy-done.2, f32[2]{0:T(128)S(1)} %bitcast.167, bf16[512,1536]{1,0:T(8,128)(2,1)S(1)} %pad_maximum_fusion.refs_2_, s32[256,9]{1,0:T(8,128)S(1)} %copy.31.refs_3_, ...), custom_call_target="tpu_custom_call" | custom-call | flops 1610612736 | bytes 7097152 | tf_op jit(solution)/shard_map/residual_chunk/pallas_call | solution.py:217
  197.0 1.1 pad_maximum_fusion.2.refs_4_
  198.0 1.3 collective-permute-start.10
  199.3 5.5 %collective-permute-start.9 = (bf16[2,2,128,1024]{3,2,1,0:T(8,128)(2,1)}, bf16[2,2,128,1024]{3,2,1,0:T(8,128)(2,1)}, u32[]{:S(2)}, u32[]{:S(2)}) collective-permute-start(bf16[2,2,128,1024]{3,2,1,0:T(8,128)(2,1)} %pad_maximum_fusion.2.refs_4_), channel_id=1, source_target_pairs={{0,8},{4,12},{8,16},{12,20},{16,24},{20,28},{1,9},{5,13},{9,17},{1... | collective-permute-start | bytes 3145736 | tf_op jit(solution)/shard_map/ppermute | solution.py:294
  204.9 1.9 collective-permute-start.5
  206.7 9.8 %place_columns.5.refs_7_ = bf16[2,128,8192]{2,1,0:T(8,128)(2,1)} custom-call(s32[2]{0:T(128)} %pad_add_fusion.2.info.refs_0_, bf16[2,128,8192]{2,1,0:T(8,128)(2,1)} %get-tuple-element.43.whole_in, bf16[2,128,512]{2,1,0:T(8,128)(2,1)} %copy-done.20), custom_call_target="tpu_custom_call", output_to_operand_aliasing={{}: (1, {})} | custom-call | bytes 524288 | tf_op jit(solution)/shard_map/place_columns/pallas_call | solution.py:69
  216.6 8.8 %residual_chunk.6 = (bf16[2,128,8192]{2,1,0:T(8,128)(2,1)}, bf16[2,128,1024]{2,1,0:T(8,128)(2,1)S(1)}, f32[2,2,128,640]{3,2,1,0:T(8,128)S(1)}, f32[2,8,128]{2,1,0:T(8,128)S(1)}) custom-call(s32[2]{0:T(128)S(1)} %copy-done.3, f32[2]{0:T(128)S(1)} %bitcast.168, bf16[512,1536]{1,0:T(8,128)(2,1)} %copy-done, ...), custom_call_target="tpu_custom_call", output_to_operand_aliasing={{0}: (7, {}), {2}: (8, {}), {3}: (9, {})} | custom-call | flops 3221225472 | bytes 9194304 | tf_op jit(solution)/shard_map/residual_chunk/pallas_call | solution.py:217
  225.5 1.1 pad_maximum_fusion.1.refs_4_
  226.6 3.2 collective-permute-start.6
  229.8 1.5 collective-permute-start.7
  231.3 3.3 collective-permute-done.20.part
  234.6 0.8 copy-done.16
  235.4 17.8 %place_columns.6.refs_7_ = bf16[2,128,8192]{2,1,0:T(8,128)(2,1)} custom-call(s32[2]{0:T(128)} %pad_add_fusion.2.info.refs_0_, bf16[2,128,8192]{2,1,0:T(8,128)(2,1)} %get-tuple-element.47.whole_in, bf16[2,128,1024]{2,1,0:T(8,128)(2,1)} %copy-done.16), custom_call_target="tpu_custom_call", output_to_operand_aliasing={{}: (1, {})} | custom-call | bytes 1048576 | tf_op jit(solution)/shard_map/place_columns/pallas_call | solution.py:69
  253.2 8.8 %residual_chunk.7 = (bf16[2,128,8192]{2,1,0:T(8,128)(2,1)}, bf16[2,128,1024]{2,1,0:T(8,128)(2,1)S(1)}, f32[2,2,128,640]{3,2,1,0:T(8,128)S(1)}, f32[2,8,128]{2,1,0:T(8,128)S(1)}) custom-call(s32[2]{0:T(128)S(1)} %copy-done.4, f32[2]{0:T(128)S(1)} %bitcast.169, bf16[512,1536]{1,0:T(8,128)(2,1)} %copy-done, ...), custom_call_target="tpu_custom_call", output_to_operand_aliasing={{0}: (7, {}), {2}: (8, {}), {3}: (9, {})} | custom-call | flops 3221225472 | bytes 9194304 | tf_op jit(solution)/shard_map/residual_chunk/pallas_call | solution.py:217
  262.0 2.0 collective-permute-start.2
  264.1 8.8 %collective-permute-done.21.part = bf16[2,128,1024]{2,1,0:T(8,128)(2,1)S(1)} collective-permute-done((bf16[2,128,1024]{2,1,0:T(8,128)(2,1)S(1)}, bf16[2,128,1024]{2,1,0:T(8,128)(2,1)S(1)}, u32[]{:S(2)}, u32[]{:S(2)}) %collective-permute-start.21) | collective-permute-done | bytes 524320 | tf_op jit(solution)/shard_map/ppermute | solution.py:294
  272.8 0.8 copy-done.17
  273.6 17.8 %place_columns.7.refs_7_ = bf16[2,128,8192]{2,1,0:T(8,128)(2,1)} custom-call(s32[2]{0:T(128)} %pad_add_fusion.2.info.refs_0_, bf16[2,128,8192]{2,1,0:T(8,128)(2,1)} %get-tuple-element.51.whole_in, bf16[2,128,1024]{2,1,0:T(8,128)(2,1)} %copy-done.17), custom_call_target="tpu_custom_call", output_to_operand_aliasing={{}: (1, {})} | custom-call | bytes 1048576 | tf_op jit(solution)/shard_map/place_columns/pallas_call | solution.py:69
  291.4 8.5 %residual_chunk.8 = (bf16[2,128,8192]{2,1,0:T(8,128)(2,1)}, bf16[2,128,1024]{2,1,0:T(8,128)(2,1)S(1)}, f32[2,2,128,640]{3,2,1,0:T(8,128)S(1)}, f32[2,8,128]{2,1,0:T(8,128)S(1)}) custom-call(s32[2]{0:T(128)S(1)} %copy-done.5, f32[2]{0:T(128)S(1)} %bitcast.170, bf16[512,1536]{1,0:T(8,128)(2,1)} %copy-done, ...), custom_call_target="tpu_custom_call", output_to_operand_aliasing={{0}: (7, {}), {2}: (8, {}), {3}: (9, {})} | custom-call | flops 3221225472 | bytes 9194304 | tf_op jit(solution)/shard_map/residual_chunk/pallas_call | solution.py:217
  300.0 1.0 pad_maximum_fusion.4.refs_4_
  301.0 2.7 collective-permute-start.3
  303.7 1.3 collective-permute-start.4
  304.9 4.2 %collective-permute-done.22.part = bf16[2,128,1024]{2,1,0:T(8,128)(2,1)S(1)} collective-permute-done((bf16[2,128,1024]{2,1,0:T(8,128)(2,1)S(1)}, bf16[2,128,1024]{2,1,0:T(8,128)(2,1)S(1)}, u32[]{:S(2)}, u32[]{:S(2)}) %collective-permute-start.22) | collective-permute-done | bytes 524320 | tf_op jit(solution)/shard_map/ppermute | solution.py:294
  309.2 0.8 copy-done.15
  309.9 17.8 %place_columns.8.refs_7_ = bf16[2,128,8192]{2,1,0:T(8,128)(2,1)} custom-call(s32[2]{0:T(128)} %pad_add_fusion.2.info.refs_0_, bf16[2,128,8192]{2,1,0:T(8,128)(2,1)} %get-tuple-element.55.whole_in, bf16[2,128,1024]{2,1,0:T(8,128)(2,1)} %copy-done.15), custom_call_target="tpu_custom_call", output_to_operand_aliasing={{}: (1, {})} | custom-call | bytes 1048576 | tf_op jit(solution)/shard_map/place_columns/pallas_call | solution.py:69
  327.8 5.0 %residual_chunk.9 = (bf16[2,128,8192]{2,1,0:T(8,128)(2,1)}, bf16[2,128,512]{2,1,0:T(8,128)(2,1)S(1)}, f32[2,2,128,640]{3,2,1,0:T(8,128)S(1)}, f32[2,8,128]{2,1,0:T(8,128)S(1)}) custom-call(s32[2]{0:T(128)S(1)} %copy-done.6, f32[2]{0:T(128)S(1)} %bitcast.171, ...), custom_call_target="tpu_custom_call", output_to_operand_aliasing={{0}: (7, {}), {2}: (8, {}), {3}: (9, {})} | custom-call | flops 1610612736 | bytes 7097152 | tf_op jit(solution)/shard_map/residual_chunk/pallas_call | solution.py:217
  332.8 0.7 copy-done.13
  333.6 2.0 collective-permute-start.23
  336.3 1.4 multiply_subtract_fusion
  337.7 41.8 %psum.7 = f32[128]{0:T(128)S(1)} all-reduce(f32[128]{0:T(128)S(1)} %multiply_subtract_fusion), channel_id=1, replica_groups=mesh['shot'=8,'freq'=4] {'shot','freq'}, use_global_device_ids=true, to_apply=%region_2.3 | all-reduce | flops 128 | bytes 1024 | tf_op jit(solution)/shard_map/psum | solution.py:329
  380.0 0.7 copy-done.21
  380.7 9.7 %place_columns.9 = bf16[2,128,8192]{2,1,0:T(8,128)(2,1)} custom-call(s32[2]{0:T(128)} %pad_add_fusion.2.info.refs_0_, bf16[2,128,8192]{2,1,0:T(8,128)(2,1)} %get-tuple-element.59.whole_in, bf16[2,128,512]{2,1,0:T(8,128)(2,1)} %copy-done.21), custom_call_target="tpu_custom_call", output_to_operand_aliasing={{}: (1, {})} | custom-call | bytes 524288 | tf_op jit(solution)/shard_map/place_columns/pallas_call | solution.py:69
  390.4 0.9 fusion
  (121 shorter events, 5.5 us)
Async XLA Ops:
  0.6 24.6 %copy-start.14 = (bf16[1,2,128,640]{3,2,1,0:T(8,128)(2,1)S(1)}, bf16[1,2,128,640]{3,2,1,0:T(8,128)(2,1)}, u32[]{:S(2)}) copy-start(bf16[1,2,128,640]{3,2,1,0:T(8,128)(2,1)} %param.6) | copy-start | bytes 983044
  0.6 26.6 %copy-start.24 = (s32[128]{0:T(128)S(1)}, s32[128]{0:T(128)}, u32[]{:S(2)}) copy-start(s32[128]{0:T(128)} %param.9) | copy-start | bytes 1540
  0.7 26.6 %copy-start.23 = (s32[128,8]{0,1:T(8,128)S(1)}, s32[128,8]{0,1:T(8,128)}, u32[]{:S(2)}) copy-start(s32[128,8]{0,1:T(8,128)} %param.8) | copy-start | bytes 12292
  18.9 145.5 %collective-permute-start.15 = (bf16[2,128,512]{2,1,0:T(8,128)(2,1)}, bf16[2,128,512]{2,1,0:T(8,128)(2,1)S(1)}, u32[]{:S(2)}, u32[]{:S(2)}) collective-permute-start(bf16[2,128,512]{2,1,0:T(8,128)(2,1)} %get-tuple-element.41.refs_4_), channel_id=1, source_target_pairs={{0,8},{4,12},{8,16},{12,20},{16,24},{20,28},{1,9},{5,13},{9,17},{1... | collective-permute-start | bytes 786440 | tf_op jit(solution)/shard_map/ppermute | solution.py:294
  23.9 145.1 %collective-permute-start.17 = (bf16[2,128,512]{2,1,0:T(8,128)(2,1)}, bf16[2,128,512]{2,1,0:T(8,128)(2,1)S(1)}, u32[]{:S(2)}, u32[]{:S(2)}) collective-permute-start(bf16[2,128,512]{2,1,0:T(8,128)(2,1)} %get-tuple-element.41.refs_4_), channel_id=1, source_target_pairs={{8,0},{12,4},{16,8},{20,12},{24,16},{28,20},{9,1},{13,5},{17,9},{2... | collective-permute-start | bytes 786440 | tf_op jit(solution)/shard_map/ppermute | solution.py:294
  25.2 117.9 %collective-permute-start = (bf16[2,128,640]{2,1,0:T(8,128)(2,1)S(1)}, bf16[2,128,640]{2,1,0:T(8,128)(2,1)S(1)}, u32[]{:S(2)}, u32[]{:S(2)}) collective-permute-start(bf16[2,128,640]{2,1,0:T(8,128)(2,1)S(1)} %bitcast.175), channel_id=1, source_target_pairs={{0,4},{4,0},{8,12},{12,8},{16,20},{20,16},{24,28},{28,24},{1,5},{5... | collective-permute-start | bytes 983048 | tf_op jit(solution)/shard_map/ppermute | solution.py:294
  26.7 137.0 %collective-permute-start.14 = (bf16[2,128,512]{2,1,0:T(8,128)(2,1)}, bf16[2,128,512]{2,1,0:T(8,128)(2,1)S(1)}, u32[]{:S(2)}, u32[]{:S(2)}) collective-permute-start(bf16[2,128,512]{2,1,0:T(8,128)(2,1)} %get-tuple-element.42), channel_id=1, source_target_pairs={{0,4},{4,0},{8,12},{12,8},{16,20},{20,16},{24,28},{28,24},{1,5},{5... | collective-permute-start | bytes 786440 | tf_op jit(solution)/shard_map/ppermute | solution.py:294
  27.3 115.0 %collective-permute-start.1 = (s32[128,9]{0,1:T(8,128)S(1)}, s32[128,9]{0,1:T(8,128)S(1)}, u32[]{:S(2)}, u32[]{:S(2)}) collective-permute-start(s32[128,9]{0,1:T(8,128)S(1)} %pad_add_fusion.1), channel_id=1, source_target_pairs={{0,4},{4,0},{8,12},{12,8},{16,20},{20,16},{24,28},{28,24},{1,5},{5... | collective-permute-start | bytes 13832 | tf_op jit(solution)/shard_map/ppermute | solution.py:294
  142.3 12.8 %collective-permute-start.11 = (bf16[2,128,1024]{2,1,0:T(8,128)(2,1)}, bf16[2,128,1024]{2,1,0:T(8,128)(2,1)S(1)}, u32[]{:S(2)}, u32[]{:S(2)}) collective-permute-start(bf16[2,128,1024]{2,1,0:T(8,128)(2,1)} %get-tuple-element.40), channel_id=1, source_target_pairs={{0,4},{4,0},{8,12},{12,8},{16,20},{20,16},{24,28},{28,24},{1,5},{5... | collective-permute-start | bytes 1572872 | tf_op jit(solution)/shard_map/ppermute | solution.py:294
  143.0 20.8 %copy-start.25 = (bf16[2,128,1024]{2,1,0:T(8,128)(2,1)S(1)}, bf16[2,128,1024]{2,1,0:T(8,128)(2,1)}, u32[]{:S(2)}) copy-start(bf16[2,128,1024]{2,1,0:T(8,128)(2,1)} %get-tuple-element.38) | copy-start | bytes 1572868
  143.2 49.2 %copy-start.2 = (s32[2]{0:T(128)S(1)}, s32[2]{0:T(128)}, u32[]{:S(2)}) copy-start(s32[2]{0:T(128)} %pad_add_fusion.2.info.refs_0_) | copy-start | bytes 28
  143.2 49.2 %copy-start.7 = (f32[1,2]{1,0:T(1,128)S(1)}, f32[1,2]{1,0:T(1,128)}, u32[]{:S(2)}) copy-start(f32[1,2]{1,0:T(1,128)} %param.7) | copy-start | bytes 28
  143.3 49.2 %copy-start.8 = (bf16[2,128,512]{2,1,0:T(8,128)(2,1)S(1)}, bf16[2,128,512]{2,1,0:T(8,128)(2,1)}, u32[]{:S(2)}) copy-start(bf16[2,128,512]{2,1,0:T(8,128)(2,1)} %get-tuple-element.41.refs_4_) | copy-start | bytes 786436
  157.2 59.4 %collective-permute-start.12 = (bf16[2,2,128,1024]{3,2,1,0:T(8,128)(2,1)}, bf16[2,2,128,1024]{3,2,1,0:T(8,128)(2,1)}, u32[]{:S(2)}, u32[]{:S(2)}) collective-permute-start(bf16[2,2,128,1024]{3,2,1,0:T(8,128)(2,1)} %pad_maximum_fusion.3.refs_4_), channel_id=1, source_target_pairs={{0,8},{4,12},{8,16},{12,20},{16,24},{20,28},{1,9},{5,13},{9,17},{1... | collective-permute-start | bytes 3145736 | tf_op jit(solution)/shard_map/ppermute | solution.py:294
  162.5 54.1 %collective-permute-start.13 = (bf16[2,2,128,1024]{3,2,1,0:T(8,128)(2,1)}, bf16[2,2,128,1024]{3,2,1,0:T(8,128)(2,1)}, u32[]{:S(2)}, u32[]{:S(2)}) collective-permute-start(bf16[2,2,128,1024]{3,2,1,0:T(8,128)(2,1)} %pad_maximum_fusion.3.refs_4_), channel_id=1, source_target_pairs={{8,0},{12,4},{16,8},{20,12},{24,16},{28,20},{9,1},{13,5},{17,9},{2... | collective-permute-start | bytes 3145736 | tf_op jit(solution)/shard_map/ppermute | solution.py:294
  163.8 33.2 %collective-permute-start.8 = (bf16[2,128,1024]{2,1,0:T(8,128)(2,1)S(1)}, bf16[2,128,1024]{2,1,0:T(8,128)(2,1)S(1)}, u32[]{:S(2)}, u32[]{:S(2)}) collective-permute-start(bf16[2,128,1024]{2,1,0:T(8,128)(2,1)S(1)} %copy-done.25), channel_id=1, source_target_pairs={{0,4},{4,0},{8,12},{12,8},{16,20},{20,16},{24,28},{28,24},{1,5},{5... | collective-permute-start | bytes 1572872 | tf_op jit(solution)/shard_map/ppermute | solution.py:294
  164.4 23.0 %collective-permute-start.16 = (bf16[2,128,512]{2,1,0:T(8,128)(2,1)S(1)}, bf16[2,128,512]{2,1,0:T(8,128)(2,1)S(1)}, u32[]{:S(2)}, u32[]{:S(2)}) collective-permute-start(bf16[2,128,512]{2,1,0:T(8,128)(2,1)S(1)} %collective-permute-done.14.refs_5_), channel_id=1, source_target_pairs={{0,8},{4,12},{8,16},{12,20},{16,24},{20,28},{1,9},{5,13},{9,17},{1... | collective-permute-start | bytes 786440 | tf_op jit(solution)/shard_map/ppermute | solution.py:294
  169.0 0.7 copy-start.9
  169.7 22.8 %collective-permute-start.18 = (bf16[2,128,512]{2,1,0:T(8,128)(2,1)S(1)}, bf16[2,128,512]{2,1,0:T(8,128)(2,1)S(1)}, u32[]{:S(2)}, u32[]{:S(2)}) collective-permute-start(bf16[2,128,512]{2,1,0:T(8,128)(2,1)S(1)} %collective-permute-done.14.refs_5_), channel_id=1, source_target_pairs={{8,0},{12,4},{16,8},{20,12},{24,16},{28,20},{9,1},{13,5},{17,9},{2... | collective-permute-start | bytes 786440 | tf_op jit(solution)/shard_map/ppermute | solution.py:294
  171.7 20.8 %copy-start.10 = (bf16[2,128,512]{2,1,0:T(8,128)(2,1)S(1)}, bf16[2,128,512]{2,1,0:T(8,128)(2,1)}, u32[]{:S(2)}) copy-start(bf16[2,128,512]{2,1,0:T(8,128)(2,1)} %copy-done.9) | copy-start | bytes 786436
  171.7 20.8 %copy-start.12 = (bf16[2,128,512]{2,1,0:T(8,128)(2,1)S(1)}, bf16[2,128,512]{2,1,0:T(8,128)(2,1)}, u32[]{:S(2)}) copy-start(bf16[2,128,512]{2,1,0:T(8,128)(2,1)} %copy-done.11) | copy-start | bytes 786436
  171.8 26.2 %copy-start = (bf16[512,1536]{1,0:T(8,128)(2,1)}, bf16[512,1536]{1,0:T(8,128)(2,1)S(1)}, u32[]{:S(2)}) copy-start(bf16[512,1536]{1,0:T(8,128)(2,1)S(1)} %pad_maximum_fusion.refs_2_) | copy-start | bytes 4718596
  171.8 25.1 %copy-start.19 = (bf16[2,128,1024]{2,1,0:T(8,128)(2,1)S(1)}, bf16[2,128,1024]{2,1,0:T(8,128)(2,1)}, u32[]{:S(2)}) copy-start(bf16[2,128,1024]{2,1,0:T(8,128)(2,1)} %get-tuple-element.37) | copy-start | bytes 1572868
  196.8 8.0 %collective-permute-start.19 = (bf16[2,128,512]{2,1,0:T(8,128)(2,1)S(1)}, bf16[2,128,512]{2,1,0:T(8,128)(2,1)S(1)}, u32[]{:S(2)}, u32[]{:S(2)}) collective-permute-start(bf16[2,128,512]{2,1,0:T(8,128)(2,1)S(1)} %get-tuple-element.44), channel_id=1, source_target_pairs={{0,4},{4,0},{8,12},{12,8},{16,20},{20,16},{24,28},{28,24},{1,5},{5... | collective-permute-start | bytes 786440 | tf_op jit(solution)/shard_map/ppermute | solution.py:294
  198.0 55.2 %collective-permute-start.10 = (bf16[2,2,128,1024]{3,2,1,0:T(8,128)(2,1)}, bf16[2,2,128,1024]{3,2,1,0:T(8,128)(2,1)}, u32[]{:S(2)}, u32[]{:S(2)}) collective-permute-start(bf16[2,2,128,1024]{3,2,1,0:T(8,128)(2,1)} %pad_maximum_fusion.2.refs_4_), channel_id=1, source_target_pairs={{8,0},{12,4},{16,8},{20,12},{24,16},{28,20},{9,1},{13,5},{17,9},{2... | collective-permute-start | bytes 3145736 | tf_op jit(solution)/shard_map/ppermute | solution.py:294
  199.3 53.9 %collective-permute-start.9 = (bf16[2,2,128,1024]{3,2,1,0:T(8,128)(2,1)}, bf16[2,2,128,1024]{3,2,1,0:T(8,128)(2,1)}, u32[]{:S(2)}, u32[]{:S(2)}) collective-permute-start(bf16[2,2,128,1024]{3,2,1,0:T(8,128)(2,1)} %pad_maximum_fusion.2.refs_4_), channel_id=1, source_target_pairs={{0,8},{4,12},{8,16},{12,20},{16,24},{20,28},{1,9},{5,13},{9,17},{1... | collective-permute-start | bytes 3145736 | tf_op jit(solution)/shard_map/ppermute | solution.py:294
  204.9 1.9 copy-start.20
  204.9 20.6 %collective-permute-start.5 = (bf16[2,128,1024]{2,1,0:T(8,128)(2,1)}, bf16[2,128,1024]{2,1,0:T(8,128)(2,1)}, u32[]{:S(2)}, u32[]{:S(2)}) collective-permute-start(bf16[2,128,1024]{2,1,0:T(8,128)(2,1)} %get-tuple-element.36), channel_id=1, source_target_pairs={{0,4},{4,0},{8,12},{12,8},{16,20},{20,16},{24,28},{28,24},{1,5},{5... | collective-permute-start | bytes 1572872 | tf_op jit(solution)/shard_map/ppermute | solution.py:294
  206.7 9.9 %copy-start.3 = (s32[2]{0:T(128)S(1)}, s32[2]{0:T(128)}, u32[]{:S(2)}) copy-start(s32[2]{0:T(128)} %pad_add_fusion.2.info.refs_0_) | copy-start | bytes 28
  216.6 8.8 %copy-start.18 = (bf16[2,128,1024]{2,1,0:T(8,128)(2,1)S(1)}, bf16[2,128,1024]{2,1,0:T(8,128)(2,1)}, u32[]{:S(2)}) copy-start(bf16[2,128,1024]{2,1,0:T(8,128)(2,1)} %get-tuple-element.35) | copy-start | bytes 1572868
  225.4 9.2 %collective-permute-start.20 = (bf16[2,128,1024]{2,1,0:T(8,128)(2,1)S(1)}, bf16[2,128,1024]{2,1,0:T(8,128)(2,1)S(1)}, u32[]{:S(2)}, u32[]{:S(2)}) collective-permute-start(bf16[2,128,1024]{2,1,0:T(8,128)(2,1)S(1)} %get-tuple-element.48), channel_id=1, source_target_pairs={{0,4},{4,0},{8,12},{12,8},{16,20},{20,16},{24,28},{28,24},{1,5},{5... | collective-permute-start | bytes 1572872 | tf_op jit(solution)/shard_map/ppermute | solution.py:294
  226.6 64.8 %collective-permute-start.6 = (bf16[2,2,128,1024]{3,2,1,0:T(8,128)(2,1)S(1)}, bf16[2,2,128,1024]{3,2,1,0:T(8,128)(2,1)}, u32[]{:S(2)}, u32[]{:S(2)}) collective-permute-start(bf16[2,2,128,1024]{3,2,1,0:T(8,128)(2,1)S(1)} %pad_maximum_fusion.1.refs_4_), channel_id=1, source_target_pairs={{0,8},{4,12},{8,16},{12,20},{16,24},{20,28},{1,9},{5,13},{9,17},{1... | collective-permute-start | bytes 3145736 | tf_op jit(solution)/shard_map/ppermute | solution.py:294
  229.8 61.6 %collective-permute-start.7 = (bf16[2,2,128,1024]{3,2,1,0:T(8,128)(2,1)S(1)}, bf16[2,2,128,1024]{3,2,1,0:T(8,128)(2,1)}, u32[]{:S(2)}, u32[]{:S(2)}) collective-permute-start(bf16[2,2,128,1024]{3,2,1,0:T(8,128)(2,1)S(1)} %pad_maximum_fusion.1.refs_4_), channel_id=1, source_target_pairs={{8,0},{12,4},{16,8},{20,12},{24,16},{28,20},{9,1},{13,5},{17,9},{2... | collective-permute-start | bytes 3145736 | tf_op jit(solution)/shard_map/ppermute | solution.py:294
  234.6 0.8 copy-start.16
  235.4 17.8 %copy-start.4 = (s32[2]{0:T(128)S(1)}, s32[2]{0:T(128)}, u32[]{:S(2)}) copy-start(s32[2]{0:T(128)} %pad_add_fusion.2.info.refs_0_) | copy-start | bytes 28
  262.0 10.8 %collective-permute-start.21 = (bf16[2,128,1024]{2,1,0:T(8,128)(2,1)S(1)}, bf16[2,128,1024]{2,1,0:T(8,128)(2,1)S(1)}, u32[]{:S(2)}, u32[]{:S(2)}) collective-permute-start(bf16[2,128,1024]{2,1,0:T(8,128)(2,1)S(1)} %get-tuple-element.52), channel_id=1, source_target_pairs={{0,4},{4,0},{8,12},{12,8},{16,20},{20,16},{24,28},{28,24},{1,5},{5... | collective-permute-start | bytes 1572872 | tf_op jit(solution)/shard_map/ppermute | solution.py:294
  262.0 37.9 %collective-permute-start.2 = (bf16[2,128,512]{2,1,0:T(8,128)(2,1)}, bf16[2,128,512]{2,1,0:T(8,128)(2,1)}, u32[]{:S(2)}, u32[]{:S(2)}) collective-permute-start(bf16[2,128,512]{2,1,0:T(8,128)(2,1)} %get-tuple-element.34), channel_id=1, source_target_pairs={{0,4},{4,0},{8,12},{12,8},{16,20},{20,16},{24,28},{28,24},{1,5},{5... | collective-permute-start | bytes 786440 | tf_op jit(solution)/shard_map/ppermute | solution.py:294
  272.8 0.8 copy-start.17
  273.6 17.8 %copy-start.5 = (s32[2]{0:T(128)S(1)}, s32[2]{0:T(128)}, u32[]{:S(2)}) copy-start(s32[2]{0:T(128)} %pad_add_fusion.2.info.refs_0_) | copy-start | bytes 28
  291.4 8.5 %copy-start.22 = (bf16[2,128,512]{2,1,0:T(8,128)(2,1)S(1)}, bf16[2,128,512]{2,1,0:T(8,128)(2,1)}, u32[]{:S(2)}) copy-start(bf16[2,128,512]{2,1,0:T(8,128)(2,1)} %get-tuple-element.33) | copy-start | bytes 786436
  300.0 9.2 %collective-permute-start.22 = (bf16[2,128,1024]{2,1,0:T(8,128)(2,1)S(1)}, bf16[2,128,1024]{2,1,0:T(8,128)(2,1)S(1)}, u32[]{:S(2)}, u32[]{:S(2)}) collective-permute-start(bf16[2,128,1024]{2,1,0:T(8,128)(2,1)S(1)} %get-tuple-element.56), channel_id=1, source_target_pairs={{0,4},{4,0},{8,12},{12,8},{16,20},{20,16},{24,28},{28,24},{1,5},{5... | collective-permute-start | bytes 1572872 | tf_op jit(solution)/shard_map/ppermute | solution.py:294
  301.0 26.8 %collective-permute-start.3 = (bf16[2,2,128,512]{3,2,1,0:T(8,128)(2,1)S(1)}, bf16[2,2,128,512]{3,2,1,0:T(8,128)(2,1)}, u32[]{:S(2)}, u32[]{:S(2)}) collective-permute-start(bf16[2,2,128,512]{3,2,1,0:T(8,128)(2,1)S(1)} %pad_maximum_fusion.4.refs_4_), channel_id=1, source_target_pairs={{0,8},{4,12},{8,16},{12,20},{16,24},{20,28},{1,9},{5,13},{9,17},{1... | collective-permute-start | bytes 1572872 | tf_op jit(solution)/shard_map/ppermute | solution.py:294
  303.7 24.1 %collective-permute-start.4 = (bf16[2,2,128,512]{3,2,1,0:T(8,128)(2,1)S(1)}, bf16[2,2,128,512]{3,2,1,0:T(8,128)(2,1)}, u32[]{:S(2)}, u32[]{:S(2)}) collective-permute-start(bf16[2,2,128,512]{3,2,1,0:T(8,128)(2,1)S(1)} %pad_maximum_fusion.4.refs_4_), channel_id=1, source_target_pairs={{8,0},{12,4},{16,8},{20,12},{24,16},{28,20},{9,1},{13,5},{17,9},{2... | collective-permute-start | bytes 1572872 | tf_op jit(solution)/shard_map/ppermute | solution.py:294
  309.1 0.8 copy-start.15
  309.9 17.8 %copy-start.1 = (bf16[512,1536]{1,0:T(8,128)(2,1)S(1)}, bf16[512,1536]{1,0:T(8,128)(2,1)}, u32[]{:S(2)}) copy-start(bf16[512,1536]{1,0:T(8,128)(2,1)} %copy-done) | copy-start | bytes 4718596
  309.9 17.8 %copy-start.6 = (s32[2]{0:T(128)S(1)}, s32[2]{0:T(128)}, u32[]{:S(2)}) copy-start(s32[2]{0:T(128)} %pad_add_fusion.2.info.refs_0_) | copy-start | bytes 28
  333.5 56.9 %collective-permute-start.24 = (f32[2,128,640]{2,1,0:T(8,128)S(1)}, f32[2,128,640]{2,1,0:T(8,128)S(1)}, u32[]{:S(2)}, u32[]{:S(2)}) collective-permute-start(f32[2,128,640]{2,1,0:T(8,128)S(1)} %slice_bitcast_fusion), channel_id=1, source_target_pairs={{0,4},{4,0},{8,12},{12,8},{16,20},{20,16},{24,28},{28,24},{1,5},{5... | collective-permute-start | bytes 1966088 | tf_op jit(solution)/shard_map/ppermute | solution.py:294
  333.6 46.4 %collective-permute-start.23 = (bf16[2,128,512]{2,1,0:T(8,128)(2,1)}, bf16[2,128,512]{2,1,0:T(8,128)(2,1)S(1)}, u32[]{:S(2)}, u32[]{:S(2)}) collective-permute-start(bf16[2,128,512]{2,1,0:T(8,128)(2,1)} %copy-done.13), channel_id=1, source_target_pairs={{0,4},{4,0},{8,12},{12,8},{16,20},{20,16},{24,28},{28,24},{1,5},{5... | collective-permute-start | bytes 786440 | tf_op jit(solution)/shard_map/ppermute | solution.py:294
  (3 other events, 2.1 us)

commit v2 on v1

v2 whole, which is shorter than its diff:
```python
import functools
import math

import jax
import jax.numpy as jnp
from jax import lax
from jax.experimental import pallas as pl
from jax.experimental.pallas import tpu as pltpu
from jax.sharding import PartitionSpec as P

RB = 512
NT = 128
VMEM = 20 * 1024 * 1024
PARTS = (2, 4, 4, 4, 2)
LOW, LOW_X, OWN, MATE, HIGH, HIGH_X = range(6)
IN_SMEM = pl.BlockSpec(memory_space=pltpu.SMEM)
IN_VMEM = pl.BlockSpec(memory_space=pltpu.VMEM)
ANYWHERE = pl.BlockSpec(memory_space=pl.ANY)


def split_kernel(half, off, size, info, whole, mine, other, sems):
    side = info[0]
    copies = []
    for which, out in ((0, mine), (1, other)):
        start = (side if which == 0 else 1 - side) * half + off
        source = whole.at[:, :, pl.ds(pl.multiple_of(start, 128), size)]
        copies.append(pltpu.make_async_copy(source, out, sems.at[which]))
    for copy in copies:
        copy.start()
    for copy in copies:
        copy.wait()


def split(info, whole, half, off, size):
    rows = whole.shape[1]
    piece = jax.ShapeDtypeStruct((2, rows, size), whole.dtype)
    return pl.pallas_call(
        functools.partial(split_kernel, half, off, size),
        out_shape=[piece, piece],
        in_specs=[IN_SMEM, ANYWHERE],
        out_specs=[IN_VMEM, IN_VMEM],
        scratch_shapes=[pltpu.SemaphoreType.DMA((2,))],
        compiler_params=pltpu.CompilerParams(vmem_limit_bytes=VMEM),
        cost_estimate=pl.CostEstimate(
            flops=0, bytes_accessed=8 * rows * size * 2, transcendentals=0
        ),
        name="split_columns",
    )(info, whole)


def place_kernel(half, off, size, info, whole_in, part, whole, sem):
    del whole_in
    start = (1 - info[0]) * half + off
    copy = pltpu.make_async_copy(
        part, whole.at[:, :, pl.ds(pl.multiple_of(start, 128), size)], sem
    )
    copy.start()
    copy.wait()


def place(info, whole, part, half, off):
    size = part.shape[2]
    return pl.pallas_call(
        functools.partial(place_kernel, half, off, size),
        out_shape=jax.ShapeDtypeStruct(whole.shape, whole.dtype),
        in_specs=[IN_SMEM, ANYWHERE, IN_VMEM],
        out_specs=ANYWHERE,
        scratch_shapes=[pltpu.SemaphoreType.DMA],
        input_output_aliases={1: 0},
        compiler_params=pltpu.CompilerParams(vmem_limit_bytes=VMEM),
        cost_estimate=pl.CostEstimate(
            flops=0, bytes_accessed=2 * part.size * 2, transcendentals=0
        ),
        name="place_columns",
    )(info, whole, part)


def chunk_kernel(conf, *refs):
    rows, size, stride, off, half, layout, first = conf
    refs = list(refs)
    info, wave, resp, ids = (refs.pop(0) for _ in range(4))
    count = max(ref for ref, _ in layout) + 1
    given = [refs.pop(0) for _ in range(count)]
    if not first:
        _, grad_in, corr_in = (refs.pop(0) for _ in range(3))
    whole, out_mate, grad_out, corr_out, ys, ms, out_own, sem = refs
    side, pos = info[0], info[1]
    mate = pos + 1 - 2 * side
    col0 = side * half + off
    blocks = (pos - 2, mate - 2, pos, mate, pos + 2, mate + 2)
    tile = min(size, RB)

    def record(slot, c, cols):
        ref, part = layout[slot]
        return given[ref][c, :, cols] if part is None else given[ref][part, c, :, cols]

    def hits(slot):
        shots = blocks[slot] * rows + lax.broadcasted_iota(jnp.int32, (rows, size), 0)
        cols = col0 + lax.broadcasted_iota(jnp.int32, (rows, size), 1)
        return shots * stride == cols

    def meets(slot):
        low = blocks[slot] * rows * stride
        return (low < col0 + size) & (low + rows * stride > col0)

    for slot in range(6):
        at = slice(slot * rows, (slot + 1) * rows)
        for c in range(2):
            ys[at, c * size : (c + 1) * size] = record(slot, c, slice(None))

        @pl.when(meets(slot))
        def _(slot=slot, at=at):
            hit = hits(slot)
            for c in range(2):
                cols = slice(c * size, (c + 1) * size)
                direct = jnp.where(hit, wave[c], 0.0)
                ys[at, cols] = (ys[at, cols].astype(jnp.float32) - direct).astype(jnp.bfloat16)

    lists = ids[...]
    entry = lax.broadcasted_iota(jnp.int32, lists.shape, 1)
    listed = (entry < lists[:, -1:]) & (entry < lists.shape[1] - 1)
    for t in range(size // tile):
        cols = slice(t * tile, (t + 1) * tile)
        cols_im = slice(size + t * tile, size + (t + 1) * tile)
        y = jnp.concatenate([ys[:, cols], ys[:, cols_im]], axis=0)
        fit = jnp.dot(resp[...], y, preferred_element_type=jnp.float32)
        recorded = listed & (lists == (col0 + t * tile) // RB)
        covered = jnp.max(jnp.where(recorded, 1.0, 0.0), axis=1, keepdims=True)
        for which, slot in ((0, OWN), (1, MATE)):
            mask = covered[which * rows : (which + 1) * rows]
            pair = []
            for c in range(2):
                at = which * 2 + c
                value = record(slot, c, cols).astype(jnp.float32) + fit[at * rows : (at + 1) * rows]
                pair.append((mask * value).astype(jnp.bfloat16))
                (out_own if which == 0 else out_mate)[c, :, cols] = pair[c]
            at = slice(which * 2 * rows, (which * 2 + 1) * rows)
            ms[at, cols] = pair[0]
            ms[at, cols_im] = pair[1]
            at = slice((which * 2 + 1) * rows, (which * 2 + 2) * rows)
            ms[at, cols] = pair[1]
            ms[at, cols_im] = -pair[0]
    copy = pltpu.make_async_copy(
        out_own, whole.at[:, :, pl.ds(pl.multiple_of(col0, 128), size)], sem
    )
    copy.start()
    across = (((1,), (1,)), ((), ()))
    total = lax.dot_general(ms[...], ys[...], across, preferred_element_type=jnp.float32)
    grad_out[...] = total if first else grad_in[...] + total
    corr_out[...] = jnp.zeros_like(corr_out) if first else corr_in[...]

    for slot in range(6):

        @pl.when(meets(slot))
        def _(slot=slot):
            one = jnp.where(hits(slot), 1.0, 0.0).astype(jnp.bfloat16)
            at_shots = lax.dot_general(
                ms[:, :size], one, across, preferred_element_type=jnp.float32
            )
            for c in range(2):
                at = c * 6 * rows + slot * rows
                x = resp[:, at : at + rows].astype(jnp.float32)
                terms = (x * at_shots).reshape(-1, 8, rows)
                corr_out[c] -= jnp.sum(terms, axis=0)

    copy.wait()


def chunk(info, wave, resp, ids, arrays, layout, carry, off, size, half, width, stride, rows, band):
    first = carry is None
    conf = (rows, size, stride, off, half, layout, first)
    args = [info, wave, resp, ids, *arrays]
    in_specs = [IN_SMEM, IN_SMEM] + [IN_VMEM] * (2 + len(arrays))
    aliases = {}
    if not first:
        aliases = {len(args): 0, len(args) + 1: 2, len(args) + 2: 3}
        args += list(carry)
        in_specs += [ANYWHERE, IN_VMEM, IN_VMEM]
    macs = 2 * resp.shape[0] * resp.shape[1] * size
    return pl.pallas_call(
        functools.partial(chunk_kernel, conf),
        out_shape=[
            jax.ShapeDtypeStruct((2, rows, width), jnp.bfloat16),
            jax.ShapeDtypeStruct((2, rows, size), jnp.bfloat16),
            jax.ShapeDtypeStruct((4 * rows, 6 * rows), jnp.float32),
            jax.ShapeDtypeStruct((2, 8, rows), jnp.float32),
        ],
        in_specs=in_specs,
        out_specs=[ANYWHERE, IN_VMEM, IN_VMEM, IN_VMEM],
        scratch_shapes=[
            pltpu.VMEM((6 * rows, 2 * size), jnp.bfloat16),
            pltpu.VMEM((4 * rows, 2 * size), jnp.bfloat16),
            pltpu.VMEM((2, rows, size), jnp.bfloat16),
            pltpu.SemaphoreType.DMA,
        ],
        input_output_aliases=aliases,
        compiler_params=pltpu.CompilerParams(vmem_limit_bytes=VMEM),
        cost_estimate=pl.CostEstimate(
            flops=2 * macs, bytes_accessed=16 * rows * size * 2, transcendentals=0
        ),
        name="residual_chunk",
    )(*args)


def in_band_order(grad, side, rows):
    even = side == 0
    slots = [grad[:, s * rows : (s + 1) * rows].reshape(2, 2, rows, rows) for s in range(6)]

    def pick(which, a, b):
        return jnp.where(even, slots[a][which], slots[b][which])

    own = [slots[LOW][0], pick(0, LOW_X, MATE), slots[OWN][0], pick(0, MATE, HIGH_X), slots[HIGH][0]]
    mate = [
        slots[LOW_X][1], pick(1, OWN, LOW), slots[MATE][1], pick(1, HIGH, OWN), slots[HIGH_X][1]
    ]
    return jnp.concatenate(own, axis=2), jnp.concatenate(mate, axis=2)


def total_over(value, axis):
    size = lax.axis_size(axis)
    if size & (size - 1):
        return lax.psum(value, axis)
    step = 1
    while step < size:
        value = value + lax.ppermute(value, axis, [(i, i ^ step) for i in range(size)])
        step *= 2
    return value


def responses(own, mate, side, rows):
    even = side == 0

    def piece(a, k):
        return a[:, :, k * rows : (k + 1) * rows]

    none = jnp.zeros_like(piece(own, 0))
    o = [piece(own, k) for k in range(5)]
    m = [piece(mate, k) for k in range(5)]
    table = [
        [o[0], jnp.where(even, o[1], none), o[2], jnp.where(even, o[3], o[1]), o[4],
         jnp.where(even, none, o[3])],
        [jnp.where(even, none, m[1]), m[0], jnp.where(even, m[1], m[3]), m[2],
         jnp.where(even, m[3], none), m[4]],
    ]
    lines = []
    for line in table:
        lines.append(jnp.concatenate([p[0] for p in line] + [-p[1] for p in line], axis=1))
        lines.append(jnp.concatenate([p[1] for p in line] + [p[0] for p in line], axis=1))
    return jnp.concatenate(lines, axis=0)


def on_device(data, primaries, wavelet, cover_ids, cover_counts):
    record = data[0]
    _, rows, width = record.shape
    band = primaries.shape[3]
    devices = lax.axis_size("shot")
    shot_count = devices * rows
    stride = width // shot_count
    half = width // 2
    position = lax.axis_index("shot").astype(jnp.int32)
    freq_index = lax.axis_index("freq")
    side = position % 2
    info = jnp.stack([side, position])
    unit = half // sum(PARTS)
    cuts, off = [], 0
    for part in PARTS:
        cuts.append((off, part * unit))
        off += part * unit

    swap = [(i, i ^ 1) for i in range(devices)]
    up = [(i, i + 2) for i in range(devices - 2)]
    down = [(i + 2, i) for i in range(devices - 2)]

    def send(a, route):
        return lax.ppermute(a, "shot", route)

    pieces = [split(info, record, half, off, size) for off, size in cuts]
    response = primaries[0]
    lists = jnp.concatenate([cover_ids, cover_counts[:, None]], axis=1)
    resp = responses(response, send(response, swap), side, rows)
    ids = jnp.concatenate([lists, send(lists, swap)], axis=0)
    wave = wavelet[0]

    carry = None
    for n, (off, size) in enumerate(cuts):
        mine, other = pieces[n]
        theirs = send(other, swap)
        if n == 0:
            arrays = [
                mine, theirs, send(mine, up), send(theirs, up), send(mine, down), send(theirs, down)
            ]
            layout = ((2, None), (3, None), (0, None), (1, None), (4, None), (5, None))
        else:
            both = jnp.stack([mine, theirs])
            arrays = [both, send(both, up), send(both, down)]
            layout = ((1, 0), (1, 1), (0, 0), (0, 1), (2, 0), (2, 1))
        whole, back, grad, corr = chunk(
            info, wave, resp, ids, arrays, layout, carry,
            off, size, half, width, stride, rows, band,
        )
        whole = place(info, whole, send(back, swap), half, off)
        carry = (whole, grad, corr)

    grad_own, grad_mate = in_band_order(grad, side, rows)
    gradient = grad_own + send(grad_mate, swap)
    total_re, total_im = jnp.sum(corr[0]), jnp.sum(corr[1])
    times = jnp.arange(NT, dtype=jnp.int32).astype(jnp.float32)
    phase = 2.0 * math.pi * (freq_index + 1).astype(jnp.float32) * times / NT
    scale = 1.0 / math.sqrt(shot_count * band)
    series = total_re * jnp.cos(phase) - total_im * jnp.sin(phase)
    wavelet_grad = total_over(total_over(series, "freq"), "shot") * scale
    return (whole[None], gradient[None], wavelet_grad)


def solution(mesh):
    in_specs = (
        P("freq", None, "shot", None),
        P("freq", None, "shot", None),
        P("freq", None),
        P("shot", None),
        P("shot"),
    )
    out_specs = (P("freq", None, "shot", None), P("freq", None, "shot", None), P())
    return jax.shard_map(
        on_device, mesh=mesh, in_specs=in_specs, out_specs=out_specs, check_vma=False
    )
```

time: 392 us -> 192 us (0.49)
  Pallas kernels: 239 us -> 38.3 us
  blocking collectives: 41.8 us -> 0 us
  waiting for transfers between devices: 48.6 us -> 78.8 us
  starting transfers between devices: 45 us -> 53.3 us
    pallas_call x2 -> x5, Pallas kernels: 131 us -> 3.98 us  [split(): pl.pallas_call(functools.partial(split_kernel, half, off, size), out_shap...]
    pallas_call x5, Pallas kernels: 72.9 us -> 7.06 us  [place(): pl.pallas_call(functools.partial(place_kernel, half, off, size), out_shap...]
    psum x1 -> x0, blocking collectives: 41.8 us -> none  [on_device(): wavelet_grad = lax.psum(series, ('shot', 'freq')) * scale]
    ppermute x0 -> x5, waiting for transfers between devices: none -> 19.5 us  [total_over(): lax.ppermute(value, axis, [(i, i ^ step) for i in range(size)])]
    ppermute x25, waiting for transfers between devices: 48.6 us -> 59.3 us  [send(): return lax.ppermute(a, 'shot', route)]
    pallas_call x5, Pallas kernels: 35.4 us -> 27.3 us  [chunk(): pl.pallas_call(functools.partial(chunk_kernel, conf), out_shape=[jax.Shap...]
    ppermute x0 -> x5, starting transfers between devices: none -> 6.5 us  [total_over(): lax.ppermute(value, axis, [(i, i ^ step) for i in range(size)])]
    unnamed x76 -> x66, local copies, waits for them, and re-layouts: 5.58 us -> 8.34 us
  transfers between devices with their start and end apart: 25 -> 30, of which waited for: 6 -> 14; matrix products, arithmetic and copies ran while one was open for 2% -> 4% of each run, Pallas kernels for 55% -> 18%
where the time goes in v2:
time: 192 us; the launch traced here: 191 us
  waiting for transfers between devices  78.8 us (41%)
  starting transfers between devices  53.3 us (28%)
  Pallas kernels  38.3 us (20%)
  other arithmetic  10 us (5%)
  local copies, waits for them, and re-layouts  9.21 us (5%)
    ppermute x25, waiting for transfers between devices, send(): return lax.ppermute(a, 'shot', route)  59.3 us
    ppermute x25, starting transfers between devices, send(): return lax.ppermute(a, 'shot', route)  46.8 us
    pallas_call x5, Pallas kernels, chunk(): pl.pallas_call(functools.partial(chunk_kernel, conf), out_shape=[jax.Shap...  27.3 us
    ppermute x5, waiting for transfers between devices, total_over(): lax.ppermute(value, axis, [(i, i ^ step) for i in range(size)])  19.5 us
    unnamed x66, local copies, waits for them, and re-layouts  8.34 us
    pallas_call x5, Pallas kernels, place(): pl.pallas_call(functools.partial(place_kernel, half, off, size), out_shap...  7.06 us
    ppermute x5, starting transfers between devices, total_over(): lax.ppermute(value, axis, [(i, i ^ step) for i in range(size)])  6.5 us
    pallas_call x5, Pallas kernels, split(): pl.pallas_call(functools.partial(split_kernel, half, off, size), out_shap...  3.98 us
  transfers between devices with their start and end apart: 30, of which 14 were waited for; matrix products, arithmetic and copies ran while one was open for 4% of the time, Pallas kernels for 18%

profile of v2, /device:TPU:0, one launch (start us, length us, event | category | flops | bytes accessed | tf_op | source)
XLA Modules:
  0.0 191.0 jit_solution(7991452848544324956)
XLA Ops:
  0.7 2.2 %copy-done = bf16[1,2,128,8192]{3,2,1,0:T(8,128)(2,1)S(1)} copy-done((bf16[1,2,128,8192]{3,2,1,0:T(8,128)(2,1)S(1)}, bf16[1,2,128,8192]{3,2,1,0:T(8,128)(2,1)}, u32[]{:S(2)}) %copy-start) | copy-done | bytes 4194328
  3.5 4.9 %collective-permute-start.15 = (bf16[2,128,512]{2,1,0:T(8,128)(2,1)S(1)}, bf16[2,128,512]{2,1,0:T(8,128)(2,1)S(1)}, u32[]{:S(2)}, u32[]{:S(2)}) collective-permute-start(bf16[2,128,512]{2,1,0:T(8,128)(2,1)S(1)} %get-tuple-element.41.refs_4_), channel_id=1, source_target_pairs={{0,8},{4,12},{8,16},{12,20},{16,24},{20,28},{1,9},{5,13},{9,17},{1... | collective-permute-start | bytes 786440 | tf_op jit(solution)/shard_map/ppermute | solution.py:275
  8.5 1.3 collective-permute-start.17
  9.8 1.6 collective-permute-start
  12.5 1.5 collective-permute-start.1
  15.1 2.2 %copy-done.1 = bf16[1,2,128,8192]{3,2,1,0:T(8,128)(2,1)S(1)} copy-done((bf16[1,2,128,8192]{3,2,1,0:T(8,128)(2,1)S(1)}, bf16[1,2,128,8192]{3,2,1,0:T(8,128)(2,1)}, u32[]{:S(2)}) %copy-start.1) | copy-done | bytes 4194328
  17.9 1.4 split_columns.7
  20.2 4.6 %collective-permute-done.1 = s32[128,9]{0,1:T(8,128)S(1)} collective-permute-done((s32[128,9]{0,1:T(8,128)}, s32[128,9]{0,1:T(8,128)S(1)}, u32[]{:S(2)}, u32[]{:S(2)}) %collective-permute-start.1) | collective-permute-done | bytes 4640 | tf_op jit(solution)/shard_map/ppermute | solution.py:275
  24.8 1.5 collective-permute-start.11
  28.2 9.2 %collective-permute-done.11 = bf16[2,128,1024]{2,1,0:T(8,128)(2,1)} collective-permute-done((bf16[2,128,1024]{2,1,0:T(8,128)(2,1)S(1)}, bf16[2,128,1024]{2,1,0:T(8,128)(2,1)}, u32[]{:S(2)}, u32[]{:S(2)}) %collective-permute-start.11) | collective-permute-done | bytes 524320 | tf_op jit(solution)/shard_map/ppermute | solution.py:275
  38.6 4.0 %collective-permute-start.12 = (bf16[2,2,128,1024]{3,2,1,0:T(8,128)(2,1)S(1)}, bf16[2,2,128,1024]{3,2,1,0:T(8,128)(2,1)S(1)}, u32[]{:S(2)}, u32[]{:S(2)}) collective-permute-start(bf16[2,2,128,1024]{3,2,1,0:T(8,128)(2,1)S(1)} %pad_maximum_fusion.3.refs_4_), channel_id=1, source_target_pairs={{0,8},{4,12},{8,16},{12,20},{16,24},{20,28},{1,9},{5,13},{9,17},{1... | collective-permute-start | bytes 3145736 | tf_op jit(solution)/shard_map/ppermute | solution.py:275
  42.6 1.3 collective-permute-start.13
  43.9 1.6 collective-permute-start.8
  46.2 4.5 %collective-permute-start.16 = (bf16[2,128,512]{2,1,0:T(8,128)(2,1)S(1)}, bf16[2,128,512]{2,1,0:T(8,128)(2,1)S(1)}, u32[]{:S(2)}, u32[]{:S(2)}) collective-permute-start(bf16[2,128,512]{2,1,0:T(8,128)(2,1)S(1)} %collective-permute-done.14.refs_5_), channel_id=1, source_target_pairs={{0,8},{4,12},{8,16},{12,20},{16,24},{20,28},{1,9},{5,13},{9,17},{1... | collective-permute-start | bytes 786440 | tf_op jit(solution)/shard_map/ppermute | solution.py:275
  51.5 1.3 collective-permute-start.18
  53.6 14.5 %collective-permute-done.16.refs_7_ = bf16[2,128,512]{2,1,0:T(8,128)(2,1)S(1)} collective-permute-done((bf16[2,128,512]{2,1,0:T(8,128)(2,1)S(1)}, bf16[2,128,512]{2,1,0:T(8,128)(2,1)S(1)}, u32[]{:S(2)}, u32[]{:S(2)}) %collective-permute-start.16) | collective-permute-done | bytes 262176 | tf_op jit(solution)/shard_map/ppermute | solution.py:275
  68.1 4.2 %collective-permute-done.18.refs_9_ = bf16[2,128,512]{2,1,0:T(8,128)(2,1)S(1)} collective-permute-done((bf16[2,128,512]{2,1,0:T(8,128)(2,1)S(1)}, bf16[2,128,512]{2,1,0:T(8,128)(2,1)S(1)}, u32[]{:S(2)}, u32[]{:S(2)}) %collective-permute-start.18) | collective-permute-done | bytes 262176 | tf_op jit(solution)/shard_map/ppermute | solution.py:275
  72.4 3.3 %residual_chunk.5 = (bf16[2,128,8192]{2,1,0:T(8,128)(2,1)}, bf16[2,128,512]{2,1,0:T(8,128)(2,1)S(1)}, f32[512,768]{1,0:T(8,128)S(1)}, f32[2,8,128]{2,1,0:T(8,128)S(1)}) custom-call(s32[2]{0:T(128)S(1)} %pad_add_fusion.2.info.refs_0_, f32[2]{0:T(128)S(1)} %bitcast.180, bf16[512,1536]{1,0:T(8,128)(2,1)S(1)} %pad_maximum_fusion.refs_2_, ...), custom_call_target="tpu_custom_call" | custom-call | flops 1610612736 | bytes 2097152 | tf_op jit(solution)/shard_map/residual_chunk/pallas_call | solution.py:180
  76.9 1.3 collective-permute-start.10
  78.2 4.6 %collective-permute-start.9 = (bf16[2,2,128,1024]{3,2,1,0:T(8,128)(2,1)S(1)}, bf16[2,2,128,1024]{3,2,1,0:T(8,128)(2,1)S(1)}, u32[]{:S(2)}, u32[]{:S(2)}) collective-permute-start(bf16[2,2,128,1024]{3,2,1,0:T(8,128)(2,1)S(1)} %pad_maximum_fusion.2.refs_4_), channel_id=1, source_target_pairs={{0,8},{4,12},{8,16},{12,20},{16,24},{20,28},{1,9},{5,13},{9,17},{1... | collective-permute-start | bytes 3145736 | tf_op jit(solution)/shard_map/ppermute | solution.py:275
  85.8 6.4 %residual_chunk.6 = (bf16[2,128,8192]{2,1,0:T(8,128)(2,1)}, bf16[2,128,1024]{2,1,0:T(8,128)(2,1)S(1)}, f32[512,768]{1,0:T(8,128)S(1)}, f32[2,8,128]{2,1,0:T(8,128)S(1)}) custom-call(s32[2]{0:T(128)S(1)} %pad_add_fusion.2.info.refs_0_, f32[2]{0:T(128)S(1)} %bitcast.181, ...), custom_call_target="tpu_custom_call", output_to_operand_aliasing={{0}: (7, {}), {2}: (8, {}), {3}: (9, {})} | custom-call | flops 3221225472 | bytes 4194304 | tf_op jit(solution)/shard_map/residual_chunk/pallas_call | solution.py:180
  92.3 4.3 %collective-permute-done.5 = bf16[2,128,1024]{2,1,0:T(8,128)(2,1)S(1)} collective-permute-done((bf16[2,128,1024]{2,1,0:T(8,128)(2,1)S(1)}, bf16[2,128,1024]{2,1,0:T(8,128)(2,1)S(1)}, u32[]{:S(2)}, u32[]{:S(2)}) %collective-permute-start.5) | collective-permute-done | bytes 524320 | tf_op jit(solution)/shard_map/ppermute | solution.py:275
  96.7 3.5 %collective-permute-start.6 = (bf16[2,2,128,1024]{3,2,1,0:T(8,128)(2,1)S(1)}, bf16[2,2,128,1024]{3,2,1,0:T(8,128)(2,1)S(1)}, u32[]{:S(2)}, u32[]{:S(2)}) collective-permute-start(bf16[2,2,128,1024]{3,2,1,0:T(8,128)(2,1)S(1)} %pad_maximum_fusion.1.refs_4_), channel_id=1, source_target_pairs={{0,8},{4,12},{8,16},{12,20},{16,24},{20,28},{1,9},{5,13},{9,17},{1... | collective-permute-start | bytes 3145736 | tf_op jit(solution)/shard_map/ppermute | solution.py:275
  100.2 1.3 collective-permute-start.7
  101.5 3.0 %collective-permute-done.20.part = bf16[2,128,1024]{2,1,0:T(8,128)(2,1)S(1)} collective-permute-done((bf16[2,128,1024]{2,1,0:T(8,128)(2,1)S(1)}, bf16[2,128,1024]{2,1,0:T(8,128)(2,1)S(1)}, u32[]{:S(2)}, u32[]{:S(2)}) %collective-permute-start.20) | collective-permute-done | bytes 524320 | tf_op jit(solution)/shard_map/ppermute | solution.py:275
  104.5 1.3 place_columns.6.refs_7_
  106.4 6.2 %residual_chunk.7 = (bf16[2,128,8192]{2,1,0:T(8,128)(2,1)}, bf16[2,128,1024]{2,1,0:T(8,128)(2,1)S(1)}, f32[512,768]{1,0:T(8,128)S(1)}, f32[2,8,128]{2,1,0:T(8,128)S(1)}) custom-call(s32[2]{0:T(128)S(1)} %pad_add_fusion.2.info.refs_0_, f32[2]{0:T(128)S(1)} %bitcast.182, ...), custom_call_target="tpu_custom_call", output_to_operand_aliasing={{0}: (7, {}), {2}: (8, {}), {3}: (9, {})} | custom-call | flops 3221225472 | bytes 4194304 | tf_op jit(solution)/shard_map/residual_chunk/pallas_call | solution.py:180
  113.3 2.1 %collective-permute-start.2 = (bf16[2,128,512]{2,1,0:T(8,128)(2,1)S(1)}, bf16[2,128,512]{2,1,0:T(8,128)(2,1)S(1)}, u32[]{:S(2)}, u32[]{:S(2)}) collective-permute-start(bf16[2,128,512]{2,1,0:T(8,128)(2,1)S(1)} %get-tuple-element.34), channel_id=1, source_target_pairs={{0,4},{4,0},{8,12},{12,8},{16,20},{20,16},{24,28},{28,24},{1,5},{5... | collective-permute-start | bytes 786440 | tf_op jit(solution)/shard_map/ppermute | solution.py:275
  115.4 10.3 %collective-permute-done.21.part = bf16[2,128,1024]{2,1,0:T(8,128)(2,1)S(1)} collective-permute-done((bf16[2,128,1024]{2,1,0:T(8,128)(2,1)S(1)}, bf16[2,128,1024]{2,1,0:T(8,128)(2,1)S(1)}, u32[]{:S(2)}, u32[]{:S(2)}) %collective-permute-start.21) | collective-permute-done | bytes 524320 | tf_op jit(solution)/shard_map/ppermute | solution.py:275
  125.7 1.3 place_columns.7.refs_7_
  127.0 7.2 %residual_chunk.8 = (bf16[2,128,8192]{2,1,0:T(8,128)(2,1)}, bf16[2,128,1024]{2,1,0:T(8,128)(2,1)}, f32[512,768]{1,0:T(8,128)S(1)}, f32[2,8,128]{2,1,0:T(8,128)S(1)}) custom-call(s32[2]{0:T(128)S(1)} %pad_add_fusion.2.info.refs_0_, f32[2]{0:T(128)S(1)} %bitcast.183, ...), custom_call_target="tpu_custom_call", output_to_operand_aliasing={{0}: (7, {}), {2}: (8, {}), {3}: (9, {})} | custom-call | flops 3221225472 | bytes 4194304 | tf_op jit(solution)/shard_map/residual_chunk/pallas_call | solution.py:180
  135.2 4.2 %collective-permute-start.3 = (bf16[2,2,128,512]{3,2,1,0:T(8,128)(2,1)}, bf16[2,2,128,512]{3,2,1,0:T(8,128)(2,1)}, u32[]{:S(2)}, u32[]{:S(2)}) collective-permute-start(bf16[2,2,128,512]{3,2,1,0:T(8,128)(2,1)} %pad_maximum_fusion.4.refs_4_), channel_id=1, source_target_pairs={{0,8},{4,12},{8,16},{12,20},{16,24},{20,28},{1,9},{5,13},{9,17},{1... | collective-permute-start | bytes 1572872 | tf_op jit(solution)/shard_map/ppermute | solution.py:275
  140.7 3.2 %collective-permute-done.22.part = bf16[2,128,1024]{2,1,0:T(8,128)(2,1)} collective-permute-done((bf16[2,128,1024]{2,1,0:T(8,128)(2,1)}, bf16[2,128,1024]{2,1,0:T(8,128)(2,1)}, u32[]{:S(2)}, u32[]{:S(2)}) %collective-permute-start.22) | collective-permute-done | bytes 524320 | tf_op jit(solution)/shard_map/ppermute | solution.py:275
  143.9 1.9 place_columns.8.refs_7_
  145.7 5.3 %collective-permute-done.4.refs_6_ = bf16[2,2,128,512]{3,2,1,0:T(8,128)(2,1)} collective-permute-done((bf16[2,2,128,512]{3,2,1,0:T(8,128)(2,1)}, bf16[2,2,128,512]{3,2,1,0:T(8,128)(2,1)}, u32[]{:S(2)}, u32[]{:S(2)}) %collective-permute-start.4) | collective-permute-done | bytes 524320 | tf_op jit(solution)/shard_map/ppermute | solution.py:275
  151.1 4.1 %residual_chunk.9 = (bf16[2,128,8192]{2,1,0:T(8,128)(2,1)}, bf16[2,128,512]{2,1,0:T(8,128)(2,1)S(1)}, f32[512,768]{1,0:T(8,128)S(1)}, f32[2,8,128]{2,1,0:T(8,128)S(1)}) custom-call(s32[2]{0:T(128)S(1)} %pad_add_fusion.2.info.refs_0_, f32[2]{0:T(128)S(1)} %bitcast.184, ...), custom_call_target="tpu_custom_call", output_to_operand_aliasing={{0}: (7, {}), {2}: (8, {}), {3}: (9, {})} | custom-call | flops 1610612736 | bytes 2097152 | tf_op jit(solution)/shard_map/residual_chunk/pallas_call | solution.py:180
  155.8 1.3 multiply_subtract_fusion
  157.5 1.4 collective-permute-start.24
  159.6 1.3 fusion.1
  161.0 1.6 collective-permute-start.26
  162.6 2.0 %collective-permute-done.26 = f32[128]{0:T(128)S(1)} collective-permute-done((f32[128]{0:T(128)S(1)}, f32[128]{0:T(128)S(1)}, u32[]{:S(2)}, u32[]{:S(2)}) %collective-permute-start.26) | collective-permute-done | bytes 544 | tf_op jit(solution)/shard_map/ppermute | solution.py:225
  164.6 1.3 fusion.2
  165.9 1.4 collective-permute-start.27
  167.3 13.0 %collective-permute-done.27 = f32[128]{0:T(128)S(1)} collective-permute-done((f32[128]{0:T(128)S(1)}, f32[128]{0:T(128)S(1)}, u32[]{:S(2)}, u32[]{:S(2)}) %collective-permute-start.27) | collective-permute-done | bytes 544 | tf_op jit(solution)/shard_map/ppermute | solution.py:225
  180.3 2.0 %collective-permute-start.28 = (f32[128]{0:T(128)S(1)}, f32[128]{0:T(128)S(1)}, u32[]{:S(2)}, u32[]{:S(2)}) collective-permute-start(f32[128]{0:T(128)S(1)} %add.30), channel_id=1, source_target_pairs={{0,8},{4,12},{8,0},{12,4},{16,24},{20,28},{24,16},{28,20},{1,9},{5... | collective-permute-start | bytes 1544 | tf_op jit(solution)/shard_map/ppermute | solution.py:225
  182.4 1.5 collective-permute-done.28
  183.9 1.4 collective-permute-start.29
  185.4 3.0 %collective-permute-done.29 = f32[128]{0:T(128)S(1)} collective-permute-done((f32[128]{0:T(128)S(1)}, f32[128]{0:T(128)S(1)}, u32[]{:S(2)}, u32[]{:S(2)}) %collective-permute-start.29) | collective-permute-done | bytes 544 | tf_op jit(solution)/shard_map/ppermute | solution.py:225
  (129 shorter events, 21.4 us)
Async XLA Ops:
  0.6 11.3 %copy-start.16 = (s32[128]{0:T(128)S(1)}, s32[128]{0:T(128)}, u32[]{:S(2)}) copy-start(s32[128]{0:T(128)} %param.9) | copy-start | bytes 1540
  0.6 11.3 %copy-start.15 = (s32[128,8]{0,1:T(8,128)S(1)}, s32[128,8]{0,1:T(8,128)}, u32[]{:S(2)}) copy-start(s32[128,8]{0,1:T(8,128)} %param.8) | copy-start | bytes 12292
  0.7 2.2 %copy-start = (bf16[1,2,128,8192]{3,2,1,0:T(8,128)(2,1)S(1)}, bf16[1,2,128,8192]{3,2,1,0:T(8,128)(2,1)}, u32[]{:S(2)}) copy-start(bf16[1,2,128,8192]{3,2,1,0:T(8,128)(2,1)} %param.5) | copy-start | bytes 12582916
  2.9 6.9 %copy-start.12 = (bf16[1,2,128,640]{3,2,1,0:T(8,128)(2,1)S(1)}, bf16[1,2,128,640]{3,2,1,0:T(8,128)(2,1)}, u32[]{:S(2)}) copy-start(bf16[1,2,128,640]{3,2,1,0:T(8,128)(2,1)} %param.6) | copy-start | bytes 983044
  3.5 42.0 %collective-permute-start.15 = (bf16[2,128,512]{2,1,0:T(8,128)(2,1)S(1)}, bf16[2,128,512]{2,1,0:T(8,128)(2,1)S(1)}, u32[]{:S(2)}, u32[]{:S(2)}) collective-permute-start(bf16[2,128,512]{2,1,0:T(8,128)(2,1)S(1)} %get-tuple-element.41.refs_4_), channel_id=1, source_target_pairs={{0,8},{4,12},{8,16},{12,20},{16,24},{20,28},{1,9},{5,13},{9,17},{1... | collective-permute-start | bytes 786440 | tf_op jit(solution)/shard_map/ppermute | solution.py:275
  8.5 42.3 %collective-permute-start.17 = (bf16[2,128,512]{2,1,0:T(8,128)(2,1)S(1)}, bf16[2,128,512]{2,1,0:T(8,128)(2,1)S(1)}, u32[]{:S(2)}, u32[]{:S(2)}) collective-permute-start(bf16[2,128,512]{2,1,0:T(8,128)(2,1)S(1)} %get-tuple-element.41.refs_4_), channel_id=1, source_target_pairs={{8,0},{12,4},{16,8},{20,12},{24,16},{28,20},{9,1},{13,5},{17,9},{2... | collective-permute-start | bytes 786440 | tf_op jit(solution)/shard_map/ppermute | solution.py:275
  9.8 18.0 %collective-permute-start = (bf16[2,128,640]{2,1,0:T(8,128)(2,1)S(1)}, bf16[2,128,640]{2,1,0:T(8,128)(2,1)S(1)}, u32[]{:S(2)}, u32[]{:S(2)}) collective-permute-start(bf16[2,128,640]{2,1,0:T(8,128)(2,1)S(1)} %bitcast.186), channel_id=1, source_target_pairs={{0,4},{4,0},{8,12},{12,8},{16,20},{20,16},{24,28},{28,24},{1,5},{5... | collective-permute-start | bytes 983048 | tf_op jit(solution)/shard_map/ppermute | solution.py:275
  11.4 32.6 %collective-permute-start.14 = (bf16[2,128,512]{2,1,0:T(8,128)(2,1)S(1)}, bf16[2,128,512]{2,1,0:T(8,128)(2,1)S(1)}, u32[]{:S(2)}, u32[]{:S(2)}) collective-permute-start(bf16[2,128,512]{2,1,0:T(8,128)(2,1)S(1)} %get-tuple-element.42), channel_id=1, source_target_pairs={{0,4},{4,0},{8,12},{12,8},{16,20},{20,16},{24,28},{28,24},{1,5},{5... | collective-permute-start | bytes 786440 | tf_op jit(solution)/shard_map/ppermute | solution.py:275
  12.5 12.3 %collective-permute-start.1 = (s32[128,9]{0,1:T(8,128)}, s32[128,9]{0,1:T(8,128)S(1)}, u32[]{:S(2)}, u32[]{:S(2)}) collective-permute-start(s32[128,9]{0,1:T(8,128)} %pad_add_fusion.1), channel_id=1, source_target_pairs={{0,4},{4,0},{8,12},{12,8},{16,20},{20,16},{24,28},{28,24},{1,5},{5... | collective-permute-start | bytes 13832 | tf_op jit(solution)/shard_map/ppermute | solution.py:275
  14.3 0.7 copy-start.13
  15.1 2.2 %copy-start.1 = (bf16[1,2,128,8192]{3,2,1,0:T(8,128)(2,1)S(1)}, bf16[1,2,128,8192]{3,2,1,0:T(8,128)(2,1)}, u32[]{:S(2)}) copy-start(bf16[1,2,128,8192]{3,2,1,0:T(8,128)(2,1)} %param.5) | copy-start | bytes 12582916
  17.9 8.4 %copy-start.17 = (s32[128]{0:T(128)S(1)}, s32[128]{0:T(128)}, u32[]{:S(2)}) copy-start(s32[128]{0:T(128)} %param.9) | copy-start | bytes 1540
  19.4 0.8 copy-start.3
  24.8 12.6 %collective-permute-start.11 = (bf16[2,128,1024]{2,1,0:T(8,128)(2,1)S(1)}, bf16[2,128,1024]{2,1,0:T(8,128)(2,1)}, u32[]{:S(2)}, u32[]{:S(2)}) collective-permute-start(bf16[2,128,1024]{2,1,0:T(8,128)(2,1)S(1)} %get-tuple-element.40), channel_id=1, source_target_pairs={{0,4},{4,0},{8,12},{12,8},{16,20},{20,16},{24,28},{28,24},{1,5},{5... | collective-permute-start | bytes 1572872 | tf_op jit(solution)/shard_map/ppermute | solution.py:275
  27.8 25.7 %copy-start.14 = (bf16[128,1536]{1,0:T(8,128)(2,1)S(1)}, bf16[128,1536]{1,0:T(8,128)(2,1)}, u32[]{:S(2)}) copy-start(bf16[128,1536]{1,0:T(8,128)(2,1)} %copy-done.13) | copy-start | bytes 1179652
  27.9 44.4 %copy-start.5 = (f32[1,2]{1,0:T(1,128)S(1)}, f32[1,2]{1,0:T(1,128)}, u32[]{:S(2)}) copy-start(f32[1,2]{1,0:T(1,128)} %param.7) | copy-start | bytes 28
  38.6 47.2 %collective-permute-start.12 = (bf16[2,2,128,1024]{3,2,1,0:T(8,128)(2,1)S(1)}, bf16[2,2,128,1024]{3,2,1,0:T(8,128)(2,1)S(1)}, u32[]{:S(2)}, u32[]{:S(2)}) collective-permute-start(bf16[2,2,128,1024]{3,2,1,0:T(8,128)(2,1)S(1)} %pad_maximum_fusion.3.refs_4_), channel_id=1, source_target_pairs={{0,8},{4,12},{8,16},{12,20},{16,24},{20,28},{1,9},{5,13},{9,17},{1... | collective-permute-start | bytes 3145736 | tf_op jit(solution)/shard_map/ppermute | solution.py:275
  42.6 43.2 %collective-permute-start.13 = (bf16[2,2,128,1024]{3,2,1,0:T(8,128)(2,1)S(1)}, bf16[2,2,128,1024]{3,2,1,0:T(8,128)(2,1)S(1)}, u32[]{:S(2)}, u32[]{:S(2)}) collective-permute-start(bf16[2,2,128,1024]{3,2,1,0:T(8,128)(2,1)S(1)} %pad_maximum_fusion.3.refs_4_), channel_id=1, source_target_pairs={{8,0},{12,4},{16,8},{20,12},{24,16},{28,20},{9,1},{13,5},{17,9},{2... | collective-permute-start | bytes 3145736 | tf_op jit(solution)/shard_map/ppermute | solution.py:275
  43.9 32.9 %collective-permute-start.8 = (bf16[2,128,1024]{2,1,0:T(8,128)(2,1)}, bf16[2,128,1024]{2,1,0:T(8,128)(2,1)S(1)}, u32[]{:S(2)}, u32[]{:S(2)}) collective-permute-start(bf16[2,128,1024]{2,1,0:T(8,128)(2,1)} %get-tuple-element.38), channel_id=1, source_target_pairs={{0,4},{4,0},{8,12},{12,8},{16,20},{20,16},{24,28},{28,24},{1,5},{5... | collective-permute-start | bytes 1572872 | tf_op jit(solution)/shard_map/ppermute | solution.py:275
  45.5 0.7 copy-start.6
  46.2 21.9 %collective-permute-start.16 = (bf16[2,128,512]{2,1,0:T(8,128)(2,1)S(1)}, bf16[2,128,512]{2,1,0:T(8,128)(2,1)S(1)}, u32[]{:S(2)}, u32[]{:S(2)}) collective-permute-start(bf16[2,128,512]{2,1,0:T(8,128)(2,1)S(1)} %collective-permute-done.14.refs_5_), channel_id=1, source_target_pairs={{0,8},{4,12},{8,16},{12,20},{16,24},{20,28},{1,9},{5,13},{9,17},{1... | collective-permute-start | bytes 786440 | tf_op jit(solution)/shard_map/ppermute | solution.py:275
  50.8 21.6 %copy-start.7 = (bf16[2,128,512]{2,1,0:T(8,128)(2,1)S(1)}, bf16[2,128,512]{2,1,0:T(8,128)(2,1)}, u32[]{:S(2)}) copy-start(bf16[2,128,512]{2,1,0:T(8,128)(2,1)} %copy-done.6) | copy-start | bytes 786436
  50.8 0.7 copy-start.8
  51.5 20.8 %collective-permute-start.18 = (bf16[2,128,512]{2,1,0:T(8,128)(2,1)S(1)}, bf16[2,128,512]{2,1,0:T(8,128)(2,1)S(1)}, u32[]{:S(2)}, u32[]{:S(2)}) collective-permute-start(bf16[2,128,512]{2,1,0:T(8,128)(2,1)S(1)} %collective-permute-done.14.refs_5_), channel_id=1, source_target_pairs={{8,0},{12,4},{16,8},{20,12},{24,16},{28,20},{9,1},{13,5},{17,9},{2... | collective-permute-start | bytes 786440 | tf_op jit(solution)/shard_map/ppermute | solution.py:275
  52.8 0.7 copy-start.10
  53.5 18.8 %copy-start.9 = (bf16[2,128,512]{2,1,0:T(8,128)(2,1)S(1)}, bf16[2,128,512]{2,1,0:T(8,128)(2,1)}, u32[]{:S(2)}) copy-start(bf16[2,128,512]{2,1,0:T(8,128)(2,1)} %copy-done.8) | copy-start | bytes 786436
  53.5 18.8 %copy-start.11 = (bf16[2,128,512]{2,1,0:T(8,128)(2,1)S(1)}, bf16[2,128,512]{2,1,0:T(8,128)(2,1)}, u32[]{:S(2)}) copy-start(bf16[2,128,512]{2,1,0:T(8,128)(2,1)} %copy-done.10) | copy-start | bytes 786436
  53.6 23.2 %copy-start.4 = (bf16[2,128,1024]{2,1,0:T(8,128)(2,1)S(1)}, bf16[2,128,1024]{2,1,0:T(8,128)(2,1)}, u32[]{:S(2)}) copy-start(bf16[2,128,1024]{2,1,0:T(8,128)(2,1)} %copy-done.3) | copy-start | bytes 1572868
  72.3 10.5 %copy-start.2 = (bf16[1,2,128,8192]{3,2,1,0:T(8,128)(2,1)S(1)}, bf16[1,2,128,8192]{3,2,1,0:T(8,128)(2,1)}, u32[]{:S(2)}) copy-start(bf16[1,2,128,8192]{3,2,1,0:T(8,128)(2,1)} %param.5) | copy-start | bytes 12582916
  75.6 7.9 %collective-permute-start.19 = (bf16[2,128,512]{2,1,0:T(8,128)(2,1)S(1)}, bf16[2,128,512]{2,1,0:T(8,128)(2,1)S(1)}, u32[]{:S(2)}, u32[]{:S(2)}) collective-permute-start(bf16[2,128,512]{2,1,0:T(8,128)(2,1)S(1)} %get-tuple-element.44), channel_id=1, source_target_pairs={{0,4},{4,0},{8,12},{12,8},{16,20},{20,16},{24,28},{28,24},{1,5},{5... | collective-permute-start | bytes 786440 | tf_op jit(solution)/shard_map/ppermute | solution.py:275
  76.9 29.0 %collective-permute-start.10 = (bf16[2,2,128,1024]{3,2,1,0:T(8,128)(2,1)S(1)}, bf16[2,2,128,1024]{3,2,1,0:T(8,128)(2,1)S(1)}, u32[]{:S(2)}, u32[]{:S(2)}) collective-permute-start(bf16[2,2,128,1024]{3,2,1,0:T(8,128)(2,1)S(1)} %pad_maximum_fusion.2.refs_4_), channel_id=1, source_target_pairs={{8,0},{12,4},{16,8},{20,12},{24,16},{28,20},{9,1},{13,5},{17,9},{2... | collective-permute-start | bytes 3145736 | tf_op jit(solution)/shard_map/ppermute | solution.py:275
  78.2 28.2 %collective-permute-start.9 = (bf16[2,2,128,1024]{3,2,1,0:T(8,128)(2,1)S(1)}, bf16[2,2,128,1024]{3,2,1,0:T(8,128)(2,1)S(1)}, u32[]{:S(2)}, u32[]{:S(2)}) collective-permute-start(bf16[2,2,128,1024]{3,2,1,0:T(8,128)(2,1)S(1)} %pad_maximum_fusion.2.refs_4_), channel_id=1, source_target_pairs={{0,8},{4,12},{8,16},{12,20},{16,24},{20,28},{1,9},{5,13},{9,17},{1... | collective-permute-start | bytes 3145736 | tf_op jit(solution)/shard_map/ppermute | solution.py:275
  83.5 13.1 %collective-permute-start.5 = (bf16[2,128,1024]{2,1,0:T(8,128)(2,1)S(1)}, bf16[2,128,1024]{2,1,0:T(8,128)(2,1)S(1)}, u32[]{:S(2)}, u32[]{:S(2)}) collective-permute-start(bf16[2,128,1024]{2,1,0:T(8,128)(2,1)S(1)} %get-tuple-element.36), channel_id=1, source_target_pairs={{0,4},{4,0},{8,12},{12,8},{16,20},{20,16},{24,28},{28,24},{1,5},{5... | collective-permute-start | bytes 1572872 | tf_op jit(solution)/shard_map/ppermute | solution.py:275
  92.2 12.3 %collective-permute-start.20 = (bf16[2,128,1024]{2,1,0:T(8,128)(2,1)S(1)}, bf16[2,128,1024]{2,1,0:T(8,128)(2,1)S(1)}, u32[]{:S(2)}, u32[]{:S(2)}) collective-permute-start(bf16[2,128,1024]{2,1,0:T(8,128)(2,1)S(1)} %get-tuple-element.48), channel_id=1, source_target_pairs={{0,4},{4,0},{8,12},{12,8},{16,20},{20,16},{24,28},{28,24},{1,5},{5... | collective-permute-start | bytes 1572872 | tf_op jit(solution)/shard_map/ppermute | solution.py:275
  96.7 30.3 %collective-permute-start.6 = (bf16[2,2,128,1024]{3,2,1,0:T(8,128)(2,1)S(1)}, bf16[2,2,128,1024]{3,2,1,0:T(8,128)(2,1)S(1)}, u32[]{:S(2)}, u32[]{:S(2)}) collective-permute-start(bf16[2,2,128,1024]{3,2,1,0:T(8,128)(2,1)S(1)} %pad_maximum_fusion.1.refs_4_), channel_id=1, source_target_pairs={{0,8},{4,12},{8,16},{12,20},{16,24},{20,28},{1,9},{5,13},{9,17},{1... | collective-permute-start | bytes 3145736 | tf_op jit(solution)/shard_map/ppermute | solution.py:275
  100.2 26.8 %collective-permute-start.7 = (bf16[2,2,128,1024]{3,2,1,0:T(8,128)(2,1)S(1)}, bf16[2,2,128,1024]{3,2,1,0:T(8,128)(2,1)S(1)}, u32[]{:S(2)}, u32[]{:S(2)}) collective-permute-start(bf16[2,2,128,1024]{3,2,1,0:T(8,128)(2,1)S(1)} %pad_maximum_fusion.1.refs_4_), channel_id=1, source_target_pairs={{8,0},{12,4},{16,8},{20,12},{24,16},{28,20},{9,1},{13,5},{17,9},{2... | collective-permute-start | bytes 3145736 | tf_op jit(solution)/shard_map/ppermute | solution.py:275
  112.6 13.1 %collective-permute-start.21 = (bf16[2,128,1024]{2,1,0:T(8,128)(2,1)S(1)}, bf16[2,128,1024]{2,1,0:T(8,128)(2,1)S(1)}, u32[]{:S(2)}, u32[]{:S(2)}) collective-permute-start(bf16[2,128,1024]{2,1,0:T(8,128)(2,1)S(1)} %get-tuple-element.52), channel_id=1, source_target_pairs={{0,4},{4,0},{8,12},{12,8},{16,20},{20,16},{24,28},{28,24},{1,5},{5... | collective-permute-start | bytes 1572872 | tf_op jit(solution)/shard_map/ppermute | solution.py:275
  113.3 21.1 %collective-permute-start.2 = (bf16[2,128,512]{2,1,0:T(8,128)(2,1)S(1)}, bf16[2,128,512]{2,1,0:T(8,128)(2,1)S(1)}, u32[]{:S(2)}, u32[]{:S(2)}) collective-permute-start(bf16[2,128,512]{2,1,0:T(8,128)(2,1)S(1)} %get-tuple-element.34), channel_id=1, source_target_pairs={{0,4},{4,0},{8,12},{12,8},{16,20},{20,16},{24,28},{28,24},{1,5},{5... | collective-permute-start | bytes 786440 | tf_op jit(solution)/shard_map/ppermute | solution.py:275
  134.3 9.6 %collective-permute-start.22 = (bf16[2,128,1024]{2,1,0:T(8,128)(2,1)}, bf16[2,128,1024]{2,1,0:T(8,128)(2,1)}, u32[]{:S(2)}, u32[]{:S(2)}) collective-permute-start(bf16[2,128,1024]{2,1,0:T(8,128)(2,1)} %get-tuple-element.56), channel_id=1, source_target_pairs={{0,4},{4,0},{8,12},{12,8},{16,20},{20,16},{24,28},{28,24},{1,5},{5... | collective-permute-start | bytes 1572872 | tf_op jit(solution)/shard_map/ppermute | solution.py:275
  135.2 10.5 %collective-permute-start.3 = (bf16[2,2,128,512]{3,2,1,0:T(8,128)(2,1)}, bf16[2,2,128,512]{3,2,1,0:T(8,128)(2,1)}, u32[]{:S(2)}, u32[]{:S(2)}) collective-permute-start(bf16[2,2,128,512]{3,2,1,0:T(8,128)(2,1)} %pad_maximum_fusion.4.refs_4_), channel_id=1, source_target_pairs={{0,8},{4,12},{8,16},{12,20},{16,24},{20,28},{1,9},{5,13},{9,17},{1... | collective-permute-start | bytes 1572872 | tf_op jit(solution)/shard_map/ppermute | solution.py:275
  139.4 11.7 %collective-permute-start.4 = (bf16[2,2,128,512]{3,2,1,0:T(8,128)(2,1)}, bf16[2,2,128,512]{3,2,1,0:T(8,128)(2,1)}, u32[]{:S(2)}, u32[]{:S(2)}) collective-permute-start(bf16[2,2,128,512]{3,2,1,0:T(8,128)(2,1)} %pad_maximum_fusion.4.refs_4_), channel_id=1, source_target_pairs={{8,0},{12,4},{16,8},{20,12},{24,16},{28,20},{9,1},{13,5},{17,9},{2... | collective-permute-start | bytes 1572872 | tf_op jit(solution)/shard_map/ppermute | solution.py:275
  157.2 2.5 %collective-permute-start.25 = (f32[128]{0:T(128)S(1)}, f32[128]{0:T(128)S(1)}, u32[]{:S(2)}, u32[]{:S(2)}) collective-permute-start(f32[128]{0:T(128)S(1)} %multiply_subtract_fusion), channel_id=1, source_target_pairs={{0,1},{1,0},{2,3},{3,2},{4,5},{5,4},{6,7},{7,6},{8,9},{9,8},{10,11... | collective-permute-start | bytes 1544 | tf_op jit(solution)/shard_map/ppermute | solution.py:225
  157.5 32.7 %collective-permute-start.24 = (f32[2,128,640]{2,1,0:T(8,128)S(1)}, f32[2,128,640]{2,1,0:T(8,128)S(1)}, u32[]{:S(2)}, u32[]{:S(2)}) collective-permute-start(f32[2,128,640]{2,1,0:T(8,128)S(1)} %constant_dynamic-update-slice_fusion.53), channel_id=1, source_target_pairs={{0,4},{4,0},{8,12},{12,8},{16,20},{20,16},{24,28},{28,24},{1,5},{5... | collective-permute-start | bytes 1966088 | tf_op jit(solution)/shard_map/ppermute | solution.py:275
  158.8 30.0 %collective-permute-start.23 = (bf16[2,128,512]{2,1,0:T(8,128)(2,1)S(1)}, bf16[2,128,512]{2,1,0:T(8,128)(2,1)S(1)}, u32[]{:S(2)}, u32[]{:S(2)}) collective-permute-start(bf16[2,128,512]{2,1,0:T(8,128)(2,1)S(1)} %get-tuple-element.60), channel_id=1, source_target_pairs={{0,4},{4,0},{8,12},{12,8},{16,20},{20,16},{24,28},{28,24},{1,5},{5... | collective-permute-start | bytes 786440 | tf_op jit(solution)/shard_map/ppermute | solution.py:275
  161.0 3.6 %collective-permute-start.26 = (f32[128]{0:T(128)S(1)}, f32[128]{0:T(128)S(1)}, u32[]{:S(2)}, u32[]{:S(2)}) collective-permute-start(f32[128]{0:T(128)S(1)} %fusion.1), channel_id=1, source_target_pairs={{0,2},{1,3},{2,0},{3,1},{4,6},{5,7},{6,4},{7,5},{8,10},{9,11},{10,... | collective-permute-start | bytes 1544 | tf_op jit(solution)/shard_map/ppermute | solution.py:225
  165.9 14.4 %collective-permute-start.27 = (f32[128]{0:T(128)S(1)}, f32[128]{0:T(128)S(1)}, u32[]{:S(2)}, u32[]{:S(2)}) collective-permute-start(f32[128]{0:T(128)S(1)} %fusion.2), channel_id=1, source_target_pairs={{0,4},{4,0},{8,12},{12,8},{16,20},{20,16},{24,28},{28,24},{1,5},{5... | collective-permute-start | bytes 1544 | tf_op jit(solution)/shard_map/ppermute | solution.py:225
  180.3 3.6 %collective-permute-start.28 = (f32[128]{0:T(128)S(1)}, f32[128]{0:T(128)S(1)}, u32[]{:S(2)}, u32[]{:S(2)}) collective-permute-start(f32[128]{0:T(128)S(1)} %add.30), channel_id=1, source_target_pairs={{0,8},{4,12},{8,0},{12,4},{16,24},{20,28},{24,16},{28,20},{1,9},{5... | collective-permute-start | bytes 1544 | tf_op jit(solution)/shard_map/ppermute | solution.py:225
  183.9 4.4 %collective-permute-start.29 = (f32[128]{0:T(128)S(1)}, f32[128]{0:T(128)S(1)}, u32[]{:S(2)}, u32[]{:S(2)}) collective-permute-start(f32[128]{0:T(128)S(1)} %add.31), channel_id=1, source_target_pairs={{0,16},{4,20},{8,24},{12,28},{16,0},{20,4},{24,8},{28,12},{1,17},{... | collective-permute-start | bytes 1544 | tf_op jit(solution)/shard_map/ppermute | solution.py:225

commit v3 on v0

v3 whole, which is shorter than its diff:
```python
import functools
import math

import jax
import jax.numpy as jnp
from jax import lax
from jax.experimental import pallas as pl
from jax.experimental.pallas import tpu as pltpu
from jax.sharding import PartitionSpec as P

RB = 512
NT = 128
VMEM = 14 * 1024 * 1024
PARTS = (4, 4, 4, 2, 2)
GROUPS = ((0,), (1,), (2,), (3, 4))
LOW, LOW_X, OWN, MATE, HIGH, HIGH_X = range(6)
IN_SMEM = pl.BlockSpec(memory_space=pltpu.SMEM)
IN_VMEM = pl.BlockSpec(memory_space=pltpu.VMEM)
IN_HBM = pl.BlockSpec(memory_space=pltpu.HBM)
PARAMS = pltpu.CompilerParams(vmem_limit_bytes=VMEM)
LIGHT = pl.CostEstimate(flops=0, bytes_accessed=0, transcendentals=0)


def columns(ref, start, size):
    return ref.at[:, :, pl.ds(pl.multiple_of(start, 128), size)]


def run(copies):
    for copy in copies:
        copy.start()
    for copy in copies:
        copy.wait()


def split_kernel(half, off, size, other, info, whole, out, sem):
    side = 1 - info[0] if other else info[0]
    run([pltpu.make_async_copy(columns(whole, side * half + off, size), out, sem)])


def split(info, whole, half, off, size, other):
    return pl.pallas_call(
        functools.partial(split_kernel, half, off, size, other),
        out_shape=jax.ShapeDtypeStruct((*whole.shape[:2], size), whole.dtype),
        in_specs=[IN_SMEM, IN_HBM],
        out_specs=IN_VMEM,
        scratch_shapes=[pltpu.SemaphoreType.DMA],
        compiler_params=PARAMS,
        cost_estimate=LIGHT,
        name="split_columns",
    )(info, whole)


def join_kernel(half, cuts, info, whole, theirs, *refs):
    outs, sems = refs[:-1], refs[-1]
    base = cuts[0][0]
    copies = []
    for n, (off, size) in enumerate(cuts):
        mine = columns(whole, info[0] * half + off, size)
        copies.append(pltpu.make_async_copy(mine, outs[n].at[0], sems.at[2 * n]))
        got = theirs.at[:, :, pl.ds(off - base, size)]
        copies.append(pltpu.make_async_copy(got, outs[n].at[1], sems.at[2 * n + 1]))
    run(copies)


def join(info, whole, theirs, half, cuts):
    return pl.pallas_call(
        functools.partial(join_kernel, half, cuts),
        out_shape=[
            jax.ShapeDtypeStruct((2, *theirs.shape[:2], size), theirs.dtype) for _, size in cuts
        ],
        in_specs=[IN_SMEM, IN_HBM, IN_VMEM],
        out_specs=[IN_VMEM] * len(cuts),
        scratch_shapes=[pltpu.SemaphoreType.DMA((2 * len(cuts),))],
        compiler_params=PARAMS,
        cost_estimate=LIGHT,
        name="join_blocks",
    )(info, whole, theirs)


def place_kernel(half, off, size, info, here, there, *refs):
    whole, sems = refs[-2:]
    side = info[0]
    run(
        [
            pltpu.make_async_copy(here, columns(whole, side * half + off, size), sems.at[0]),
            pltpu.make_async_copy(there, columns(whole, (1 - side) * half + off, size), sems.at[1]),
        ]
    )


def place(info, here, there, whole, half, off):
    _, rows, size = here.shape
    first = whole is None
    return pl.pallas_call(
        functools.partial(place_kernel, half, off, size),
        out_shape=jax.ShapeDtypeStruct((2, rows, 2 * half), here.dtype),
        in_specs=[IN_SMEM, IN_VMEM, IN_VMEM] + ([] if first else [IN_HBM]),
        out_specs=IN_HBM,
        scratch_shapes=[pltpu.SemaphoreType.DMA((2,))],
        input_output_aliases={} if first else {3: 0},
        compiler_params=PARAMS,
        cost_estimate=LIGHT,
        name="place_columns",
    )(info, here, there, *([] if first else [whole]))


def prepare_kernel(info, own, mate, resp, mask):
    rows = mask.shape[0] // 2
    none = None
    tables = (
        ((0, 1, 2, 3, 4, none), (none, 0, 1, 2, 3, 4)),
        ((0, none, 2, 1, 4, 3), (1, 0, 3, 2, none, 4)),
    )
    for which, params in ((0, own), (1, mate)):
        mask[which * rows : (which + 1) * rows, :] = params[2 * rows :, :rows].astype(jnp.float32).T
        line = slice(2 * which * rows, (2 * which + 1) * rows)
        line_im = slice((2 * which + 1) * rows, (2 * which + 2) * rows)
        for side in range(2):

            @pl.when(info[0] == side)
            def _(params=params, line=line, line_im=line_im, table=tables[side][which]):
                for slot, k in enumerate(table):
                    at = slice(slot * rows, (slot + 1) * rows)
                    at_im = slice((6 + slot) * rows, (7 + slot) * rows)
                    if k is None:
                        re = im = jnp.zeros((rows, rows), resp.dtype)
                    else:
                        re = params[:rows, k * rows : (k + 1) * rows]
                        im = params[rows : 2 * rows, k * rows : (k + 1) * rows]
                    resp[line, at] = re
                    resp[line, at_im] = -im
                    resp[line_im, at] = im
                    resp[line_im, at_im] = re


def prepare(info, own, mate, rows):
    blocks = own.shape[0] - 2 * rows
    return pl.pallas_call(
        prepare_kernel,
        out_shape=[
            jax.ShapeDtypeStruct((4 * rows, 12 * rows), own.dtype),
            jax.ShapeDtypeStruct((2 * rows, blocks), jnp.float32),
        ],
        in_specs=[IN_SMEM, IN_VMEM, IN_VMEM],
        out_specs=[IN_VMEM, IN_VMEM],
        compiler_params=PARAMS,
        cost_estimate=LIGHT,
        name="prepare_response",
    )(info, own, mate)


def chunk_kernel(conf, *refs):
    rows, size, stride, half, off, band, layout, first, last = conf
    refs = list(refs)
    info, wave, waves, resp, mask = (refs.pop(0) for _ in range(5))
    given = [refs.pop(0) for _ in range(max(ref for ref, _ in layout) + 1)]
    if not first:
        grad_in, corr_in = refs.pop(0), refs.pop(0)
    out_own, out_mate = refs.pop(0), refs.pop(0)
    if last:
        grad_own, grad_mate, corr_out = (refs.pop(0) for _ in range(3))
    else:
        grad_out, corr_out = refs.pop(0), refs.pop(0)
    ys, ms, sums, corrs = refs
    side, pos = info[0], info[1]
    mate = pos + 1 - 2 * side
    blocks = (pos - 2, mate - 2, pos, mate, pos + 2, mate + 2)
    col0 = side * half + off
    tile = RB if (off | size) % RB == 0 else RB // 2

    def record(slot, c, cols=slice(None)):
        ref, part = layout[slot]
        return given[ref][c, :, cols] if part is None else given[ref][part, c, :, cols]

    def hits(slot, start):
        shots = blocks[slot] * rows + lax.broadcasted_iota(jnp.int32, (rows, tile), 0)
        cols = start + lax.broadcasted_iota(jnp.int32, (rows, tile), 1)
        return shots * stride == cols

    def meets(slot, start):
        low = blocks[slot] * rows * stride
        return (low < start + tile) & (low + rows * stride > start)

    for slot in range(6):
        at = slice(slot * rows, (slot + 1) * rows)
        for c in range(2):
            ys[at, c * size : (c + 1) * size] = record(slot, c)

    @pl.loop(0, size // tile)
    def _(t):
        for slot in range(6):

            @pl.when(meets(slot, col0 + t * tile))
            def _(slot=slot):
                hit = hits(slot, col0 + t * tile)
                at = slice(slot * rows, (slot + 1) * rows)
                for c in range(2):
                    cols = pl.ds(pl.multiple_of(c * size + t * tile, tile), tile)
                    direct = jnp.where(hit, wave[c], 0.0)
                    ys[at, cols] = (ys[at, cols].astype(jnp.float32) - direct).astype(jnp.bfloat16)

    across = (((1,), (1,)), ((), ()))
    corrs[...] = jnp.zeros_like(corrs) if first else corr_in[...]
    listed = mask[...]
    receiver_block = lax.broadcasted_iota(jnp.int32, listed.shape, 1)
    for t in range(size // tile):
        cols = slice(t * tile, (t + 1) * tile)
        cols_im = slice(size + t * tile, size + (t + 1) * tile)
        y = jnp.concatenate([ys[:, cols], ys[:, cols_im]], axis=0)
        fit = jnp.dot(resp[...], y, preferred_element_type=jnp.float32)
        here = receiver_block == (col0 + t * tile) // RB
        covered = jnp.max(jnp.where(here, listed, 0.0), axis=1, keepdims=True)
        for which, slot, out in ((0, OWN, out_own), (1, MATE, out_mate)):
            weight = covered[which * rows : (which + 1) * rows]
            pair = []
            for c in range(2):
                at = 2 * which + c
                value = record(slot, c, cols).astype(jnp.float32) + fit[at * rows : (at + 1) * rows]
                pair.append((weight * value).astype(jnp.bfloat16))
                out[c, :, cols] = pair[c]
            at = slice(2 * which * rows, (2 * which + 1) * rows)
            ms[at, cols] = pair[0]
            ms[at, cols_im] = pair[1]
            at = slice((2 * which + 1) * rows, (2 * which + 2) * rows)
            ms[at, cols] = pair[1]
            ms[at, cols_im] = -pair[0]

    @pl.loop(0, size // tile)
    def _(t):
        for slot in range(6):

            @pl.when(meets(slot, col0 + t * tile))
            def _(slot=slot):
                one = jnp.where(hits(slot, col0 + t * tile), 1.0, 0.0).astype(jnp.bfloat16)
                cols = pl.ds(pl.multiple_of(t * tile, tile), tile)
                at_shots = lax.dot_general(
                    ms[:, cols], one, across, preferred_element_type=jnp.float32
                )
                for c in range(2):
                    at = c * 6 * rows + slot * rows
                    x = resp[:, at : at + rows].astype(jnp.float32)
                    terms = (x * at_shots).reshape(-1, 8, rows)
                    corrs[c] -= jnp.sum(terms, axis=0)

    total = lax.dot_general(ys[...], ms[...], across, preferred_element_type=jnp.float32)
    if not first:
        total = grad_in[...] + total
    if not last:
        grad_out[...] = total
        corr_out[...] = corrs[...]
        return
    sums[...] = total
    even = side == 0
    orders = (
        (grad_own, (LOW, (LOW_X, MATE), OWN, (MATE, HIGH_X), HIGH)),
        (grad_mate, (LOW_X, (OWN, LOW), MATE, (HIGH, OWN), HIGH_X)),
    )
    for which, (out, order) in enumerate(orders):
        for c in range(2):
            at = slice((2 * which + c) * rows, (2 * which + c + 1) * rows)
            for k, slot in enumerate(order):
                pair = slot if isinstance(slot, tuple) else (slot,)
                value = [sums[s * rows : (s + 1) * rows, at] for s in pair]
                value = value[0] if len(pair) == 1 else jnp.where(even, *value)
                out[c, :, k * rows : (k + 1) * rows] = value.T
    corr = [jnp.sum(jnp.sum(corrs[c], axis=0, keepdims=True), axis=1, keepdims=True) for c in range(2)]
    corr_out[...] = corr[0] * waves[0:1, :] - corr[1] * waves[1:2, :]


def chunk(consts, arrays, layout, carry, off, size, half, stride, rows, band, last):
    info, wave, waves, resp, mask = consts
    first = carry is None
    conf = (rows, size, stride, half, off, band, layout, first, last)
    args = [info, wave, waves, resp, mask, *arrays]
    in_specs = [IN_SMEM, IN_SMEM] + [IN_VMEM] * (len(args) - 2)
    aliases = {}
    if not first:
        if not last:
            aliases = {len(args): 2, len(args) + 1: 3}
        args += list(carry)
        in_specs += [IN_VMEM, IN_VMEM]
    if last:
        sums = [jax.ShapeDtypeStruct((2, rows, band), jnp.float32)] * 2
        sums.append(jax.ShapeDtypeStruct((1, waves.shape[1]), jnp.float32))
    else:
        sums = [jax.ShapeDtypeStruct((6 * rows, 4 * rows), jnp.float32)]
        sums.append(jax.ShapeDtypeStruct((2, 8, rows), jnp.float32))
    out_shape = [jax.ShapeDtypeStruct((2, rows, size), jnp.bfloat16)] * 2 + sums
    return pl.pallas_call(
        functools.partial(chunk_kernel, conf),
        out_shape=out_shape,
        in_specs=in_specs,
        out_specs=[IN_VMEM] * len(out_shape),
        scratch_shapes=[
            pltpu.VMEM((6 * rows, 2 * size), jnp.bfloat16),
            pltpu.VMEM((4 * rows, 2 * size), jnp.bfloat16),
            pltpu.VMEM((6 * rows, 4 * rows), jnp.float32),
            pltpu.VMEM((2, 8, rows), jnp.float32),
        ],
        input_output_aliases=aliases,
        compiler_params=PARAMS,
        cost_estimate=LIGHT,
        name="residual_chunk",
    )(*args)


def total_over(value, axis, steps):
    size = lax.axis_size(axis)
    for step in steps:
        value = value + lax.ppermute(value, axis, [(i, i ^ step) for i in range(size)])
    return value


def after(value, *others):
    others = [a for a in others if a is not None]
    return lax.optimization_barrier((value, *others))[0] if others else value


def on_device(data, primaries, wavelet, cover_ids, cover_counts):
    record = data[0]
    _, rows, width = record.shape
    band = primaries.shape[3]
    shots, freqs = lax.axis_size("shot"), lax.axis_size("freq")
    shot_count = shots * rows
    stride = width // shot_count
    half = width // 2
    position = lax.axis_index("shot").astype(jnp.int32)
    freq_index = lax.axis_index("freq").astype(jnp.int32)
    info = jnp.stack([position % 2, position])
    cuts, off = [], 0
    for part in PARTS:
        size = part * (half // sum(PARTS))
        cuts.append((off, size))
        off += size
    steps = len(cuts)

    def swap(a):
        return lax.ppermute(a, "shot", [(s, s ^ 1) for s in range(shots)])

    def neighbours(a):
        return [
            lax.ppermute(a, "shot", [(s, s + d) for s in range(shots) if 0 <= s + d < shots])
            for d in (2, -2)
        ]

    swapped = []
    for n, group in enumerate(GROUPS):
        off, size = cuts[group[0]][0], sum(cuts[m][1] for m in group)
        piece = split(info, record, half, off, size, True)
        swapped.append(swap(after(piece, *swapped[n - 2 : n - 1]) if n >= 2 else piece))
    mine = split(info, record, half, *cuts[0], False)
    near = neighbours(mine)

    listed = jnp.arange(cover_ids.shape[1], dtype=jnp.int32)[None, :] < cover_counts[:, None]
    ids = jnp.arange(width // RB, dtype=jnp.int32)
    covered = jnp.any((cover_ids[:, :, None] == ids) & listed[:, :, None], axis=1)
    covered = jnp.pad(covered.T.astype(jnp.bfloat16), ((0, 0), (0, band - rows)))
    params = jnp.concatenate([primaries[0].reshape(2 * rows, band), covered], axis=0)
    params_there = swap(after(params, swapped[0]))
    resp, mask = prepare(info, params, params_there, rows)
    times = jnp.arange(NT, dtype=jnp.int32).astype(jnp.float32)
    phase = 2.0 * math.pi * (freq_index + 1).astype(jnp.float32) * times / NT
    scale = 1.0 / math.sqrt(shot_count * band)
    waves = jnp.stack([jnp.cos(phase), jnp.sin(phase)]) * scale
    consts = (info, wavelet[0], waves, resp, mask)

    far = neighbours(swapped[0])
    arrays = [near[0], far[0], mine, swapped[0], near[1], far[1]]
    layout = tuple((n, None) for n in range(6))
    both = [None]
    carry = whole = None
    sent = []
    for n, (off, size) in enumerate(cuts):
        if n + 1 < steps:
            if n + 1 == len(both):
                group = GROUPS[n + 1]
                both += join(info, record, swapped[n + 1], half, [cuts[m] for m in group])
            ahead = neighbours(both[n + 1])
        gate = list(both[n + 1 : n + 2])
        if n >= 2:
            here, back, at = sent[n - 2]
            whole = place(info, here, back, whole, half, at)
            info_now, whole = lax.optimization_barrier((info, whole, *gate))[:2]
        else:
            info_now = after(info, *gate)
        here, there, *grad, corr = chunk(
            (info_now, *consts[1:]),
            arrays, layout, carry, off, size, half, stride, rows, band, n == steps - 1,
        )
        carry = (grad[0], corr)
        sent.append((here, swap(there), off))
        if n + 1 < steps:
            arrays = [both[n + 1], *ahead]
            layout = ((1, 0), (1, 1), (0, 0), (0, 1), (2, 0), (2, 1))
    for here, back, at in sent[-2:]:
        whole = place(info, here, back, whole, half, at)
    gradient = grad[0] + swap(grad[1])
    if shots & (shots - 1) or freqs & (freqs - 1):
        total = lax.psum(corr, ("shot", "freq"))
    else:
        total = total_over(corr, "shot", [2**i for i in range(1, shots.bit_length() - 1)])
        total = total_over(total, "freq", [2**i for i in range(freqs.bit_length() - 1)])
        total = total_over(total, "shot", [1])
    return (whole[None], gradient[None], total[0])


def solution(mesh):
    in_specs = (
        P("freq", None, "shot", None),
        P("freq", None, "shot", None),
        P("freq", None),
        P("shot", None),
        P("shot"),
    )
    out_specs = (P("freq", None, "shot", None), P("freq", None, "shot", None), P())
    return jax.shard_map(
        on_device, mesh=mesh, in_specs=in_specs, out_specs=out_specs, check_vma=False
    )
```

time: 291 us -> 143 us (0.49)
  waiting for transfers between devices: 158 us -> 36.1 us
  starting transfers between devices: 14.8 us -> 55.4 us
  Pallas kernels: 0 us -> 38.6 us
  local copies, waits for them, and re-layouts: 38.1 us -> 9.49 us
  matrix products: 26.1 us -> 0 us
  blocking collectives: 25.8 us -> 0 us
  other arithmetic: 26.3 us -> 1.66 us
    ppermute x4 -> x28, waiting for transfers between devices: 158 us -> 36.1 us  [the longest x11 21.2 us: swap(): return lax.ppermute(a, 'shot', [(s, s ^ 1) for s in range(shots)])]
    ppermute x4 -> x28, starting transfers between devices: 14.8 us -> 55.4 us  [the longest x12 36.6 us: neighbours(): lax.ppermute(a, 'shot', [(s, s + d) for s in range(shots) if 0 <= s + d <...]
    pallas_call x0 -> x19, Pallas kernels: none -> 38.6 us  [the longest x5 25.6 us: chunk(): pl.pallas_call(functools.partial(chunk_kernel, conf), out_shape=out_shape...]
    dot_general x2 -> x0, matrix products: 26.1 us -> none  [the longest x1 13.6 us: on_device(): jnp.einsum('gcik,ckj->gij', response_pair, operand, preferred_element_typ...]
    psum x2 -> x0, blocking collectives: 25.8 us -> none  [the longest x1 20.1 us: on_device(): total_re, total_im = lax.psum((corr_re, corr_im), 'shot')]
    slice x2 -> x0, local copies, waits for them, and re-layouts: 20.5 us -> none  [the longest x1 19.1 us: on_device(): misfit[:, :, ::stride_cols]]
    another operation x3 -> x1, other arithmetic: 15.8 us -> 0.08 us  [on_device(): info = jnp.stack([position % 2, position])]
    slice x1 -> x0, other arithmetic: 3.82 us -> none  [on_device(): misfit_pair = jnp.stack([misfit, jnp.stack([misfit[1], -misfit[0]])])]
  transfers between devices with their start and end apart: 4 -> 28, of which waited for: 2 -> 12; matrix products, arithmetic and copies ran while one was open for 8% -> 0% of each run, Pallas kernels for 0% -> 24%
where the time goes in v3:
time: 143 us; the launch traced here: 142 us
  starting transfers between devices  55.4 us (39%)
  Pallas kernels  38.6 us (27%)
  waiting for transfers between devices  36.1 us (25%)
  local copies, waits for them, and re-layouts  9.49 us (7%)
  other arithmetic  1.66 us (1%)
    ppermute x12, starting transfers between devices, neighbours(): lax.ppermute(a, 'shot', [(s, s + d) for s in range(shots) if 0 <= s + d <...  36.6 us
    pallas_call x5, Pallas kernels, chunk(): pl.pallas_call(functools.partial(chunk_kernel, conf), out_shape=out_shape...  25.6 us
    ppermute x11, waiting for transfers between devices, swap(): return lax.ppermute(a, 'shot', [(s, s ^ 1) for s in range(shots)])  21.2 us
    ppermute x11, starting transfers between devices, swap(): return lax.ppermute(a, 'shot', [(s, s ^ 1) for s in range(shots)])  11.7 us
    unnamed x30, local copies, waits for them, and re-layouts  9.49 us
    ppermute x5, waiting for transfers between devices, total_over(): lax.ppermute(value, axis, [(i, i ^ step) for i in range(size)])  7.77 us
    pallas_call x5, Pallas kernels, place(): pl.pallas_call(functools.partial(place_kernel, half, off, size), out_shap...  7.29 us
    ppermute x12, waiting for transfers between devices, neighbours(): lax.ppermute(a, 'shot', [(s, s + d) for s in range(shots) if 0 <= s + d <...  7.19 us
  transfers between devices with their start and end apart: 28, of which 12 were waited for; matrix products, arithmetic and copies ran while one was open for 0% of the time, Pallas kernels for 24%

profile of v3, /device:TPU:0, one launch (start us, length us, event | category | flops | bytes accessed | tf_op | source)
XLA Modules:
  0.0 142.4 jit_solution(13498285067322166601)
XLA Ops:
  0.7 2.2 %copy-done = bf16[1,2,128,8192]{3,2,1,0:T(8,128)(2,1)S(1)} copy-done((bf16[1,2,128,8192]{3,2,1,0:T(8,128)(2,1)S(1)}, bf16[1,2,128,8192]{3,2,1,0:T(8,128)(2,1)}, u32[]{:S(2)}) %copy-start) | copy-done | bytes 4194328
  3.5 3.0 %collective-permute-start = (bf16[2,128,1024]{2,1,0:T(8,128)(2,1)S(1)}, bf16[2,128,1024]{2,1,0:T(8,128)(2,1)S(1)}, u32[]{:S(2)}, u32[]{:S(2)}) collective-permute-start(bf16[2,128,1024]{2,1,0:T(8,128)(2,1)S(1)} %split_columns.5), channel_id=1, source_target_pairs={{0,4},{4,0},{8,12},{12,8},{16,20},{20,16},{24,28},{28,24},{1,5},{5... | collective-permute-start | bytes 1572872 | tf_op jit(solution)/shard_map/ppermute | solution.py:338
  7.9 4.2 %collective-permute-start.3 = (bf16[2,128,1024]{2,1,0:T(8,128)(2,1)S(1)}, bf16[2,128,1024]{2,1,0:T(8,128)(2,1)S(1)}, u32[]{:S(2)}, u32[]{:S(2)}) collective-permute-start(bf16[2,128,1024]{2,1,0:T(8,128)(2,1)S(1)} %split_columns.7.refs_7_), channel_id=1, source_target_pairs={{0,8},{4,12},{8,16},{12,20},{16,24},{20,28},{1,9},{5,13},{9,17},{1... | collective-permute-start | bytes 1572872 | tf_op jit(solution)/shard_map/ppermute | solution.py:342
  12.0 1.3 collective-permute-start.5
  14.0 5.3 %collective-permute-done.theirs = bf16[2,128,1024]{2,1,0:T(8,128)(2,1)S(1)} collective-permute-done((bf16[2,128,1024]{2,1,0:T(8,128)(2,1)S(1)}, bf16[2,128,1024]{2,1,0:T(8,128)(2,1)S(1)}, u32[]{:S(2)}, u32[]{:S(2)}) %collective-permute-start) | collective-permute-done | bytes 524320 | tf_op jit(solution)/shard_map/ppermute | solution.py:338
  19.9 5.1 %collective-permute-start.12 = (bf16[2,2,128,1024]{3,2,1,0:T(8,128)(2,1)S(1)}, bf16[2,2,128,1024]{3,2,1,0:T(8,128)(2,1)}, u32[]{:S(2)}, u32[]{:S(2)}) collective-permute-start(bf16[2,2,128,1024]{3,2,1,0:T(8,128)(2,1)S(1)} %join_blocks.3.refs_5_), channel_id=1, source_target_pairs={{0,8},{4,12},{8,16},{12,20},{16,24},{20,28},{1,9},{5,13},{9,17},{1... | collective-permute-start | bytes 3145736 | tf_op jit(solution)/shard_map/ppermute | solution.py:342
  25.0 1.3 collective-permute-start.13
  26.3 3.4 %collective-permute-done.1.refs_8_ = bf16[2,128,1024]{2,1,0:T(8,128)(2,1)S(1)} collective-permute-done((bf16[2,128,1024]{2,1,0:T(8,128)(2,1)S(1)}, bf16[2,128,1024]{2,1,0:T(8,128)(2,1)S(1)}, u32[]{:S(2)}, u32[]{:S(2)}) %collective-permute-start.1) | collective-permute-done | bytes 524320 | tf_op jit(solution)/shard_map/ppermute | solution.py:338
  29.7 1.7 %collective-permute-start.9 = (bf16[2,128,1024]{2,1,0:T(8,128)(2,1)S(1)}, bf16[2,128,1024]{2,1,0:T(8,128)(2,1)S(1)}, u32[]{:S(2)}, u32[]{:S(2)}) collective-permute-start(bf16[2,128,1024]{2,1,0:T(8,128)(2,1)S(1)} %split_columns.9), channel_id=1, source_target_pairs={{0,4},{4,0},{8,12},{12,8},{16,20},{20,16},{24,28},{28,24},{1,5},{5... | collective-permute-start | bytes 1572872 | tf_op jit(solution)/shard_map/ppermute | solution.py:338
  31.4 3.5 %collective-permute-start.4 = (bf16[2,128,1024]{2,1,0:T(8,128)(2,1)S(1)}, bf16[2,128,1024]{2,1,0:T(8,128)(2,1)S(1)}, u32[]{:S(2)}, u32[]{:S(2)}) collective-permute-start(bf16[2,128,1024]{2,1,0:T(8,128)(2,1)S(1)} %collective-permute-done.1.refs_8_), channel_id=1, source_target_pairs={{0,8},{4,12},{8,16},{12,20},{16,24},{20,28},{1,9},{5,13},{9,17},{1... | collective-permute-start | bytes 1572872 | tf_op jit(solution)/shard_map/ppermute | solution.py:342
  36.4 8.2 %collective-permute-done.9.theirs = bf16[2,128,1024]{2,1,0:T(8,128)(2,1)S(1)} collective-permute-done((bf16[2,128,1024]{2,1,0:T(8,128)(2,1)S(1)}, bf16[2,128,1024]{2,1,0:T(8,128)(2,1)S(1)}, u32[]{:S(2)}, u32[]{:S(2)}) %collective-permute-start.9) | collective-permute-done | bytes 524320 | tf_op jit(solution)/shard_map/ppermute | solution.py:338
  44.5 1.3 collective-permute-start.6
  46.5 3.8 %collective-permute-done.2.mate = bf16[272,640]{1,0:T(8,128)(2,1)S(1)} collective-permute-done((bf16[272,640]{1,0:T(8,128)(2,1)S(1)}, bf16[272,640]{1,0:T(8,128)(2,1)S(1)}, u32[]{:S(2)}, u32[]{:S(2)}) %collective-permute-start.2) | collective-permute-done | bytes 348192 | tf_op jit(solution)/shard_map/ppermute | solution.py:338
  51.0 4.5 %collective-permute-start.10 = (bf16[2,2,128,1024]{3,2,1,0:T(8,128)(2,1)S(1)}, bf16[2,2,128,1024]{3,2,1,0:T(8,128)(2,1)}, u32[]{:S(2)}, u32[]{:S(2)}) collective-permute-start(bf16[2,2,128,1024]{3,2,1,0:T(8,128)(2,1)S(1)} %join_blocks.5.refs_5_), channel_id=1, source_target_pairs={{0,8},{4,12},{8,16},{12,20},{16,24},{20,28},{1,9},{5,13},{9,17},{1... | collective-permute-start | bytes 3145736 | tf_op jit(solution)/shard_map/ppermute | solution.py:342
  55.5 3.3 %collective-permute-done.4.refs_6_ = bf16[2,128,1024]{2,1,0:T(8,128)(2,1)S(1)} collective-permute-done((bf16[2,128,1024]{2,1,0:T(8,128)(2,1)S(1)}, bf16[2,128,1024]{2,1,0:T(8,128)(2,1)S(1)}, u32[]{:S(2)}, u32[]{:S(2)}) %collective-permute-start.4) | collective-permute-done | bytes 524320 | tf_op jit(solution)/shard_map/ppermute | solution.py:342
  59.6 1.3 collective-permute-start.11
  62.4 1.0 copy-done.10
  64.2 1.7 %collective-permute-start.8 = (bf16[2,128,1024]{2,1,0:T(8,128)(2,1)}, bf16[2,128,1024]{2,1,0:T(8,128)(2,1)S(1)}, u32[]{:S(2)}, u32[]{:S(2)}) collective-permute-start(bf16[2,128,1024]{2,1,0:T(8,128)(2,1)} %copy-done.8), channel_id=1, source_target_pairs={{0,4},{4,0},{8,12},{12,8},{16,20},{20,16},{24,28},{28,24},{1,5},{5... | collective-permute-start | bytes 1572872 | tf_op jit(solution)/shard_map/ppermute | solution.py:338
  65.9 1.0 copy-done.3
  67.0 1.0 copy-done.5
  68.0 1.0 copy-done.7
  69.0 5.9 %residual_chunk.5 = (bf16[2,128,1024]{2,1,0:T(8,128)(2,1)S(1)}, bf16[2,128,1024]{2,1,0:T(8,128)(2,1)S(1)}, f32[768,512]{1,0:T(8,128)S(1)}, f32[2,8,128]{2,1,0:T(8,128)S(1)}) custom-call(s32[2]{0:T(128)S(1)} %pad_add_fusion.info.refs_0_, f32[2]{0:T(128)S(1)} %bitcast.19, f32[2,128]{1,0:T(2,128)S(1)} %maximum_multiply_fusion.refs_2_, ...), custom_call_target="tpu_custom_call" | custom-call | tf_op jit(solution)/shard_map/residual_chunk/pallas_call | solution.py:289
  75.1 6.6 %residual_chunk.6 = (bf16[2,128,1024]{2,1,0:T(8,128)(2,1)S(1)}, bf16[2,128,1024]{2,1,0:T(8,128)(2,1)S(1)}, f32[768,512]{1,0:T(8,128)S(1)}, f32[2,8,128]{2,1,0:T(8,128)S(1)}) custom-call(s32[2]{0:T(128)S(1)} %pad_add_fusion.info.refs_0_, f32[2]{0:T(128)S(1)} %bitcast.20, ...), custom_call_target="tpu_custom_call", output_to_operand_aliasing={{2}: (8, {}), {3}: (9, {})} | custom-call | tf_op jit(solution)/shard_map/residual_chunk/pallas_call | solution.py:289
  81.7 1.1 collective-permute-start.15
  83.5 5.9 %collective-permute-start.18 = (bf16[2,2,128,512]{3,2,1,0:T(8,128)(2,1)S(1)}, bf16[2,2,128,512]{3,2,1,0:T(8,128)(2,1)S(1)}, u32[]{:S(2)}, u32[]{:S(2)}) collective-permute-start(bf16[2,2,128,512]{3,2,1,0:T(8,128)(2,1)S(1)} %get-tuple-element.46.refs_5_), channel_id=1, source_target_pairs={{0,8},{4,12},{8,16},{12,20},{16,24},{20,28},{1,9},{5,13},{9,17},{1... | collective-permute-start | bytes 1572872 | tf_op jit(solution)/shard_map/ppermute | solution.py:342
  89.9 1.5 %collective-permute-start.19 = (bf16[2,2,128,512]{3,2,1,0:T(8,128)(2,1)S(1)}, bf16[2,2,128,512]{3,2,1,0:T(8,128)(2,1)S(1)}, u32[]{:S(2)}, u32[]{:S(2)}) collective-permute-start(bf16[2,2,128,512]{3,2,1,0:T(8,128)(2,1)S(1)} %get-tuple-element.46.refs_5_), channel_id=1, source_target_pairs={{8,0},{12,4},{16,8},{20,12},{24,16},{28,20},{9,1},{13,5},{17,9},{2... | collective-permute-start | bytes 1572872 | tf_op jit(solution)/shard_map/ppermute | solution.py:342
  91.4 1.5 %place_columns.5.refs_0_ = bf16[2,128,8192]{2,1,0:T(8,128)(2,1)} custom-call(s32[2]{0:T(128)S(1)} %pad_add_fusion.info.refs_0_, bf16[2,128,1024]{2,1,0:T(8,128)(2,1)S(1)} %get-tuple-element.43.here, bf16[2,128,1024]{2,1,0:T(8,128)(2,1)S(1)} %collective-permute-done.7.there), custom_call_target="tpu_custom_call" | custom-call | tf_op jit(solution)/shard_map/place_columns/pallas_call | solution.py:94
  92.9 6.5 %residual_chunk.7 = (bf16[2,128,1024]{2,1,0:T(8,128)(2,1)S(1)}, bf16[2,128,1024]{2,1,0:T(8,128)(2,1)S(1)}, f32[768,512]{1,0:T(8,128)S(1)}, f32[2,8,128]{2,1,0:T(8,128)S(1)}) custom-call(s32[2]{0:T(128)S(1)} %pad_add_fusion.info.refs_0_, f32[2]{0:T(128)S(1)} %bitcast.21, ...), custom_call_target="tpu_custom_call", output_to_operand_aliasing={{2}: (8, {}), {3}: (9, {})} | custom-call | tf_op jit(solution)/shard_map/residual_chunk/pallas_call | solution.py:289
  99.5 5.7 %collective-permute-start.16 = (bf16[2,2,128,512]{3,2,1,0:T(8,128)(2,1)S(1)}, bf16[2,2,128,512]{3,2,1,0:T(8,128)(2,1)S(1)}, u32[]{:S(2)}, u32[]{:S(2)}) collective-permute-start(bf16[2,2,128,512]{3,2,1,0:T(8,128)(2,1)S(1)} %get-tuple-element.59.refs_5_), channel_id=1, source_target_pairs={{0,8},{4,12},{8,16},{12,20},{16,24},{20,28},{1,9},{5,13},{9,17},{1... | collective-permute-start | bytes 1572872 | tf_op jit(solution)/shard_map/ppermute | solution.py:342
  105.2 1.3 collective-permute-start.17
  106.5 1.5 %place_columns.6.refs_0_ = bf16[2,128,8192]{2,1,0:T(8,128)(2,1)} custom-call(s32[2]{0:T(128)S(1)} %pad_add_fusion.info.refs_0_, bf16[2,128,1024]{2,1,0:T(8,128)(2,1)S(1)} %get-tuple-element.56.here, bf16[2,128,1024]{2,1,0:T(8,128)(2,1)S(1)} %collective-permute-done.15.there, bf16[2,128,8192]{2,1,0:T(8,128)(2,1)} %place_columns.5.refs_0_), custom_call_target="tpu_custom_call", output_to_operand_aliasing={{}: (3, {})} | custom-call | tf_op jit(solution)/shard_map/place_columns/pallas_call | solution.py:94
  108.0 3.1 %residual_chunk.8 = (bf16[2,128,512]{2,1,0:T(8,128)(2,1)S(1)}, bf16[2,128,512]{2,1,0:T(8,128)(2,1)S(1)}, f32[768,512]{1,0:T(8,128)S(1)}, f32[2,8,128]{2,1,0:T(8,128)S(1)}) custom-call(s32[2]{0:T(128)S(1)} %pad_add_fusion.info.refs_0_, f32[2]{0:T(128)S(1)} %bitcast.22, ...), custom_call_target="tpu_custom_call", output_to_operand_aliasing={{2}: (8, {}), {3}: (9, {})} | custom-call | tf_op jit(solution)/shard_map/residual_chunk/pallas_call | solution.py:289
  111.2 1.5 %place_columns.7.refs_0_ = bf16[2,128,8192]{2,1,0:T(8,128)(2,1)} custom-call(s32[2]{0:T(128)S(1)} %pad_add_fusion.info.refs_0_, bf16[2,128,1024]{2,1,0:T(8,128)(2,1)S(1)} %get-tuple-element.54.here, bf16[2,128,1024]{2,1,0:T(8,128)(2,1)S(1)} %collective-permute-done.14.there, bf16[2,128,8192]{2,1,0:T(8,128)(2,1)} %place_columns.6.refs_0_), custom_call_target="tpu_custom_call", output_to_operand_aliasing={{}: (3, {})} | custom-call | tf_op jit(solution)/shard_map/place_columns/pallas_call | solution.py:94
  112.8 3.8 %collective-permute-done.17.refs_7_ = bf16[2,2,128,512]{3,2,1,0:T(8,128)(2,1)S(1)} collective-permute-done((bf16[2,2,128,512]{3,2,1,0:T(8,128)(2,1)S(1)}, bf16[2,2,128,512]{3,2,1,0:T(8,128)(2,1)S(1)}, u32[]{:S(2)}, u32[]{:S(2)}) %collective-permute-start.17) | collective-permute-done | bytes 524320 | tf_op jit(solution)/shard_map/ppermute | solution.py:342
  116.6 3.4 %residual_chunk.9 = (bf16[2,128,512]{2,1,0:T(8,128)(2,1)S(1)}, bf16[2,128,512]{2,1,0:T(8,128)(2,1)S(1)}, f32[2,128,640]{2,1,0:T(8,128)S(1)}, f32[2,128,640]{2,1,0:T(8,128)S(1)}, f32[1,128]{1,0:T(1,128)S(1)}) custom-call(s32[2]{0:T(128)S(1)} %pad_add_fusion.info.refs_0_, f32[2]{0:T(128)S(1)} %bitcast.23, f32[2,128]{1,0:T(2,128)S(1)} %maximum_multiply_fusion.refs_2_, ...), custom_call_target="tpu_custom_call" | custom-call | tf_op jit(solution)/shard_map/residual_chunk/pallas_call | solution.py:289
  120.0 1.4 collective-permute-start.22
  122.1 1.3 collective-permute-start.20
  123.4 2.0 %collective-permute-start.23 = (f32[1,128]{1,0:T(1,128)S(1)}, f32[1,128]{1,0:T(1,128)S(1)}, u32[]{:S(2)}, u32[]{:S(2)}) collective-permute-start(f32[1,128]{1,0:T(1,128)S(1)} %get-tuple-element.74), channel_id=1, source_target_pairs={{0,8},{4,12},{8,0},{12,4},{16,24},{20,28},{24,16},{28,20},{1,9},{5... | collective-permute-start | bytes 1544 | tf_op jit(solution)/shard_map/ppermute | solution.py:310
  125.4 1.6 %collective-permute-done.23 = f32[1,128]{1,0:T(1,128)S(1)} collective-permute-done((f32[1,128]{1,0:T(1,128)S(1)}, f32[1,128]{1,0:T(1,128)S(1)}, u32[]{:S(2)}, u32[]{:S(2)}) %collective-permute-start.23) | collective-permute-done | bytes 544 | tf_op jit(solution)/shard_map/ppermute | solution.py:310
  126.9 2.3 %collective-permute-start.24 = (f32[1,128]{1,0:T(1,128)S(1)}, f32[1,128]{1,0:T(1,128)S(1)}, u32[]{:S(2)}, u32[]{:S(2)}) collective-permute-start(f32[1,128]{1,0:T(1,128)S(1)} %add.28), channel_id=1, source_target_pairs={{0,16},{4,20},{8,24},{12,28},{16,0},{20,4},{24,8},{28,12},{1,17},{... | collective-permute-start | bytes 1544 | tf_op jit(solution)/shard_map/ppermute | solution.py:310
  129.2 2.2 %collective-permute-done.24 = f32[1,128]{1,0:T(1,128)S(1)} collective-permute-done((f32[1,128]{1,0:T(1,128)S(1)}, f32[1,128]{1,0:T(1,128)S(1)}, u32[]{:S(2)}, u32[]{:S(2)}) %collective-permute-start.24) | collective-permute-done | bytes 544 | tf_op jit(solution)/shard_map/ppermute | solution.py:310
  131.4 1.1 collective-permute-done.25
  132.5 1.5 %collective-permute-start.26 = (f32[1,128]{1,0:T(1,128)S(1)}, f32[1,128]{1,0:T(1,128)S(1)}, u32[]{:S(2)}, u32[]{:S(2)}) collective-permute-start(f32[1,128]{1,0:T(1,128)S(1)} %add.30), channel_id=1, source_target_pairs={{0,2},{1,3},{2,0},{3,1},{4,6},{5,7},{6,4},{7,5},{8,10},{9,11},{10,... | collective-permute-start | bytes 1544 | tf_op jit(solution)/shard_map/ppermute | solution.py:310
  134.0 2.0 %collective-permute-done.26 = f32[1,128]{1,0:T(1,128)S(1)} collective-permute-done((f32[1,128]{1,0:T(1,128)S(1)}, f32[1,128]{1,0:T(1,128)S(1)}, u32[]{:S(2)}, u32[]{:S(2)}) %collective-permute-start.26) | collective-permute-done | bytes 544 | tf_op jit(solution)/shard_map/ppermute | solution.py:310
  136.1 1.3 collective-permute-start.27
  137.3 1.4 place_columns.8.refs_0_
  140.1 1.4 place_columns.9
  141.5 0.9 add_bitcast_fusion
  (70 shorter events, 12.7 us)
Async XLA Ops:
  0.7 2.2 %copy-start = (bf16[1,2,128,8192]{3,2,1,0:T(8,128)(2,1)S(1)}, bf16[1,2,128,8192]{3,2,1,0:T(8,128)(2,1)}, u32[]{:S(2)}) copy-start(bf16[1,2,128,8192]{3,2,1,0:T(8,128)(2,1)} %param.5) | copy-start | bytes 12582916
  3.5 15.8 %collective-permute-start = (bf16[2,128,1024]{2,1,0:T(8,128)(2,1)S(1)}, bf16[2,128,1024]{2,1,0:T(8,128)(2,1)S(1)}, u32[]{:S(2)}, u32[]{:S(2)}) collective-permute-start(bf16[2,128,1024]{2,1,0:T(8,128)(2,1)S(1)} %split_columns.5), channel_id=1, source_target_pairs={{0,4},{4,0},{8,12},{12,8},{16,20},{20,16},{24,28},{28,24},{1,5},{5... | collective-permute-start | bytes 1572872 | tf_op jit(solution)/shard_map/ppermute | solution.py:338
  7.1 6.8 %copy-start.14 = (s32[128]{0:T(128)S(1)}, s32[128]{0:T(128)}, u32[]{:S(2)}) copy-start(s32[128]{0:T(128)} %param.9) | copy-start | bytes 1540
  7.1 6.8 %copy-start.13 = (s32[128,8]{0,1:T(8,128)S(1)}, s32[128,8]{0,1:T(8,128)}, u32[]{:S(2)}) copy-start(s32[128,8]{0,1:T(8,128)} %param.8) | copy-start | bytes 12292
  7.2 22.5 %collective-permute-start.1 = (bf16[2,128,1024]{2,1,0:T(8,128)(2,1)S(1)}, bf16[2,128,1024]{2,1,0:T(8,128)(2,1)S(1)}, u32[]{:S(2)}, u32[]{:S(2)}) collective-permute-start(bf16[2,128,1024]{2,1,0:T(8,128)(2,1)S(1)} %split_columns.6), channel_id=1, source_target_pairs={{0,4},{4,0},{8,12},{12,8},{16,20},{20,16},{24,28},{28,24},{1,5},{5... | collective-permute-start | bytes 1572872 | tf_op jit(solution)/shard_map/ppermute | solution.py:338
  7.8 27.1 %copy-start.12 = (bf16[1,2,128,640]{3,2,1,0:T(8,128)(2,1)S(1)}, bf16[1,2,128,640]{3,2,1,0:T(8,128)(2,1)}, u32[]{:S(2)}) copy-start(bf16[1,2,128,640]{3,2,1,0:T(8,128)(2,1)} %param.6) | copy-start | bytes 983044
  7.9 23.6 %collective-permute-start.3 = (bf16[2,128,1024]{2,1,0:T(8,128)(2,1)S(1)}, bf16[2,128,1024]{2,1,0:T(8,128)(2,1)S(1)}, u32[]{:S(2)}, u32[]{:S(2)}) collective-permute-start(bf16[2,128,1024]{2,1,0:T(8,128)(2,1)S(1)} %split_columns.7.refs_7_), channel_id=1, source_target_pairs={{0,8},{4,12},{8,16},{12,20},{16,24},{20,28},{1,9},{5,13},{9,17},{1... | collective-permute-start | bytes 1572872 | tf_op jit(solution)/shard_map/ppermute | solution.py:342
  12.0 23.0 %collective-permute-start.5 = (bf16[2,128,1024]{2,1,0:T(8,128)(2,1)S(1)}, bf16[2,128,1024]{2,1,0:T(8,128)(2,1)S(1)}, u32[]{:S(2)}, u32[]{:S(2)}) collective-permute-start(bf16[2,128,1024]{2,1,0:T(8,128)(2,1)S(1)} %split_columns.7.refs_7_), channel_id=1, source_target_pairs={{8,0},{12,4},{16,8},{20,12},{24,16},{28,20},{9,1},{13,5},{17,9},{2... | collective-permute-start | bytes 1572872 | tf_op jit(solution)/shard_map/ppermute | solution.py:342
  19.9 55.1 %collective-permute-start.12 = (bf16[2,2,128,1024]{3,2,1,0:T(8,128)(2,1)S(1)}, bf16[2,2,128,1024]{3,2,1,0:T(8,128)(2,1)}, u32[]{:S(2)}, u32[]{:S(2)}) collective-permute-start(bf16[2,2,128,1024]{3,2,1,0:T(8,128)(2,1)S(1)} %join_blocks.3.refs_5_), channel_id=1, source_target_pairs={{0,8},{4,12},{8,16},{12,20},{16,24},{20,28},{1,9},{5,13},{9,17},{1... | collective-permute-start | bytes 3145736 | tf_op jit(solution)/shard_map/ppermute | solution.py:342
  25.0 50.1 %collective-permute-start.13 = (bf16[2,2,128,1024]{3,2,1,0:T(8,128)(2,1)S(1)}, bf16[2,2,128,1024]{3,2,1,0:T(8,128)(2,1)}, u32[]{:S(2)}, u32[]{:S(2)}) collective-permute-start(bf16[2,2,128,1024]{3,2,1,0:T(8,128)(2,1)S(1)} %join_blocks.3.refs_5_), channel_id=1, source_target_pairs={{8,0},{12,4},{16,8},{20,12},{24,16},{28,20},{9,1},{13,5},{17,9},{2... | collective-permute-start | bytes 3145736 | tf_op jit(solution)/shard_map/ppermute | solution.py:342
  29.7 14.9 %collective-permute-start.9 = (bf16[2,128,1024]{2,1,0:T(8,128)(2,1)S(1)}, bf16[2,128,1024]{2,1,0:T(8,128)(2,1)S(1)}, u32[]{:S(2)}, u32[]{:S(2)}) collective-permute-start(bf16[2,128,1024]{2,1,0:T(8,128)(2,1)S(1)} %split_columns.9), channel_id=1, source_target_pairs={{0,4},{4,0},{8,12},{12,8},{16,20},{20,16},{24,28},{28,24},{1,5},{5... | collective-permute-start | bytes 1572872 | tf_op jit(solution)/shard_map/ppermute | solution.py:338
  31.4 13.1 %copy-start.2 = (bf16[2,128,1024]{2,1,0:T(8,128)(2,1)}, bf16[2,128,1024]{2,1,0:T(8,128)(2,1)S(1)}, u32[]{:S(2)}) copy-start(bf16[2,128,1024]{2,1,0:T(8,128)(2,1)S(1)} %collective-permute-done.3.refs_5_) | copy-start | bytes 1572868
  31.4 27.4 %collective-permute-start.4 = (bf16[2,128,1024]{2,1,0:T(8,128)(2,1)S(1)}, bf16[2,128,1024]{2,1,0:T(8,128)(2,1)S(1)}, u32[]{:S(2)}, u32[]{:S(2)}) collective-permute-start(bf16[2,128,1024]{2,1,0:T(8,128)(2,1)S(1)} %collective-permute-done.1.refs_8_), channel_id=1, source_target_pairs={{0,8},{4,12},{8,16},{12,20},{16,24},{20,28},{1,9},{5,13},{9,17},{1... | collective-permute-start | bytes 1572872 | tf_op jit(solution)/shard_map/ppermute | solution.py:342
  35.0 30.9 %copy-start.11 = (f32[1,2]{1,0:T(1,128)S(1)}, f32[1,2]{1,0:T(1,128)}, u32[]{:S(2)}) copy-start(f32[1,2]{1,0:T(1,128)} %param.7) | copy-start | bytes 28
  35.0 0.8 copy-start.4
  35.9 14.4 %collective-permute-start.2 = (bf16[272,640]{1,0:T(8,128)(2,1)S(1)}, bf16[272,640]{1,0:T(8,128)(2,1)S(1)}, u32[]{:S(2)}, u32[]{:S(2)}) collective-permute-start(bf16[272,640]{1,0:T(8,128)(2,1)S(1)} %pad_maximum_fusion.own), channel_id=1, source_target_pairs={{0,4},{4,0},{8,12},{12,8},{16,20},{20,16},{24,28},{28,24},{1,5},{5... | collective-permute-start | bytes 1044488 | tf_op jit(solution)/shard_map/ppermute | solution.py:338
  44.5 19.6 %collective-permute-start.6 = (bf16[2,128,1024]{2,1,0:T(8,128)(2,1)S(1)}, bf16[2,128,1024]{2,1,0:T(8,128)(2,1)}, u32[]{:S(2)}, u32[]{:S(2)}) collective-permute-start(bf16[2,128,1024]{2,1,0:T(8,128)(2,1)S(1)} %collective-permute-done.1.refs_8_), channel_id=1, source_target_pairs={{8,0},{12,4},{16,8},{20,12},{24,16},{28,20},{9,1},{13,5},{17,9},{2... | collective-permute-start | bytes 1572872 | tf_op jit(solution)/shard_map/ppermute | solution.py:342
  50.3 0.7 copy-start.9
  51.0 41.9 %collective-permute-start.10 = (bf16[2,2,128,1024]{3,2,1,0:T(8,128)(2,1)S(1)}, bf16[2,2,128,1024]{3,2,1,0:T(8,128)(2,1)}, u32[]{:S(2)}, u32[]{:S(2)}) collective-permute-start(bf16[2,2,128,1024]{3,2,1,0:T(8,128)(2,1)S(1)} %join_blocks.5.refs_5_), channel_id=1, source_target_pairs={{0,8},{4,12},{8,16},{12,20},{16,24},{20,28},{1,9},{5,13},{9,17},{1... | collective-permute-start | bytes 3145736 | tf_op jit(solution)/shard_map/ppermute | solution.py:342
  58.8 0.8 copy-start.6
  59.6 33.3 %collective-permute-start.11 = (bf16[2,2,128,1024]{3,2,1,0:T(8,128)(2,1)S(1)}, bf16[2,2,128,1024]{3,2,1,0:T(8,128)(2,1)}, u32[]{:S(2)}, u32[]{:S(2)}) collective-permute-start(bf16[2,2,128,1024]{3,2,1,0:T(8,128)(2,1)S(1)} %join_blocks.5.refs_5_), channel_id=1, source_target_pairs={{8,0},{12,4},{16,8},{20,12},{24,16},{28,20},{9,1},{13,5},{17,9},{2... | collective-permute-start | bytes 3145736 | tf_op jit(solution)/shard_map/ppermute | solution.py:342
  61.5 0.8 copy-start.8
  62.4 1.0 copy-start.10
  64.2 18.6 %collective-permute-start.8 = (bf16[2,128,1024]{2,1,0:T(8,128)(2,1)}, bf16[2,128,1024]{2,1,0:T(8,128)(2,1)S(1)}, u32[]{:S(2)}, u32[]{:S(2)}) collective-permute-start(bf16[2,128,1024]{2,1,0:T(8,128)(2,1)} %copy-done.8), channel_id=1, source_target_pairs={{0,4},{4,0},{8,12},{12,8},{16,20},{20,16},{24,28},{28,24},{1,5},{5... | collective-permute-start | bytes 1572872 | tf_op jit(solution)/shard_map/ppermute | solution.py:338
  65.9 1.0 copy-start.3
  67.0 1.0 copy-start.5
  68.0 1.0 copy-start.7
  75.0 7.8 %copy-start.1 = (bf16[1,2,128,8192]{3,2,1,0:T(8,128)(2,1)S(1)}, bf16[1,2,128,8192]{3,2,1,0:T(8,128)(2,1)}, u32[]{:S(2)}) copy-start(bf16[1,2,128,8192]{3,2,1,0:T(8,128)(2,1)} %param.5) | copy-start | bytes 12582916
  75.0 14.9 %collective-permute-start.7 = (bf16[2,128,1024]{2,1,0:T(8,128)(2,1)S(1)}, bf16[2,128,1024]{2,1,0:T(8,128)(2,1)S(1)}, u32[]{:S(2)}, u32[]{:S(2)}) collective-permute-start(bf16[2,128,1024]{2,1,0:T(8,128)(2,1)S(1)} %get-tuple-element.44), channel_id=1, source_target_pairs={{0,4},{4,0},{8,12},{12,8},{16,20},{20,16},{24,28},{28,24},{1,5},{5... | collective-permute-start | bytes 1572872 | tf_op jit(solution)/shard_map/ppermute | solution.py:338
  81.7 23.5 %collective-permute-start.15 = (bf16[2,128,1024]{2,1,0:T(8,128)(2,1)S(1)}, bf16[2,128,1024]{2,1,0:T(8,128)(2,1)S(1)}, u32[]{:S(2)}, u32[]{:S(2)}) collective-permute-start(bf16[2,128,1024]{2,1,0:T(8,128)(2,1)S(1)} %get-tuple-element.57), channel_id=1, source_target_pairs={{0,4},{4,0},{8,12},{12,8},{16,20},{20,16},{24,28},{28,24},{1,5},{5... | collective-permute-start | bytes 1572872 | tf_op jit(solution)/shard_map/ppermute | solution.py:338
  83.5 24.6 %collective-permute-start.18 = (bf16[2,2,128,512]{3,2,1,0:T(8,128)(2,1)S(1)}, bf16[2,2,128,512]{3,2,1,0:T(8,128)(2,1)S(1)}, u32[]{:S(2)}, u32[]{:S(2)}) collective-permute-start(bf16[2,2,128,512]{3,2,1,0:T(8,128)(2,1)S(1)} %get-tuple-element.46.refs_5_), channel_id=1, source_target_pairs={{0,8},{4,12},{8,16},{12,20},{16,24},{20,28},{1,9},{5,13},{9,17},{1... | collective-permute-start | bytes 1572872 | tf_op jit(solution)/shard_map/ppermute | solution.py:342
  89.9 18.1 %collective-permute-start.19 = (bf16[2,2,128,512]{3,2,1,0:T(8,128)(2,1)S(1)}, bf16[2,2,128,512]{3,2,1,0:T(8,128)(2,1)S(1)}, u32[]{:S(2)}, u32[]{:S(2)}) collective-permute-start(bf16[2,2,128,512]{3,2,1,0:T(8,128)(2,1)S(1)} %get-tuple-element.46.refs_5_), channel_id=1, source_target_pairs={{8,0},{12,4},{16,8},{20,12},{24,16},{28,20},{9,1},{13,5},{17,9},{2... | collective-permute-start | bytes 1572872 | tf_op jit(solution)/shard_map/ppermute | solution.py:342
  99.4 11.8 %collective-permute-start.14 = (bf16[2,128,1024]{2,1,0:T(8,128)(2,1)S(1)}, bf16[2,128,1024]{2,1,0:T(8,128)(2,1)S(1)}, u32[]{:S(2)}, u32[]{:S(2)}) collective-permute-start(bf16[2,128,1024]{2,1,0:T(8,128)(2,1)S(1)} %get-tuple-element.55), channel_id=1, source_target_pairs={{0,4},{4,0},{8,12},{12,8},{16,20},{20,16},{24,28},{28,24},{1,5},{5... | collective-permute-start | bytes 1572872 | tf_op jit(solution)/shard_map/ppermute | solution.py:338
  99.5 13.3 %collective-permute-start.16 = (bf16[2,2,128,512]{3,2,1,0:T(8,128)(2,1)S(1)}, bf16[2,2,128,512]{3,2,1,0:T(8,128)(2,1)S(1)}, u32[]{:S(2)}, u32[]{:S(2)}) collective-permute-start(bf16[2,2,128,512]{3,2,1,0:T(8,128)(2,1)S(1)} %get-tuple-element.59.refs_5_), channel_id=1, source_target_pairs={{0,8},{4,12},{8,16},{12,20},{16,24},{20,28},{1,9},{5,13},{9,17},{1... | collective-permute-start | bytes 1572872 | tf_op jit(solution)/shard_map/ppermute | solution.py:342
  105.2 11.4 %collective-permute-start.17 = (bf16[2,2,128,512]{3,2,1,0:T(8,128)(2,1)S(1)}, bf16[2,2,128,512]{3,2,1,0:T(8,128)(2,1)S(1)}, u32[]{:S(2)}, u32[]{:S(2)}) collective-permute-start(bf16[2,2,128,512]{3,2,1,0:T(8,128)(2,1)S(1)} %get-tuple-element.59.refs_5_), channel_id=1, source_target_pairs={{8,0},{12,4},{16,8},{20,12},{24,16},{28,20},{9,1},{13,5},{17,9},{2... | collective-permute-start | bytes 1572872 | tf_op jit(solution)/shard_map/ppermute | solution.py:342
  120.0 21.5 %collective-permute-start.22 = (f32[2,128,640]{2,1,0:T(8,128)S(1)}, f32[2,128,640]{2,1,0:T(8,128)S(1)}, u32[]{:S(2)}, u32[]{:S(2)}) collective-permute-start(f32[2,128,640]{2,1,0:T(8,128)S(1)} %get-tuple-element.73), channel_id=1, source_target_pairs={{0,4},{4,0},{8,12},{12,8},{16,20},{20,16},{24,28},{28,24},{1,5},{5... | collective-permute-start | bytes 1966088 | tf_op jit(solution)/shard_map/ppermute | solution.py:338
  121.4 16.0 %collective-permute-start.21 = (bf16[2,128,512]{2,1,0:T(8,128)(2,1)S(1)}, bf16[2,128,512]{2,1,0:T(8,128)(2,1)S(1)}, u32[]{:S(2)}, u32[]{:S(2)}) collective-permute-start(bf16[2,128,512]{2,1,0:T(8,128)(2,1)S(1)} %get-tuple-element.70), channel_id=1, source_target_pairs={{0,4},{4,0},{8,12},{12,8},{16,20},{20,16},{24,28},{28,24},{1,5},{5... | collective-permute-start | bytes 786440 | tf_op jit(solution)/shard_map/ppermute | solution.py:338
  122.1 18.0 %collective-permute-start.20 = (bf16[2,128,512]{2,1,0:T(8,128)(2,1)S(1)}, bf16[2,128,512]{2,1,0:T(8,128)(2,1)S(1)}, u32[]{:S(2)}, u32[]{:S(2)}) collective-permute-start(bf16[2,128,512]{2,1,0:T(8,128)(2,1)S(1)} %get-tuple-element.68), channel_id=1, source_target_pairs={{0,4},{4,0},{8,12},{12,8},{16,20},{20,16},{24,28},{28,24},{1,5},{5... | collective-permute-start | bytes 786440 | tf_op jit(solution)/shard_map/ppermute | solution.py:338
  123.4 3.5 %collective-permute-start.23 = (f32[1,128]{1,0:T(1,128)S(1)}, f32[1,128]{1,0:T(1,128)S(1)}, u32[]{:S(2)}, u32[]{:S(2)}) collective-permute-start(f32[1,128]{1,0:T(1,128)S(1)} %get-tuple-element.74), channel_id=1, source_target_pairs={{0,8},{4,12},{8,0},{12,4},{16,24},{20,28},{24,16},{28,20},{1,9},{5... | collective-permute-start | bytes 1544 | tf_op jit(solution)/shard_map/ppermute | solution.py:310
  126.9 4.4 %collective-permute-start.24 = (f32[1,128]{1,0:T(1,128)S(1)}, f32[1,128]{1,0:T(1,128)S(1)}, u32[]{:S(2)}, u32[]{:S(2)}) collective-permute-start(f32[1,128]{1,0:T(1,128)S(1)} %add.28), channel_id=1, source_target_pairs={{0,16},{4,20},{8,24},{12,28},{16,0},{20,4},{24,8},{28,12},{1,17},{... | collective-permute-start | bytes 1544 | tf_op jit(solution)/shard_map/ppermute | solution.py:310
  131.4 1.1 collective-permute-start.25
  132.5 3.5 %collective-permute-start.26 = (f32[1,128]{1,0:T(1,128)S(1)}, f32[1,128]{1,0:T(1,128)S(1)}, u32[]{:S(2)}, u32[]{:S(2)}) collective-permute-start(f32[1,128]{1,0:T(1,128)S(1)} %add.30), channel_id=1, source_target_pairs={{0,2},{1,3},{2,0},{3,1},{4,6},{5,7},{6,4},{7,5},{8,10},{9,11},{10,... | collective-permute-start | bytes 1544 | tf_op jit(solution)/shard_map/ppermute | solution.py:310
  136.1 3.5 %collective-permute-start.27 = (f32[1,128]{1,0:T(1,128)S(1)}, f32[1,128]{1,0:T(1,128)S(1)}, u32[]{:S(2)}, u32[]{:S(2)}) collective-permute-start(f32[1,128]{1,0:T(1,128)S(1)} %add.31), channel_id=1, source_target_pairs={{0,4},{4,0},{8,12},{12,8},{16,20},{20,16},{24,28},{28,24},{1,5},{5... | collective-permute-start | bytes 1544 | tf_op jit(solution)/shard_map/ppermute | solution.py:310

commit v4 on v3

--- a/solution.py
+++ b/solution.py
@@ -150,9 +150,9 @@
 
 
 def chunk_kernel(conf, *refs):
-    rows, size, stride, half, off, band, layout, first, last = conf
+    rows, size, stride, half, off, scale, layout, first, last = conf
     refs = list(refs)
-    info, wave, waves, resp, mask = (refs.pop(0) for _ in range(5))
+    info, wave, resp, mask = (refs.pop(0) for _ in range(4))
     given = [refs.pop(0) for _ in range(max(ref for ref, _ in layout) + 1)]
     if not first:
         grad_in, corr_in = refs.pop(0), refs.pop(0)
@@ -163,8 +163,7 @@
         grad_out, corr_out = refs.pop(0), refs.pop(0)
     ys, ms, sums, corrs = refs
     side, pos = info[0], info[1]
-    mate = pos + 1 - 2 * side
-    blocks = (pos - 2, mate - 2, pos, mate, pos + 2, mate + 2)
+    even = side == 0
     col0 = side * half + off
     tile = RB if (off | size) % RB == 0 else RB // 2
 
@@ -172,32 +171,35 @@
         ref, part = layout[slot]
         return given[ref][c, :, cols] if part is None else given[ref][part, c, :, cols]
 
-    def hits(slot, start):
-        shots = blocks[slot] * rows + lax.broadcasted_iota(jnp.int32, (rows, tile), 0)
-        cols = start + lax.broadcasted_iota(jnp.int32, (rows, tile), 1)
+    piece = min(RB // 2, rows * stride)
+
+    def hit_slot(start):
+        ahead = start // (rows * stride) - (pos - side - 2)
+        inside = (ahead >= 0) & (ahead < 6)
+        return inside, jnp.where(even, ahead, ahead + 1 - 2 * lax.rem(ahead, 2))
+
+    def hits(start):
+        shots = lax.broadcasted_iota(jnp.int32, (rows, piece), 0)
+        cols = lax.rem(start, rows * stride) + lax.broadcasted_iota(jnp.int32, (rows, piece), 1)
         return shots * stride == cols
-
-    def meets(slot, start):
-        low = blocks[slot] * rows * stride
-        return (low < start + tile) & (low + rows * stride > start)
 
     for slot in range(6):
         at = slice(slot * rows, (slot + 1) * rows)
         for c in range(2):
             ys[at, c * size : (c + 1) * size] = record(slot, c)
 
-    @pl.loop(0, size // tile)
+    @pl.loop(0, size // piece)
     def _(t):
-        for slot in range(6):
-
-            @pl.when(meets(slot, col0 + t * tile))
-            def _(slot=slot):
-                hit = hits(slot, col0 + t * tile)
-                at = slice(slot * rows, (slot + 1) * rows)
-                for c in range(2):
-                    cols = pl.ds(pl.multiple_of(c * size + t * tile, tile), tile)
-                    direct = jnp.where(hit, wave[c], 0.0)
-                    ys[at, cols] = (ys[at, cols].astype(jnp.float32) - direct).astype(jnp.bfloat16)
+        inside, slot = hit_slot(col0 + t * piece)
+
+        @pl.when(inside)
+        def _():
+            hit = hits(col0 + t * piece)
+            at = pl.ds(pl.multiple_of(slot * rows, rows), rows)
+            for c in range(2):
+                cols = pl.ds(pl.multiple_of(c * size + t * piece, piece), piece)
+                direct = jnp.where(hit, wave[c], 0.0)
+                ys[at, cols] = (ys[at, cols].astype(jnp.float32) - direct).astype(jnp.bfloat16)
 
     across = (((1,), (1,)), ((), ()))
     corrs[...] = jnp.zeros_like(corrs) if first else corr_in[...]
@@ -225,22 +227,19 @@
             ms[at, cols] = pair[1]
             ms[at, cols_im] = -pair[0]
 
-    @pl.loop(0, size // tile)
+    @pl.loop(0, size // piece)
     def _(t):
-        for slot in range(6):
-
-            @pl.when(meets(slot, col0 + t * tile))
-            def _(slot=slot):
-                one = jnp.where(hits(slot, col0 + t * tile), 1.0, 0.0).astype(jnp.bfloat16)
-                cols = pl.ds(pl.multiple_of(t * tile, tile), tile)
-                at_shots = lax.dot_general(
-                    ms[:, cols], one, across, preferred_element_type=jnp.float32
-                )
-                for c in range(2):
-                    at = c * 6 * rows + slot * rows
-                    x = resp[:, at : at + rows].astype(jnp.float32)
-                    terms = (x * at_shots).reshape(-1, 8, rows)
-                    corrs[c] -= jnp.sum(terms, axis=0)
+        inside, slot = hit_slot(col0 + t * piece)
+
+        @pl.when(inside)
+        def _():
+            one = jnp.where(hits(col0 + t * piece), 1.0, 0.0).astype(jnp.bfloat16)
+            cols = pl.ds(pl.multiple_of(t * piece, piece), piece)
+            at_shots = lax.dot_general(ms[:, cols], one, across, preferred_element_type=jnp.float32)
+            for c in range(2):
+                at = pl.ds(pl.multiple_of((c * 6 + slot) * rows, rows), rows)
+                terms = (resp[:, at].astype(jnp.float32) * at_shots).reshape(-1, 8, rows)
+                corrs[c] -= jnp.sum(terms, axis=0)
 
     total = lax.dot_general(ys[...], ms[...], across, preferred_element_type=jnp.float32)
     if not first:
@@ -250,7 +249,6 @@
         corr_out[...] = corrs[...]
         return
     sums[...] = total
-    even = side == 0
     orders = (
         (grad_own, (LOW, (LOW_X, MATE), OWN, (MATE, HIGH_X), HIGH)),
         (grad_mate, (LOW_X, (OWN, LOW), MATE, (HIGH, OWN), HIGH_X)),
@@ -264,14 +262,17 @@
                 value = value[0] if len(pair) == 1 else jnp.where(even, *value)
                 out[c, :, k * rows : (k + 1) * rows] = value.T
     corr = [jnp.sum(jnp.sum(corrs[c], axis=0, keepdims=True), axis=1, keepdims=True) for c in range(2)]
-    corr_out[...] = corr[0] * waves[0:1, :] - corr[1] * waves[1:2, :]
+    turns = lax.rem((info[2] + 1) * lax.broadcasted_iota(jnp.int32, (1, NT), 1), NT)
+    phase = turns.astype(jnp.float32) * (2.0 * math.pi / NT)
+    corr_out[...] = (corr[0] * jnp.cos(phase) - corr[1] * jnp.sin(phase)) * scale
 
 
 def chunk(consts, arrays, layout, carry, off, size, half, stride, rows, band, last):
-    info, wave, waves, resp, mask = consts
+    info, wave, resp, mask = consts
     first = carry is None
-    conf = (rows, size, stride, half, off, band, layout, first, last)
-    args = [info, wave, waves, resp, mask, *arrays]
+    scale = 1.0 / math.sqrt(2 * half // stride * band)
+    conf = (rows, size, stride, half, off, scale, layout, first, last)
+    args = [info, wave, resp, mask, *arrays]
     in_specs = [IN_SMEM, IN_SMEM] + [IN_VMEM] * (len(args) - 2)
     aliases = {}
     if not first:
@@ -281,7 +282,7 @@
         in_specs += [IN_VMEM, IN_VMEM]
     if last:
         sums = [jax.ShapeDtypeStruct((2, rows, band), jnp.float32)] * 2
-        sums.append(jax.ShapeDtypeStruct((1, waves.shape[1]), jnp.float32))
+        sums.append(jax.ShapeDtypeStruct((1, NT), jnp.float32))
     else:
         sums = [jax.ShapeDtypeStruct((6 * rows, 4 * rows), jnp.float32)]
         sums.append(jax.ShapeDtypeStruct((2, 8, rows), jnp.float32))
@@ -326,7 +327,7 @@
     half = width // 2
     position = lax.axis_index("shot").astype(jnp.int32)
     freq_index = lax.axis_index("freq").astype(jnp.int32)
-    info = jnp.stack([position % 2, position])
+    info = jnp.stack([position % 2, position, freq_index])
     cuts, off = [], 0
     for part in PARTS:
         size = part * (half // sum(PARTS))
@@ -358,11 +359,7 @@
     params = jnp.concatenate([primaries[0].reshape(2 * rows, band), covered], axis=0)
     params_there = swap(after(params, swapped[0]))
     resp, mask = prepare(info, params, params_there, rows)
-    times = jnp.arange(NT, dtype=jnp.int32).astype(jnp.float32)
-    phase = 2.0 * math.pi * (freq_index + 1).astype(jnp.float32) * times / NT
-    scale = 1.0 / math.sqrt(shot_count * band)
-    waves = jnp.stack([jnp.cos(phase), jnp.sin(phase)]) * scale
-    consts = (info, wavelet[0], waves, resp, mask)
+    consts = (info, wavelet[0], resp, mask)
 
     far = neighbours(swapped[0])
     arrays = [near[0], far[0], mine, swapped[0], near[1], far[1]]

time: 143 us -> 141 us (0.986)
  local copies, waits for them, and re-layouts: 9.49 us -> 2.22 us
  waiting for transfers between devices: 36.1 us -> 42.6 us
    unnamed x30 -> x12, local copies, waits for them, and re-layouts: 9.49 us -> 2.22 us
    ppermute x11, waiting for transfers between devices: 21.2 us -> 26.4 us  [swap(): return lax.ppermute(a, 'shot', [(s, s ^ 1) for s in range(shots)])]
    ppermute x12, waiting for transfers between devices: 7.19 us -> 9.78 us  [neighbours(): lax.ppermute(a, 'shot', [(s, s + d) for s in range(shots) if 0 <= s + d <...]
    ppermute x5, starting transfers between devices: 7.05 us -> 8.9 us  [total_over(): lax.ppermute(value, axis, [(i, i ^ step) for i in range(size)])]
    ppermute x12, starting transfers between devices: 36.6 us -> 34.9 us  [neighbours(): lax.ppermute(a, 'shot', [(s, s + d) for s in range(shots) if 0 <= s + d <...]
  transfers between devices with their start and end apart: 28 -> 28, of which waited for: 12 -> 13; matrix products, arithmetic and copies ran while one was open for 0% -> 0% of each run, Pallas kernels for 24% -> 24%
where the time goes in v4:
time: 141 us; the launch traced here: 140 us
  starting transfers between devices  55.2 us (39%)
  waiting for transfers between devices  42.6 us (30%)
  Pallas kernels  37.6 us (27%)
  local copies, waits for them, and re-layouts  2.22 us (2%)
  other arithmetic  1.6 us (1%)
    ppermute x12, starting transfers between devices, neighbours(): lax.ppermute(a, 'shot', [(s, s + d) for s in range(shots) if 0 <= s + d <...  34.9 us
    ppermute x11, waiting for transfers between devices, swap(): return lax.ppermute(a, 'shot', [(s, s ^ 1) for s in range(shots)])  26.4 us
    pallas_call x5, Pallas kernels, chunk(): pl.pallas_call(functools.partial(chunk_kernel, conf), out_shape=out_shape...  24.5 us
    ppermute x11, starting transfers between devices, swap(): return lax.ppermute(a, 'shot', [(s, s ^ 1) for s in range(shots)])  11.4 us
    ppermute x12, waiting for transfers between devices, neighbours(): lax.ppermute(a, 'shot', [(s, s + d) for s in range(shots) if 0 <= s + d <...  9.78 us
    ppermute x5, starting transfers between devices, total_over(): lax.ppermute(value, axis, [(i, i ^ step) for i in range(size)])  8.9 us
    pallas_call x5, Pallas kernels, place(): pl.pallas_call(functools.partial(place_kernel, half, off, size), out_shap...  7.29 us
    ppermute x5, waiting for transfers between devices, total_over(): lax.ppermute(value, axis, [(i, i ^ step) for i in range(size)])  6.4 us
  transfers between devices with their start and end apart: 28, of which 13 were waited for; matrix products, arithmetic and copies ran while one was open for 0% of the time, Pallas kernels for 24%

profile of v4, /device:TPU:0, one launch (start us, length us, event | category | flops | bytes accessed | tf_op | source)
XLA Modules:
  0.0 140.2 jit_solution(3628492193797663788)
XLA Ops:
  0.7 2.2 %copy-done = bf16[1,2,128,8192]{3,2,1,0:T(8,128)(2,1)S(1)} copy-done((bf16[1,2,128,8192]{3,2,1,0:T(8,128)(2,1)S(1)}, bf16[1,2,128,8192]{3,2,1,0:T(8,128)(2,1)}, u32[]{:S(2)}) %copy-start) | copy-done | bytes 4194328
  3.5 3.0 %collective-permute-start = (bf16[2,128,1024]{2,1,0:T(8,128)(2,1)S(1)}, bf16[2,128,1024]{2,1,0:T(8,128)(2,1)S(1)}, u32[]{:S(2)}, u32[]{:S(2)}) collective-permute-start(bf16[2,128,1024]{2,1,0:T(8,128)(2,1)S(1)} %split_columns.5), channel_id=1, source_target_pairs={{0,4},{4,0},{8,12},{12,8},{16,20},{20,16},{24,28},{28,24},{1,5},{5... | collective-permute-start | bytes 1572872 | tf_op jit(solution)/shard_map/ppermute | solution.py:339
  7.9 4.2 %collective-permute-start.3 = (bf16[2,128,1024]{2,1,0:T(8,128)(2,1)S(1)}, bf16[2,128,1024]{2,1,0:T(8,128)(2,1)S(1)}, u32[]{:S(2)}, u32[]{:S(2)}) collective-permute-start(bf16[2,128,1024]{2,1,0:T(8,128)(2,1)S(1)} %split_columns.7.refs_6_), channel_id=1, source_target_pairs={{0,8},{4,12},{8,16},{12,20},{16,24},{20,28},{1,9},{5,13},{9,17},{1... | collective-permute-start | bytes 1572872 | tf_op jit(solution)/shard_map/ppermute | solution.py:343
  12.0 1.3 collective-permute-start.5
  14.0 5.3 %collective-permute-done.theirs = bf16[2,128,1024]{2,1,0:T(8,128)(2,1)S(1)} collective-permute-done((bf16[2,128,1024]{2,1,0:T(8,128)(2,1)S(1)}, bf16[2,128,1024]{2,1,0:T(8,128)(2,1)S(1)}, u32[]{:S(2)}, u32[]{:S(2)}) %collective-permute-start) | collective-permute-done | bytes 524320 | tf_op jit(solution)/shard_map/ppermute | solution.py:339
  19.9 4.1 %collective-permute-start.12 = (bf16[2,2,128,1024]{3,2,1,0:T(8,128)(2,1)S(1)}, bf16[2,2,128,1024]{3,2,1,0:T(8,128)(2,1)S(1)}, u32[]{:S(2)}, u32[]{:S(2)}) collective-permute-start(bf16[2,2,128,1024]{3,2,1,0:T(8,128)(2,1)S(1)} %join_blocks.3.refs_4_), channel_id=1, source_target_pairs={{0,8},{4,12},{8,16},{12,20},{16,24},{20,28},{1,9},{5,13},{9,17},{1... | collective-permute-start | bytes 3145736 | tf_op jit(solution)/shard_map/ppermute | solution.py:343
  24.1 1.3 collective-permute-start.13
  25.4 4.3 %collective-permute-done.1.refs_7_ = bf16[2,128,1024]{2,1,0:T(8,128)(2,1)S(1)} collective-permute-done((bf16[2,128,1024]{2,1,0:T(8,128)(2,1)S(1)}, bf16[2,128,1024]{2,1,0:T(8,128)(2,1)S(1)}, u32[]{:S(2)}, u32[]{:S(2)}) %collective-permute-start.1) | collective-permute-done | bytes 524320 | tf_op jit(solution)/shard_map/ppermute | solution.py:339
  29.7 1.7 %collective-permute-start.9 = (bf16[2,128,1024]{2,1,0:T(8,128)(2,1)S(1)}, bf16[2,128,1024]{2,1,0:T(8,128)(2,1)S(1)}, u32[]{:S(2)}, u32[]{:S(2)}) collective-permute-start(bf16[2,128,1024]{2,1,0:T(8,128)(2,1)S(1)} %split_columns.9), channel_id=1, source_target_pairs={{0,4},{4,0},{8,12},{12,8},{16,20},{20,16},{24,28},{28,24},{1,5},{5... | collective-permute-start | bytes 1572872 | tf_op jit(solution)/shard_map/ppermute | solution.py:339
  31.4 3.5 %collective-permute-start.4 = (bf16[2,128,1024]{2,1,0:T(8,128)(2,1)S(1)}, bf16[2,128,1024]{2,1,0:T(8,128)(2,1)S(1)}, u32[]{:S(2)}, u32[]{:S(2)}) collective-permute-start(bf16[2,128,1024]{2,1,0:T(8,128)(2,1)S(1)} %collective-permute-done.1.refs_7_), channel_id=1, source_target_pairs={{0,8},{4,12},{8,16},{12,20},{16,24},{20,28},{1,9},{5,13},{9,17},{1... | collective-permute-start | bytes 1572872 | tf_op jit(solution)/shard_map/ppermute | solution.py:343
  35.6 8.9 %collective-permute-done.9.theirs = bf16[2,128,1024]{2,1,0:T(8,128)(2,1)S(1)} collective-permute-done((bf16[2,128,1024]{2,1,0:T(8,128)(2,1)S(1)}, bf16[2,128,1024]{2,1,0:T(8,128)(2,1)S(1)}, u32[]{:S(2)}, u32[]{:S(2)}) %collective-permute-start.9) | collective-permute-done | bytes 524320 | tf_op jit(solution)/shard_map/ppermute | solution.py:339
  44.5 1.3 collective-permute-start.6
  45.8 0.7 join_blocks.5.refs_4_
  46.5 3.8 %collective-permute-done.2.mate = bf16[272,640]{1,0:T(8,128)(2,1)S(1)} collective-permute-done((bf16[272,640]{1,0:T(8,128)(2,1)S(1)}, bf16[272,640]{1,0:T(8,128)(2,1)S(1)}, u32[]{:S(2)}, u32[]{:S(2)}) %collective-permute-start.2) | collective-permute-done | bytes 348192 | tf_op jit(solution)/shard_map/ppermute | solution.py:339
  50.3 3.5 %collective-permute-start.10 = (bf16[2,2,128,1024]{3,2,1,0:T(8,128)(2,1)S(1)}, bf16[2,2,128,1024]{3,2,1,0:T(8,128)(2,1)S(1)}, u32[]{:S(2)}, u32[]{:S(2)}) collective-permute-start(bf16[2,2,128,1024]{3,2,1,0:T(8,128)(2,1)S(1)} %join_blocks.5.refs_4_), channel_id=1, source_target_pairs={{0,8},{4,12},{8,16},{12,20},{16,24},{20,28},{1,9},{5,13},{9,17},{1... | collective-permute-start | bytes 3145736 | tf_op jit(solution)/shard_map/ppermute | solution.py:343
  53.7 5.1 %collective-permute-done.4.refs_5_ = bf16[2,128,1024]{2,1,0:T(8,128)(2,1)S(1)} collective-permute-done((bf16[2,128,1024]{2,1,0:T(8,128)(2,1)S(1)}, bf16[2,128,1024]{2,1,0:T(8,128)(2,1)S(1)}, u32[]{:S(2)}, u32[]{:S(2)}) %collective-permute-start.4) | collective-permute-done | bytes 524320 | tf_op jit(solution)/shard_map/ppermute | solution.py:343
  58.8 1.3 collective-permute-start.11
  60.7 0.8 prepare_response.1
  61.7 1.5 %collective-permute-start.8 = (bf16[2,128,1024]{2,1,0:T(8,128)(2,1)S(1)}, bf16[2,128,1024]{2,1,0:T(8,128)(2,1)S(1)}, u32[]{:S(2)}, u32[]{:S(2)}) collective-permute-start(bf16[2,128,1024]{2,1,0:T(8,128)(2,1)S(1)} %split_columns.8), channel_id=1, source_target_pairs={{0,4},{4,0},{8,12},{12,8},{16,20},{20,16},{24,28},{28,24},{1,5},{5... | collective-permute-start | bytes 1572872 | tf_op jit(solution)/shard_map/ppermute | solution.py:339
  63.3 5.8 %residual_chunk.5 = (bf16[2,128,1024]{2,1,0:T(8,128)(2,1)S(1)}, bf16[2,128,1024]{2,1,0:T(8,128)(2,1)S(1)}, f32[768,512]{1,0:T(8,128)S(1)}, f32[2,8,128]{2,1,0:T(8,128)S(1)}) custom-call(s32[3]{0:T(128)S(1)} %pad_add_fusion.info.refs_0_, f32[2]{0:T(128)S(1)} %bitcast.20, bf16[512,1536]{1,0:T(8,128)(2,1)S(1)} %get-tuple-element.41.refs_2_, ...), custom_call_target="tpu_custom_call" | custom-call | tf_op jit(solution)/shard_map/residual_chunk/pallas_call | solution.py:290
  69.2 5.8 %residual_chunk.6 = (bf16[2,128,1024]{2,1,0:T(8,128)(2,1)S(1)}, bf16[2,128,1024]{2,1,0:T(8,128)(2,1)S(1)}, f32[768,512]{1,0:T(8,128)S(1)}, f32[2,8,128]{2,1,0:T(8,128)S(1)}) custom-call(s32[3]{0:T(128)S(1)} %pad_add_fusion.info.refs_0_, f32[2]{0:T(128)S(1)} %bitcast.21, ...), custom_call_target="tpu_custom_call", output_to_operand_aliasing={{2}: (7, {}), {3}: (8, {})} | custom-call | tf_op jit(solution)/shard_map/residual_chunk/pallas_call | solution.py:290
  75.0 0.8 collective-permute-start.15
  75.9 0.7 join_blocks.4
  76.5 6.3 %collective-permute-start.18 = (bf16[2,2,128,512]{3,2,1,0:T(8,128)(2,1)S(1)}, bf16[2,2,128,512]{3,2,1,0:T(8,128)(2,1)S(1)}, u32[]{:S(2)}, u32[]{:S(2)}) collective-permute-start(bf16[2,2,128,512]{3,2,1,0:T(8,128)(2,1)S(1)} %get-tuple-element.46.refs_4_), channel_id=1, source_target_pairs={{0,8},{4,12},{8,16},{12,20},{16,24},{20,28},{1,9},{5,13},{9,17},{1... | collective-permute-start | bytes 1572872 | tf_op jit(solution)/shard_map/ppermute | solution.py:343
  82.8 4.1 %collective-permute-done.7.there = bf16[2,128,1024]{2,1,0:T(8,128)(2,1)S(1)} collective-permute-done((bf16[2,128,1024]{2,1,0:T(8,128)(2,1)S(1)}, bf16[2,128,1024]{2,1,0:T(8,128)(2,1)S(1)}, u32[]{:S(2)}, u32[]{:S(2)}) %collective-permute-start.7) | collective-permute-done | bytes 524320 | tf_op jit(solution)/shard_map/ppermute | solution.py:339
  86.9 1.5 %collective-permute-start.19 = (bf16[2,2,128,512]{3,2,1,0:T(8,128)(2,1)S(1)}, bf16[2,2,128,512]{3,2,1,0:T(8,128)(2,1)S(1)}, u32[]{:S(2)}, u32[]{:S(2)}) collective-permute-start(bf16[2,2,128,512]{3,2,1,0:T(8,128)(2,1)S(1)} %get-tuple-element.46.refs_4_), channel_id=1, source_target_pairs={{8,0},{12,4},{16,8},{20,12},{24,16},{28,20},{9,1},{13,5},{17,9},{2... | collective-permute-start | bytes 1572872 | tf_op jit(solution)/shard_map/ppermute | solution.py:343
  88.4 1.5 %place_columns.5.refs_0_ = bf16[2,128,8192]{2,1,0:T(8,128)(2,1)} custom-call(s32[3]{0:T(128)S(1)} %pad_add_fusion.info.refs_0_, bf16[2,128,1024]{2,1,0:T(8,128)(2,1)S(1)} %get-tuple-element.43.here, bf16[2,128,1024]{2,1,0:T(8,128)(2,1)S(1)} %collective-permute-done.7.there), custom_call_target="tpu_custom_call" | custom-call | tf_op jit(solution)/shard_map/place_columns/pallas_call | solution.py:94
  89.9 5.8 %residual_chunk.7 = (bf16[2,128,1024]{2,1,0:T(8,128)(2,1)S(1)}, bf16[2,128,1024]{2,1,0:T(8,128)(2,1)S(1)}, f32[768,512]{1,0:T(8,128)S(1)}, f32[2,8,128]{2,1,0:T(8,128)S(1)}) custom-call(s32[3]{0:T(128)S(1)} %pad_add_fusion.info.refs_0_, f32[2]{0:T(128)S(1)} %bitcast.22, ...), custom_call_target="tpu_custom_call", output_to_operand_aliasing={{2}: (7, {}), {3}: (8, {})} | custom-call | tf_op jit(solution)/shard_map/residual_chunk/pallas_call | solution.py:290
  95.7 1.3 collective-permute-start.14
  97.0 5.5 %collective-permute-start.16 = (bf16[2,2,128,512]{3,2,1,0:T(8,128)(2,1)S(1)}, bf16[2,2,128,512]{3,2,1,0:T(8,128)(2,1)S(1)}, u32[]{:S(2)}, u32[]{:S(2)}) collective-permute-start(bf16[2,2,128,512]{3,2,1,0:T(8,128)(2,1)S(1)} %get-tuple-element.59.refs_4_), channel_id=1, source_target_pairs={{0,8},{4,12},{8,16},{12,20},{16,24},{20,28},{1,9},{5,13},{9,17},{1... | collective-permute-start | bytes 1572872 | tf_op jit(solution)/shard_map/ppermute | solution.py:343
  102.6 1.3 collective-permute-start.17
  103.9 1.5 %place_columns.6.refs_0_ = bf16[2,128,8192]{2,1,0:T(8,128)(2,1)} custom-call(s32[3]{0:T(128)S(1)} %pad_add_fusion.info.refs_0_, bf16[2,128,1024]{2,1,0:T(8,128)(2,1)S(1)} %get-tuple-element.56.here, bf16[2,128,1024]{2,1,0:T(8,128)(2,1)S(1)} %collective-permute-done.15.there, bf16[2,128,8192]{2,1,0:T(8,128)(2,1)} %place_columns.5.refs_0_), custom_call_target="tpu_custom_call", output_to_operand_aliasing={{}: (3, {})} | custom-call | tf_op jit(solution)/shard_map/place_columns/pallas_call | solution.py:94
  105.4 3.4 %residual_chunk.8 = (bf16[2,128,512]{2,1,0:T(8,128)(2,1)S(1)}, bf16[2,128,512]{2,1,0:T(8,128)(2,1)S(1)}, f32[768,512]{1,0:T(8,128)S(1)}, f32[2,8,128]{2,1,0:T(8,128)S(1)}) custom-call(s32[3]{0:T(128)S(1)} %pad_add_fusion.info.refs_0_, f32[2]{0:T(128)S(1)} %bitcast.23, ...), custom_call_target="tpu_custom_call", output_to_operand_aliasing={{2}: (7, {}), {3}: (8, {})} | custom-call | tf_op jit(solution)/shard_map/residual_chunk/pallas_call | solution.py:290
  108.8 1.5 %place_columns.7.refs_0_ = bf16[2,128,8192]{2,1,0:T(8,128)(2,1)} custom-call(s32[3]{0:T(128)S(1)} %pad_add_fusion.info.refs_0_, bf16[2,128,1024]{2,1,0:T(8,128)(2,1)S(1)} %get-tuple-element.54.here, bf16[2,128,1024]{2,1,0:T(8,128)(2,1)S(1)} %collective-permute-done.14.there, bf16[2,128,8192]{2,1,0:T(8,128)(2,1)} %place_columns.6.refs_0_), custom_call_target="tpu_custom_call", output_to_operand_aliasing={{}: (3, {})} | custom-call | tf_op jit(solution)/shard_map/place_columns/pallas_call | solution.py:94
  110.4 4.5 %collective-permute-done.17.refs_6_ = bf16[2,2,128,512]{3,2,1,0:T(8,128)(2,1)S(1)} collective-permute-done((bf16[2,2,128,512]{3,2,1,0:T(8,128)(2,1)S(1)}, bf16[2,2,128,512]{3,2,1,0:T(8,128)(2,1)S(1)}, u32[]{:S(2)}, u32[]{:S(2)}) %collective-permute-start.17) | collective-permute-done | bytes 524320 | tf_op jit(solution)/shard_map/ppermute | solution.py:343
  114.8 3.7 %residual_chunk.9 = (bf16[2,128,512]{2,1,0:T(8,128)(2,1)S(1)}, bf16[2,128,512]{2,1,0:T(8,128)(2,1)S(1)}, f32[2,128,640]{2,1,0:T(8,128)S(1)}, f32[2,128,640]{2,1,0:T(8,128)S(1)}, f32[1,128]{1,0:T(1,128)S(1)}) custom-call(s32[3]{0:T(128)S(1)} %pad_add_fusion.info.refs_0_, f32[2]{0:T(128)S(1)} %bitcast.24, bf16[512,1536]{1,0:T(8,128)(2,1)S(1)} %get-tuple-element.41.refs_2_, ...), custom_call_target="tpu_custom_call" | custom-call | tf_op jit(solution)/shard_map/residual_chunk/pallas_call | solution.py:290
  118.6 2.0 %collective-permute-start.21 = (bf16[2,128,512]{2,1,0:T(8,128)(2,1)S(1)}, bf16[2,128,512]{2,1,0:T(8,128)(2,1)S(1)}, u32[]{:S(2)}, u32[]{:S(2)}) collective-permute-start(bf16[2,128,512]{2,1,0:T(8,128)(2,1)S(1)} %get-tuple-element.70), channel_id=1, source_target_pairs={{0,4},{4,0},{8,12},{12,8},{16,20},{20,16},{24,28},{28,24},{1,5},{5... | collective-permute-start | bytes 786440 | tf_op jit(solution)/shard_map/ppermute | solution.py:339
  120.7 2.0 %collective-permute-start.23 = (f32[1,128]{1,0:T(1,128)S(1)}, f32[1,128]{1,0:T(1,128)S(1)}, u32[]{:S(2)}, u32[]{:S(2)}) collective-permute-start(f32[1,128]{1,0:T(1,128)S(1)} %get-tuple-element.74), channel_id=1, source_target_pairs={{0,8},{4,12},{8,0},{12,4},{16,24},{20,28},{24,16},{28,20},{1,9},{5... | collective-permute-start | bytes 1544 | tf_op jit(solution)/shard_map/ppermute | solution.py:311
  122.7 1.5 %collective-permute-done.23 = f32[1,128]{1,0:T(1,128)S(1)} collective-permute-done((f32[1,128]{1,0:T(1,128)S(1)}, f32[1,128]{1,0:T(1,128)S(1)}, u32[]{:S(2)}, u32[]{:S(2)}) %collective-permute-start.23) | collective-permute-done | bytes 544 | tf_op jit(solution)/shard_map/ppermute | solution.py:311
  124.2 3.4 %collective-permute-start.24 = (f32[1,128]{1,0:T(1,128)S(1)}, f32[1,128]{1,0:T(1,128)S(1)}, u32[]{:S(2)}, u32[]{:S(2)}) collective-permute-start(f32[1,128]{1,0:T(1,128)S(1)} %add.24), channel_id=1, source_target_pairs={{0,16},{4,20},{8,24},{12,28},{16,0},{20,4},{24,8},{28,12},{1,17},{... | collective-permute-start | bytes 1544 | tf_op jit(solution)/shard_map/ppermute | solution.py:311
  127.6 1.5 %collective-permute-done.24 = f32[1,128]{1,0:T(1,128)S(1)} collective-permute-done((f32[1,128]{1,0:T(1,128)S(1)}, f32[1,128]{1,0:T(1,128)S(1)}, u32[]{:S(2)}, u32[]{:S(2)}) %collective-permute-start.24) | collective-permute-done | bytes 544 | tf_op jit(solution)/shard_map/ppermute | solution.py:311
  129.2 1.1 collective-permute-done.25
  130.3 1.5 %collective-permute-start.26 = (f32[1,128]{1,0:T(1,128)S(1)}, f32[1,128]{1,0:T(1,128)S(1)}, u32[]{:S(2)}, u32[]{:S(2)}) collective-permute-start(f32[1,128]{1,0:T(1,128)S(1)} %add.26), channel_id=1, source_target_pairs={{0,2},{1,3},{2,0},{3,1},{4,6},{5,7},{6,4},{7,5},{8,10},{9,11},{10,... | collective-permute-start | bytes 1544 | tf_op jit(solution)/shard_map/ppermute | solution.py:311
  131.8 2.0 %collective-permute-done.26 = f32[1,128]{1,0:T(1,128)S(1)} collective-permute-done((f32[1,128]{1,0:T(1,128)S(1)}, f32[1,128]{1,0:T(1,128)S(1)}, u32[]{:S(2)}, u32[]{:S(2)}) %collective-permute-start.26) | collective-permute-done | bytes 544 | tf_op jit(solution)/shard_map/ppermute | solution.py:311
  133.8 1.9 %collective-permute-start.27 = (f32[1,128]{1,0:T(1,128)S(1)}, f32[1,128]{1,0:T(1,128)S(1)}, u32[]{:S(2)}, u32[]{:S(2)}) collective-permute-start(f32[1,128]{1,0:T(1,128)S(1)} %add.27), channel_id=1, source_target_pairs={{0,4},{4,0},{8,12},{12,8},{16,20},{20,16},{24,28},{28,24},{1,5},{5... | collective-permute-start | bytes 1544 | tf_op jit(solution)/shard_map/ppermute | solution.py:311
  135.8 1.4 place_columns.8.refs_0_
  137.9 1.4 place_columns.9
  139.3 0.9 add_bitcast_fusion
  (50 shorter events, 5.7 us)
Async XLA Ops:
  0.7 2.2 %copy-start = (bf16[1,2,128,8192]{3,2,1,0:T(8,128)(2,1)S(1)}, bf16[1,2,128,8192]{3,2,1,0:T(8,128)(2,1)}, u32[]{:S(2)}) copy-start(bf16[1,2,128,8192]{3,2,1,0:T(8,128)(2,1)} %param.5) | copy-start | bytes 12582916
  3.5 15.8 %collective-permute-start = (bf16[2,128,1024]{2,1,0:T(8,128)(2,1)S(1)}, bf16[2,128,1024]{2,1,0:T(8,128)(2,1)S(1)}, u32[]{:S(2)}, u32[]{:S(2)}) collective-permute-start(bf16[2,128,1024]{2,1,0:T(8,128)(2,1)S(1)} %split_columns.5), channel_id=1, source_target_pairs={{0,4},{4,0},{8,12},{12,8},{16,20},{20,16},{24,28},{28,24},{1,5},{5... | collective-permute-start | bytes 1572872 | tf_op jit(solution)/shard_map/ppermute | solution.py:339
  7.1 6.8 %copy-start.5 = (s32[128]{0:T(128)S(1)}, s32[128]{0:T(128)}, u32[]{:S(2)}) copy-start(s32[128]{0:T(128)} %param.9) | copy-start | bytes 1540
  7.1 6.8 %copy-start.4 = (s32[128,8]{0,1:T(8,128)S(1)}, s32[128,8]{0,1:T(8,128)}, u32[]{:S(2)}) copy-start(s32[128,8]{0,1:T(8,128)} %param.8) | copy-start | bytes 12292
  7.2 22.5 %collective-permute-start.1 = (bf16[2,128,1024]{2,1,0:T(8,128)(2,1)S(1)}, bf16[2,128,1024]{2,1,0:T(8,128)(2,1)S(1)}, u32[]{:S(2)}, u32[]{:S(2)}) collective-permute-start(bf16[2,128,1024]{2,1,0:T(8,128)(2,1)S(1)} %split_columns.6), channel_id=1, source_target_pairs={{0,4},{4,0},{8,12},{12,8},{16,20},{20,16},{24,28},{28,24},{1,5},{5... | collective-permute-start | bytes 1572872 | tf_op jit(solution)/shard_map/ppermute | solution.py:339
  7.8 27.1 %copy-start.3 = (bf16[1,2,128,640]{3,2,1,0:T(8,128)(2,1)S(1)}, bf16[1,2,128,640]{3,2,1,0:T(8,128)(2,1)}, u32[]{:S(2)}) copy-start(bf16[1,2,128,640]{3,2,1,0:T(8,128)(2,1)} %param.6) | copy-start | bytes 983044
  7.9 23.6 %collective-permute-start.3 = (bf16[2,128,1024]{2,1,0:T(8,128)(2,1)S(1)}, bf16[2,128,1024]{2,1,0:T(8,128)(2,1)S(1)}, u32[]{:S(2)}, u32[]{:S(2)}) collective-permute-start(bf16[2,128,1024]{2,1,0:T(8,128)(2,1)S(1)} %split_columns.7.refs_6_), channel_id=1, source_target_pairs={{0,8},{4,12},{8,16},{12,20},{16,24},{20,28},{1,9},{5,13},{9,17},{1... | collective-permute-start | bytes 1572872 | tf_op jit(solution)/shard_map/ppermute | solution.py:343
  12.0 23.0 %collective-permute-start.5 = (bf16[2,128,1024]{2,1,0:T(8,128)(2,1)S(1)}, bf16[2,128,1024]{2,1,0:T(8,128)(2,1)S(1)}, u32[]{:S(2)}, u32[]{:S(2)}) collective-permute-start(bf16[2,128,1024]{2,1,0:T(8,128)(2,1)S(1)} %split_columns.7.refs_6_), channel_id=1, source_target_pairs={{8,0},{12,4},{16,8},{20,12},{24,16},{28,20},{9,1},{13,5},{17,9},{2... | collective-permute-start | bytes 1572872 | tf_op jit(solution)/shard_map/ppermute | solution.py:343
  19.9 49.1 %collective-permute-start.12 = (bf16[2,2,128,1024]{3,2,1,0:T(8,128)(2,1)S(1)}, bf16[2,2,128,1024]{3,2,1,0:T(8,128)(2,1)S(1)}, u32[]{:S(2)}, u32[]{:S(2)}) collective-permute-start(bf16[2,2,128,1024]{3,2,1,0:T(8,128)(2,1)S(1)} %join_blocks.3.refs_4_), channel_id=1, source_target_pairs={{0,8},{4,12},{8,16},{12,20},{16,24},{20,28},{1,9},{5,13},{9,17},{1... | collective-permute-start | bytes 3145736 | tf_op jit(solution)/shard_map/ppermute | solution.py:343
  24.1 45.1 %collective-permute-start.13 = (bf16[2,2,128,1024]{3,2,1,0:T(8,128)(2,1)S(1)}, bf16[2,2,128,1024]{3,2,1,0:T(8,128)(2,1)S(1)}, u32[]{:S(2)}, u32[]{:S(2)}) collective-permute-start(bf16[2,2,128,1024]{3,2,1,0:T(8,128)(2,1)S(1)} %join_blocks.3.refs_4_), channel_id=1, source_target_pairs={{8,0},{12,4},{16,8},{20,12},{24,16},{28,20},{9,1},{13,5},{17,9},{2... | collective-permute-start | bytes 3145736 | tf_op jit(solution)/shard_map/ppermute | solution.py:343
  29.7 14.9 %collective-permute-start.9 = (bf16[2,128,1024]{2,1,0:T(8,128)(2,1)S(1)}, bf16[2,128,1024]{2,1,0:T(8,128)(2,1)S(1)}, u32[]{:S(2)}, u32[]{:S(2)}) collective-permute-start(bf16[2,128,1024]{2,1,0:T(8,128)(2,1)S(1)} %split_columns.9), channel_id=1, source_target_pairs={{0,4},{4,0},{8,12},{12,8},{16,20},{20,16},{24,28},{28,24},{1,5},{5... | collective-permute-start | bytes 1572872 | tf_op jit(solution)/shard_map/ppermute | solution.py:339
  31.4 27.4 %collective-permute-start.4 = (bf16[2,128,1024]{2,1,0:T(8,128)(2,1)S(1)}, bf16[2,128,1024]{2,1,0:T(8,128)(2,1)S(1)}, u32[]{:S(2)}, u32[]{:S(2)}) collective-permute-start(bf16[2,128,1024]{2,1,0:T(8,128)(2,1)S(1)} %collective-permute-done.1.refs_7_), channel_id=1, source_target_pairs={{0,8},{4,12},{8,16},{12,20},{16,24},{20,28},{1,9},{5,13},{9,17},{1... | collective-permute-start | bytes 1572872 | tf_op jit(solution)/shard_map/ppermute | solution.py:343
  35.0 28.3 %copy-start.2 = (f32[1,2]{1,0:T(1,128)S(1)}, f32[1,2]{1,0:T(1,128)}, u32[]{:S(2)}) copy-start(f32[1,2]{1,0:T(1,128)} %param.7) | copy-start | bytes 28
  35.0 15.2 %collective-permute-start.2 = (bf16[272,640]{1,0:T(8,128)(2,1)S(1)}, bf16[272,640]{1,0:T(8,128)(2,1)S(1)}, u32[]{:S(2)}, u32[]{:S(2)}) collective-permute-start(bf16[272,640]{1,0:T(8,128)(2,1)S(1)} %pad_maximum_fusion.own), channel_id=1, source_target_pairs={{0,4},{4,0},{8,12},{12,8},{16,20},{20,16},{24,28},{28,24},{1,5},{5... | collective-permute-start | bytes 1044488 | tf_op jit(solution)/shard_map/ppermute | solution.py:339
  44.5 17.2 %collective-permute-start.6 = (bf16[2,128,1024]{2,1,0:T(8,128)(2,1)S(1)}, bf16[2,128,1024]{2,1,0:T(8,128)(2,1)S(1)}, u32[]{:S(2)}, u32[]{:S(2)}) collective-permute-start(bf16[2,128,1024]{2,1,0:T(8,128)(2,1)S(1)} %collective-permute-done.1.refs_7_), channel_id=1, source_target_pairs={{8,0},{12,4},{16,8},{20,12},{24,16},{28,20},{9,1},{13,5},{17,9},{2... | collective-permute-start | bytes 1572872 | tf_op jit(solution)/shard_map/ppermute | solution.py:343
  50.3 39.6 %collective-permute-start.10 = (bf16[2,2,128,1024]{3,2,1,0:T(8,128)(2,1)S(1)}, bf16[2,2,128,1024]{3,2,1,0:T(8,128)(2,1)S(1)}, u32[]{:S(2)}, u32[]{:S(2)}) collective-permute-start(bf16[2,2,128,1024]{3,2,1,0:T(8,128)(2,1)S(1)} %join_blocks.5.refs_4_), channel_id=1, source_target_pairs={{0,8},{4,12},{8,16},{12,20},{16,24},{20,28},{1,9},{5,13},{9,17},{1... | collective-permute-start | bytes 3145736 | tf_op jit(solution)/shard_map/ppermute | solution.py:343
  58.8 31.1 %collective-permute-start.11 = (bf16[2,2,128,1024]{3,2,1,0:T(8,128)(2,1)S(1)}, bf16[2,2,128,1024]{3,2,1,0:T(8,128)(2,1)S(1)}, u32[]{:S(2)}, u32[]{:S(2)}) collective-permute-start(bf16[2,2,128,1024]{3,2,1,0:T(8,128)(2,1)S(1)} %join_blocks.5.refs_4_), channel_id=1, source_target_pairs={{8,0},{12,4},{16,8},{20,12},{24,16},{28,20},{9,1},{13,5},{17,9},{2... | collective-permute-start | bytes 3145736 | tf_op jit(solution)/shard_map/ppermute | solution.py:343
  61.7 14.1 %collective-permute-start.8 = (bf16[2,128,1024]{2,1,0:T(8,128)(2,1)S(1)}, bf16[2,128,1024]{2,1,0:T(8,128)(2,1)S(1)}, u32[]{:S(2)}, u32[]{:S(2)}) collective-permute-start(bf16[2,128,1024]{2,1,0:T(8,128)(2,1)S(1)} %split_columns.8), channel_id=1, source_target_pairs={{0,4},{4,0},{8,12},{12,8},{16,20},{20,16},{24,28},{28,24},{1,5},{5... | collective-permute-start | bytes 1572872 | tf_op jit(solution)/shard_map/ppermute | solution.py:339
  69.1 6.8 %copy-start.1 = (bf16[1,2,128,8192]{3,2,1,0:T(8,128)(2,1)S(1)}, bf16[1,2,128,8192]{3,2,1,0:T(8,128)(2,1)}, u32[]{:S(2)}) copy-start(bf16[1,2,128,8192]{3,2,1,0:T(8,128)(2,1)} %param.5) | copy-start | bytes 12582916
  69.1 17.8 %collective-permute-start.7 = (bf16[2,128,1024]{2,1,0:T(8,128)(2,1)S(1)}, bf16[2,128,1024]{2,1,0:T(8,128)(2,1)S(1)}, u32[]{:S(2)}, u32[]{:S(2)}) collective-permute-start(bf16[2,128,1024]{2,1,0:T(8,128)(2,1)S(1)} %get-tuple-element.44), channel_id=1, source_target_pairs={{0,4},{4,0},{8,12},{12,8},{16,20},{20,16},{24,28},{28,24},{1,5},{5... | collective-permute-start | bytes 1572872 | tf_op jit(solution)/shard_map/ppermute | solution.py:339
  75.0 27.5 %collective-permute-start.15 = (bf16[2,128,1024]{2,1,0:T(8,128)(2,1)S(1)}, bf16[2,128,1024]{2,1,0:T(8,128)(2,1)S(1)}, u32[]{:S(2)}, u32[]{:S(2)}) collective-permute-start(bf16[2,128,1024]{2,1,0:T(8,128)(2,1)S(1)} %get-tuple-element.57), channel_id=1, source_target_pairs={{0,4},{4,0},{8,12},{12,8},{16,20},{20,16},{24,28},{28,24},{1,5},{5... | collective-permute-start | bytes 1572872 | tf_op jit(solution)/shard_map/ppermute | solution.py:339
  76.5 28.9 %collective-permute-start.18 = (bf16[2,2,128,512]{3,2,1,0:T(8,128)(2,1)S(1)}, bf16[2,2,128,512]{3,2,1,0:T(8,128)(2,1)S(1)}, u32[]{:S(2)}, u32[]{:S(2)}) collective-permute-start(bf16[2,2,128,512]{3,2,1,0:T(8,128)(2,1)S(1)} %get-tuple-element.46.refs_4_), channel_id=1, source_target_pairs={{0,8},{4,12},{8,16},{12,20},{16,24},{20,28},{1,9},{5,13},{9,17},{1... | collective-permute-start | bytes 1572872 | tf_op jit(solution)/shard_map/ppermute | solution.py:343
  86.9 18.5 %collective-permute-start.19 = (bf16[2,2,128,512]{3,2,1,0:T(8,128)(2,1)S(1)}, bf16[2,2,128,512]{3,2,1,0:T(8,128)(2,1)S(1)}, u32[]{:S(2)}, u32[]{:S(2)}) collective-permute-start(bf16[2,2,128,512]{3,2,1,0:T(8,128)(2,1)S(1)} %get-tuple-element.46.refs_4_), channel_id=1, source_target_pairs={{8,0},{12,4},{16,8},{20,12},{24,16},{28,20},{9,1},{13,5},{17,9},{2... | collective-permute-start | bytes 1572872 | tf_op jit(solution)/shard_map/ppermute | solution.py:343
  95.7 13.1 %collective-permute-start.14 = (bf16[2,128,1024]{2,1,0:T(8,128)(2,1)S(1)}, bf16[2,128,1024]{2,1,0:T(8,128)(2,1)S(1)}, u32[]{:S(2)}, u32[]{:S(2)}) collective-permute-start(bf16[2,128,1024]{2,1,0:T(8,128)(2,1)S(1)} %get-tuple-element.55), channel_id=1, source_target_pairs={{0,4},{4,0},{8,12},{12,8},{16,20},{20,16},{24,28},{28,24},{1,5},{5... | collective-permute-start | bytes 1572872 | tf_op jit(solution)/shard_map/ppermute | solution.py:339
  97.0 13.3 %collective-permute-start.16 = (bf16[2,2,128,512]{3,2,1,0:T(8,128)(2,1)S(1)}, bf16[2,2,128,512]{3,2,1,0:T(8,128)(2,1)S(1)}, u32[]{:S(2)}, u32[]{:S(2)}) collective-permute-start(bf16[2,2,128,512]{3,2,1,0:T(8,128)(2,1)S(1)} %get-tuple-element.59.refs_4_), channel_id=1, source_target_pairs={{0,8},{4,12},{8,16},{12,20},{16,24},{20,28},{1,9},{5,13},{9,17},{1... | collective-permute-start | bytes 1572872 | tf_op jit(solution)/shard_map/ppermute | solution.py:343
  102.6 12.3 %collective-permute-start.17 = (bf16[2,2,128,512]{3,2,1,0:T(8,128)(2,1)S(1)}, bf16[2,2,128,512]{3,2,1,0:T(8,128)(2,1)S(1)}, u32[]{:S(2)}, u32[]{:S(2)}) collective-permute-start(bf16[2,2,128,512]{3,2,1,0:T(8,128)(2,1)S(1)} %get-tuple-element.59.refs_4_), channel_id=1, source_target_pairs={{8,0},{12,4},{16,8},{20,12},{24,16},{28,20},{9,1},{13,5},{17,9},{2... | collective-permute-start | bytes 1572872 | tf_op jit(solution)/shard_map/ppermute | solution.py:343
  118.5 20.7 %collective-permute-start.22 = (f32[2,128,640]{2,1,0:T(8,128)S(1)}, f32[2,128,640]{2,1,0:T(8,128)S(1)}, u32[]{:S(2)}, u32[]{:S(2)}) collective-permute-start(f32[2,128,640]{2,1,0:T(8,128)S(1)} %get-tuple-element.73), channel_id=1, source_target_pairs={{0,4},{4,0},{8,12},{12,8},{16,20},{20,16},{24,28},{28,24},{1,5},{5... | collective-permute-start | bytes 1966088 | tf_op jit(solution)/shard_map/ppermute | solution.py:339
  118.6 17.2 %collective-permute-start.21 = (bf16[2,128,512]{2,1,0:T(8,128)(2,1)S(1)}, bf16[2,128,512]{2,1,0:T(8,128)(2,1)S(1)}, u32[]{:S(2)}, u32[]{:S(2)}) collective-permute-start(bf16[2,128,512]{2,1,0:T(8,128)(2,1)S(1)} %get-tuple-element.70), channel_id=1, source_target_pairs={{0,4},{4,0},{8,12},{12,8},{16,20},{20,16},{24,28},{28,24},{1,5},{5... | collective-permute-start | bytes 786440 | tf_op jit(solution)/shard_map/ppermute | solution.py:339
  120.6 17.3 %collective-permute-start.20 = (bf16[2,128,512]{2,1,0:T(8,128)(2,1)S(1)}, bf16[2,128,512]{2,1,0:T(8,128)(2,1)S(1)}, u32[]{:S(2)}, u32[]{:S(2)}) collective-permute-start(bf16[2,128,512]{2,1,0:T(8,128)(2,1)S(1)} %get-tuple-element.68), channel_id=1, source_target_pairs={{0,4},{4,0},{8,12},{12,8},{16,20},{20,16},{24,28},{28,24},{1,5},{5... | collective-permute-start | bytes 786440 | tf_op jit(solution)/shard_map/ppermute | solution.py:339
  120.7 3.5 %collective-permute-start.23 = (f32[1,128]{1,0:T(1,128)S(1)}, f32[1,128]{1,0:T(1,128)S(1)}, u32[]{:S(2)}, u32[]{:S(2)}) collective-permute-start(f32[1,128]{1,0:T(1,128)S(1)} %get-tuple-element.74), channel_id=1, source_target_pairs={{0,8},{4,12},{8,0},{12,4},{16,24},{20,28},{24,16},{28,20},{1,9},{5... | collective-permute-start | bytes 1544 | tf_op jit(solution)/shard_map/ppermute | solution.py:311
  124.2 4.9 %collective-permute-start.24 = (f32[1,128]{1,0:T(1,128)S(1)}, f32[1,128]{1,0:T(1,128)S(1)}, u32[]{:S(2)}, u32[]{:S(2)}) collective-permute-start(f32[1,128]{1,0:T(1,128)S(1)} %add.24), channel_id=1, source_target_pairs={{0,16},{4,20},{8,24},{12,28},{16,0},{20,4},{24,8},{28,12},{1,17},{... | collective-permute-start | bytes 1544 | tf_op jit(solution)/shard_map/ppermute | solution.py:311
  129.2 1.1 collective-permute-start.25
  130.3 3.5 %collective-permute-start.26 = (f32[1,128]{1,0:T(1,128)S(1)}, f32[1,128]{1,0:T(1,128)S(1)}, u32[]{:S(2)}, u32[]{:S(2)}) collective-permute-start(f32[1,128]{1,0:T(1,128)S(1)} %add.26), channel_id=1, source_target_pairs={{0,2},{1,3},{2,0},{3,1},{4,6},{5,7},{6,4},{7,5},{8,10},{9,11},{10,... | collective-permute-start | bytes 1544 | tf_op jit(solution)/shard_map/ppermute | solution.py:311
  133.8 3.5 %collective-permute-start.27 = (f32[1,128]{1,0:T(1,128)S(1)}, f32[1,128]{1,0:T(1,128)S(1)}, u32[]{:S(2)}, u32[]{:S(2)}) collective-permute-start(f32[1,128]{1,0:T(1,128)S(1)} %add.27), channel_id=1, source_target_pairs={{0,4},{4,0},{8,12},{12,8},{16,20},{20,16},{24,28},{28,24},{1,5},{5... | collective-permute-start | bytes 1544 | tf_op jit(solution)/shard_map/ppermute | solution.py:311

commit v5 on v4

--- a/solution.py
+++ b/solution.py
@@ -11,8 +11,8 @@
 RB = 512
 NT = 128
 VMEM = 14 * 1024 * 1024
-PARTS = (4, 4, 4, 2, 2)
-GROUPS = ((0,), (1,), (2,), (3, 4))
+PARTS = (7, 4, 4, 1)
+GROUPS = ((0,), (1,), (2, 3))
 LOW, LOW_X, OWN, MATE, HIGH, HIGH_X = range(6)
 IN_SMEM = pl.BlockSpec(memory_space=pltpu.SMEM)
 IN_VMEM = pl.BlockSpec(memory_space=pltpu.VMEM)
@@ -165,7 +165,11 @@
     side, pos = info[0], info[1]
     even = side == 0
     col0 = side * half + off
-    tile = RB if (off | size) % RB == 0 else RB // 2
+    spans, at = [], 0
+    while at < size:
+        wide = RB if (off + at) % RB == 0 and at + RB <= size else RB // 2
+        spans.append((at, at + wide))
+        at += wide
 
     def record(slot, c, cols=slice(None)):
         ref, part = layout[slot]
@@ -205,12 +209,12 @@
     corrs[...] = jnp.zeros_like(corrs) if first else corr_in[...]
     listed = mask[...]
     receiver_block = lax.broadcasted_iota(jnp.int32, listed.shape, 1)
-    for t in range(size // tile):
-        cols = slice(t * tile, (t + 1) * tile)
-        cols_im = slice(size + t * tile, size + (t + 1) * tile)
+    for low, high in spans:
+        cols = slice(low, high)
+        cols_im = slice(size + low, size + high)
         y = jnp.concatenate([ys[:, cols], ys[:, cols_im]], axis=0)
         fit = jnp.dot(resp[...], y, preferred_element_type=jnp.float32)
-        here = receiver_block == (col0 + t * tile) // RB
+        here = receiver_block == (col0 + low) // RB
         covered = jnp.max(jnp.where(here, listed, 0.0), axis=1, keepdims=True)
         for which, slot, out in ((0, OWN, out_own), (1, MATE, out_mate)):
             weight = covered[which * rows : (which + 1) * rows]

time: 141 us -> 138 us (0.979)
  waiting for transfers between devices: 42.6 us -> 55.9 us
  starting transfers between devices: 55.2 us -> 42.8 us
  Pallas kernels: 37.6 us -> 34.2 us
    ppermute x12 -> x10, starting transfers between devices: 34.9 us -> 27 us  [neighbours(): lax.ppermute(a, 'shot', [(s, s + d) for s in range(shots) if 0 <= s + d <...]
    ppermute x12 -> x10, waiting for transfers between devices: 9.78 us -> 17.2 us  [neighbours(): lax.ppermute(a, 'shot', [(s, s + d) for s in range(shots) if 0 <= s + d <...]
    ppermute x5, waiting for transfers between devices: 6.4 us -> 13.8 us  [total_over(): lax.ppermute(value, axis, [(i, i ^ step) for i in range(size)])]
    ppermute x5, starting transfers between devices: 8.9 us -> 6.4 us  [total_over(): lax.ppermute(value, axis, [(i, i ^ step) for i in range(size)])]
    ppermute x11 -> x9, starting transfers between devices: 11.4 us -> 9.41 us  [swap(): return lax.ppermute(a, 'shot', [(s, s ^ 1) for s in range(shots)])]
    ppermute x11 -> x9, waiting for transfers between devices: 26.4 us -> 24.9 us  [swap(): return lax.ppermute(a, 'shot', [(s, s ^ 1) for s in range(shots)])]
    pallas_call x5 -> x4, Pallas kernels: 7.29 us -> 6.11 us  [place(): pl.pallas_call(functools.partial(place_kernel, half, off, size), out_shap...]
    pallas_call x5 -> x4, Pallas kernels: 24.5 us -> 23.5 us  [chunk(): pl.pallas_call(functools.partial(chunk_kernel, conf), out_shape=out_shape...]
  transfers between devices with their start and end apart: 28 -> 24, of which waited for: 13 -> 15; matrix products, arithmetic and copies ran while one was open for 0% -> 0% of each run, Pallas kernels for 24% -> 23%
where the time goes in v5:
time: 138 us
  waiting for transfers between devices  55.9 us (41%)
  starting transfers between devices  42.8 us (31%)
  Pallas kernels  34.2 us (25%)
  local copies, waits for them, and re-layouts  2.22 us (2%)
  other arithmetic  1.57 us (1%)
    ppermute x10, starting transfers between devices, neighbours(): lax.ppermute(a, 'shot', [(s, s + d) for s in range(shots) if 0 <= s + d <...  27 us
    ppermute x9, waiting for transfers between devices, swap(): return lax.ppermute(a, 'shot', [(s, s ^ 1) for s in range(shots)])  24.9 us
    pallas_call x4, Pallas kernels, chunk(): pl.pallas_call(functools.partial(chunk_kernel, conf), out_shape=out_shape...  23.5 us
    ppermute x10, waiting for transfers between devices, neighbours(): lax.ppermute(a, 'shot', [(s, s + d) for s in range(shots) if 0 <= s + d <...  17.2 us
    ppermute x5, waiting for transfers between devices, total_over(): lax.ppermute(value, axis, [(i, i ^ step) for i in range(size)])  13.8 us
    ppermute x9, starting transfers between devices, swap(): return lax.ppermute(a, 'shot', [(s, s ^ 1) for s in range(shots)])  9.41 us
    ppermute x5, starting transfers between devices, total_over(): lax.ppermute(value, axis, [(i, i ^ step) for i in range(size)])  6.4 us
    pallas_call x4, Pallas kernels, place(): pl.pallas_call(functools.partial(place_kernel, half, off, size), out_shap...  6.11 us
  transfers between devices with their start and end apart: 24, of which 15 were waited for; matrix products, arithmetic and copies ran while one was open for 0% of the time, Pallas kernels for 23%

profile of v5, /device:TPU:0, one launch (start us, length us, event | category | flops | bytes accessed | tf_op | source)
XLA Modules:
  0.0 137.7 jit_solution(4536620570923253379)
XLA Ops:
  0.7 2.2 %copy-done = bf16[1,2,128,8192]{3,2,1,0:T(8,128)(2,1)S(1)} copy-done((bf16[1,2,128,8192]{3,2,1,0:T(8,128)(2,1)S(1)}, bf16[1,2,128,8192]{3,2,1,0:T(8,128)(2,1)}, u32[]{:S(2)}) %copy-start) | copy-done | bytes 4194328
  2.9 0.6 split_columns.5
  3.6 3.0 %collective-permute-start = (bf16[2,128,1792]{2,1,0:T(8,128)(2,1)S(1)}, bf16[2,128,1792]{2,1,0:T(8,128)(2,1)S(1)}, u32[]{:S(2)}, u32[]{:S(2)}) collective-permute-start(bf16[2,128,1792]{2,1,0:T(8,128)(2,1)S(1)} %split_columns.5), channel_id=1, source_target_pairs={{0,4},{4,0},{8,12},{12,8},{16,20},{20,16},{24,28},{28,24},{1,5},{5... | collective-permute-start | bytes 2752520 | tf_op jit(solution)/shard_map/ppermute | solution.py:343
  6.6 0.6 split_columns.7.refs_6_
  7.2 3.5 %collective-permute-start.6 = (bf16[2,128,1792]{2,1,0:T(8,128)(2,1)S(1)}, bf16[2,128,1792]{2,1,0:T(8,128)(2,1)S(1)}, u32[]{:S(2)}, u32[]{:S(2)}) collective-permute-start(bf16[2,128,1792]{2,1,0:T(8,128)(2,1)S(1)} %split_columns.7.refs_6_), channel_id=1, source_target_pairs={{0,8},{4,12},{8,16},{12,20},{16,24},{20,28},{1,9},{5,13},{9,17},{1... | collective-permute-start | bytes 2752520 | tf_op jit(solution)/shard_map/ppermute | solution.py:347
  10.8 1.3 collective-permute-start.8
  13.3 14.4 %collective-permute-done.refs_7_ = bf16[2,128,1792]{2,1,0:T(8,128)(2,1)S(1)} collective-permute-done((bf16[2,128,1792]{2,1,0:T(8,128)(2,1)S(1)}, bf16[2,128,1792]{2,1,0:T(8,128)(2,1)S(1)}, u32[]{:S(2)}, u32[]{:S(2)}) %collective-permute-start) | collective-permute-done | bytes 917536 | tf_op jit(solution)/shard_map/ppermute | solution.py:343
  27.8 4.1 %collective-permute-start.7 = (bf16[2,128,1792]{2,1,0:T(8,128)(2,1)S(1)}, bf16[2,128,1792]{2,1,0:T(8,128)(2,1)S(1)}, u32[]{:S(2)}, u32[]{:S(2)}) collective-permute-start(bf16[2,128,1792]{2,1,0:T(8,128)(2,1)S(1)} %collective-permute-done.refs_7_), channel_id=1, source_target_pairs={{0,8},{4,12},{8,16},{12,20},{16,24},{20,28},{1,9},{5,13},{9,17},{1... | collective-permute-start | bytes 2752520 | tf_op jit(solution)/shard_map/ppermute | solution.py:347
  31.9 1.3 collective-permute-start.9
  33.2 4.9 %collective-permute-done.3.theirs = bf16[2,128,1024]{2,1,0:T(8,128)(2,1)S(1)} collective-permute-done((bf16[2,128,1024]{2,1,0:T(8,128)(2,1)S(1)}, bf16[2,128,1024]{2,1,0:T(8,128)(2,1)S(1)}, u32[]{:S(2)}, u32[]{:S(2)}) %collective-permute-start.3) | collective-permute-done | bytes 524320 | tf_op jit(solution)/shard_map/ppermute | solution.py:343
  38.2 1.7 %collective-permute-start.2 = (bf16[272,640]{1,0:T(8,128)(2,1)S(1)}, bf16[272,640]{1,0:T(8,128)(2,1)S(1)}, u32[]{:S(2)}, u32[]{:S(2)}) collective-permute-start(bf16[272,640]{1,0:T(8,128)(2,1)S(1)} %pad_maximum_fusion.own), channel_id=1, source_target_pairs={{0,4},{4,0},{8,12},{12,8},{16,20},{20,16},{24,28},{28,24},{1,5},{5... | collective-permute-start | bytes 1044488 | tf_op jit(solution)/shard_map/ppermute | solution.py:343
  40.9 0.6 join_blocks.3.refs_4_
  41.6 4.1 %collective-permute-start.4 = (bf16[2,2,128,1024]{3,2,1,0:T(8,128)(2,1)S(1)}, bf16[2,2,128,1024]{3,2,1,0:T(8,128)(2,1)S(1)}, u32[]{:S(2)}, u32[]{:S(2)}) collective-permute-start(bf16[2,2,128,1024]{3,2,1,0:T(8,128)(2,1)S(1)} %join_blocks.3.refs_4_), channel_id=1, source_target_pairs={{0,8},{4,12},{8,16},{12,20},{16,24},{20,28},{1,9},{5,13},{9,17},{1... | collective-permute-start | bytes 3145736 | tf_op jit(solution)/shard_map/ppermute | solution.py:347
  45.7 3.6 %collective-permute-done.2.mate = bf16[272,640]{1,0:T(8,128)(2,1)S(1)} collective-permute-done((bf16[272,640]{1,0:T(8,128)(2,1)S(1)}, bf16[272,640]{1,0:T(8,128)(2,1)S(1)}, u32[]{:S(2)}, u32[]{:S(2)}) %collective-permute-start.2) | collective-permute-done | bytes 348192 | tf_op jit(solution)/shard_map/ppermute | solution.py:343
  49.3 1.3 collective-permute-start.5
  50.5 0.8 prepare_response.1
  51.3 1.3 collective-permute-done.7.refs_5_
  52.6 4.5 %collective-permute-done.9.refs_9_ = bf16[2,128,1792]{2,1,0:T(8,128)(2,1)S(1)} collective-permute-done((bf16[2,128,1792]{2,1,0:T(8,128)(2,1)S(1)}, bf16[2,128,1792]{2,1,0:T(8,128)(2,1)S(1)}, u32[]{:S(2)}, u32[]{:S(2)}) %collective-permute-start.9) | collective-permute-done | bytes 917536 | tf_op jit(solution)/shard_map/ppermute | solution.py:347
  57.1 9.4 %residual_chunk.4 = (bf16[2,128,1792]{2,1,0:T(8,128)(2,1)S(1)}, bf16[2,128,1792]{2,1,0:T(8,128)(2,1)S(1)}, f32[768,512]{1,0:T(8,128)S(1)}, f32[2,8,128]{2,1,0:T(8,128)S(1)}) custom-call(s32[3]{0:T(128)S(1)} %pad_add_fusion.info.refs_0_, f32[2]{0:T(128)S(1)} %bitcast.18, bf16[512,1536]{1,0:T(8,128)(2,1)S(1)} %get-tuple-element.36.refs_2_, ...), custom_call_target="tpu_custom_call" | custom-call | tf_op jit(solution)/shard_map/residual_chunk/pallas_call | solution.py:294
  66.6 0.7 join_blocks.2
  67.3 5.0 %collective-permute-start.14 = (bf16[2,2,128,1024]{3,2,1,0:T(8,128)(2,1)S(1)}, bf16[2,2,128,1024]{3,2,1,0:T(8,128)(2,1)S(1)}, u32[]{:S(2)}, u32[]{:S(2)}) collective-permute-start(bf16[2,2,128,1024]{3,2,1,0:T(8,128)(2,1)S(1)} %get-tuple-element.33.refs_4_), channel_id=1, source_target_pairs={{0,8},{4,12},{8,16},{12,20},{16,24},{20,28},{1,9},{5,13},{9,17},{1... | collective-permute-start | bytes 3145736 | tf_op jit(solution)/shard_map/ppermute | solution.py:347
  72.2 1.3 collective-permute-start.15
  73.5 1.5 %collective-permute-done.4.refs_5_ = bf16[2,2,128,1024]{3,2,1,0:T(8,128)(2,1)S(1)} collective-permute-done((bf16[2,2,128,1024]{3,2,1,0:T(8,128)(2,1)S(1)}, bf16[2,2,128,1024]{3,2,1,0:T(8,128)(2,1)S(1)}, u32[]{:S(2)}, u32[]{:S(2)}) %collective-permute-start.4) | collective-permute-done | bytes 1048608 | tf_op jit(solution)/shard_map/ppermute | solution.py:347
  75.1 4.5 %collective-permute-done.5.refs_6_ = bf16[2,2,128,1024]{3,2,1,0:T(8,128)(2,1)S(1)} collective-permute-done((bf16[2,2,128,1024]{3,2,1,0:T(8,128)(2,1)S(1)}, bf16[2,2,128,1024]{3,2,1,0:T(8,128)(2,1)S(1)}, u32[]{:S(2)}, u32[]{:S(2)}) %collective-permute-start.5) | collective-permute-done | bytes 1048608 | tf_op jit(solution)/shard_map/ppermute | solution.py:347
  79.5 5.8 %residual_chunk.5 = (bf16[2,128,1024]{2,1,0:T(8,128)(2,1)S(1)}, bf16[2,128,1024]{2,1,0:T(8,128)(2,1)S(1)}, f32[768,512]{1,0:T(8,128)S(1)}, f32[2,8,128]{2,1,0:T(8,128)S(1)}) custom-call(s32[3]{0:T(128)S(1)} %pad_add_fusion.info.refs_0_, f32[2]{0:T(128)S(1)} %bitcast.19, ...), custom_call_target="tpu_custom_call", output_to_operand_aliasing={{2}: (7, {}), {3}: (8, {})} | custom-call | tf_op jit(solution)/shard_map/residual_chunk/pallas_call | solution.py:294
  85.7 3.7 %collective-permute-start.12 = (bf16[2,2,128,256]{3,2,1,0:T(8,128)(2,1)S(1)}, bf16[2,2,128,256]{3,2,1,0:T(8,128)(2,1)S(1)}, u32[]{:S(2)}, u32[]{:S(2)}) collective-permute-start(bf16[2,2,128,256]{3,2,1,0:T(8,128)(2,1)S(1)} %get-tuple-element.45.refs_4_), channel_id=1, source_target_pairs={{0,8},{4,12},{8,16},{12,20},{16,24},{20,28},{1,9},{5,13},{9,17},{1... | collective-permute-start | bytes 786440 | tf_op jit(solution)/shard_map/ppermute | solution.py:347
  89.4 1.5 %collective-permute-start.13 = (bf16[2,2,128,256]{3,2,1,0:T(8,128)(2,1)S(1)}, bf16[2,2,128,256]{3,2,1,0:T(8,128)(2,1)S(1)}, u32[]{:S(2)}, u32[]{:S(2)}) collective-permute-start(bf16[2,2,128,256]{3,2,1,0:T(8,128)(2,1)S(1)} %get-tuple-element.45.refs_4_), channel_id=1, source_target_pairs={{8,0},{12,4},{16,8},{20,12},{24,16},{28,20},{9,1},{13,5},{17,9},{2... | collective-permute-start | bytes 786440 | tf_op jit(solution)/shard_map/ppermute | solution.py:347
  90.9 1.8 %place_columns.4.refs_0_ = bf16[2,128,8192]{2,1,0:T(8,128)(2,1)} custom-call(s32[3]{0:T(128)S(1)} %pad_add_fusion.info.refs_0_, bf16[2,128,1792]{2,1,0:T(8,128)(2,1)S(1)} %get-tuple-element.43.here, bf16[2,128,1792]{2,1,0:T(8,128)(2,1)S(1)} %collective-permute-done.11.there), custom_call_target="tpu_custom_call" | custom-call | tf_op jit(solution)/shard_map/place_columns/pallas_call | solution.py:94
  92.7 1.9 %collective-permute-done.10.there = bf16[2,128,1024]{2,1,0:T(8,128)(2,1)S(1)} collective-permute-done((bf16[2,128,1024]{2,1,0:T(8,128)(2,1)S(1)}, bf16[2,128,1024]{2,1,0:T(8,128)(2,1)S(1)}, u32[]{:S(2)}, u32[]{:S(2)}) %collective-permute-start.10) | collective-permute-done | bytes 524320 | tf_op jit(solution)/shard_map/ppermute | solution.py:343
  94.6 1.5 %place_columns.5.refs_0_ = bf16[2,128,8192]{2,1,0:T(8,128)(2,1)} custom-call(s32[3]{0:T(128)S(1)} %pad_add_fusion.info.refs_0_, bf16[2,128,1024]{2,1,0:T(8,128)(2,1)S(1)} %get-tuple-element.41.here, bf16[2,128,1024]{2,1,0:T(8,128)(2,1)S(1)} %collective-permute-done.10.there, bf16[2,128,8192]{2,1,0:T(8,128)(2,1)} %place_columns.4.refs_0_), custom_call_target="tpu_custom_call", output_to_operand_aliasing={{}: (3, {})} | custom-call | tf_op jit(solution)/shard_map/place_columns/pallas_call | solution.py:94
  96.1 1.3 collective-permute-done.14.refs_5_
  97.4 4.2 %collective-permute-done.15.refs_6_ = bf16[2,2,128,1024]{3,2,1,0:T(8,128)(2,1)S(1)} collective-permute-done((bf16[2,2,128,1024]{3,2,1,0:T(8,128)(2,1)S(1)}, bf16[2,2,128,1024]{3,2,1,0:T(8,128)(2,1)S(1)}, u32[]{:S(2)}, u32[]{:S(2)}) %collective-permute-start.15) | collective-permute-done | bytes 1048608 | tf_op jit(solution)/shard_map/ppermute | solution.py:347
  101.6 5.8 %residual_chunk.6 = (bf16[2,128,1024]{2,1,0:T(8,128)(2,1)S(1)}, bf16[2,128,1024]{2,1,0:T(8,128)(2,1)S(1)}, f32[768,512]{1,0:T(8,128)S(1)}, f32[2,8,128]{2,1,0:T(8,128)S(1)}) custom-call(s32[3]{0:T(128)S(1)} %pad_add_fusion.info.refs_0_, f32[2]{0:T(128)S(1)} %bitcast.20, ...), custom_call_target="tpu_custom_call", output_to_operand_aliasing={{2}: (7, {}), {3}: (8, {})} | custom-call | tf_op jit(solution)/shard_map/residual_chunk/pallas_call | solution.py:294
  107.5 2.4 %residual_chunk.7 = (bf16[2,128,256]{2,1,0:T(8,128)(2,1)S(1)}, bf16[2,128,256]{2,1,0:T(8,128)(2,1)S(1)}, f32[2,128,640]{2,1,0:T(8,128)S(1)}, f32[2,128,640]{2,1,0:T(8,128)S(1)}, f32[1,128]{1,0:T(1,128)S(1)}) custom-call(s32[3]{0:T(128)S(1)} %pad_add_fusion.info.refs_0_, f32[2]{0:T(128)S(1)} %bitcast.21, bf16[512,1536]{1,0:T(8,128)(2,1)S(1)} %get-tuple-element.36.refs_2_, ...), custom_call_target="tpu_custom_call" | custom-call | tf_op jit(solution)/shard_map/residual_chunk/pallas_call | solution.py:294
  110.0 2.0 %collective-permute-start.17 = (bf16[2,128,1024]{2,1,0:T(8,128)(2,1)S(1)}, bf16[2,128,1024]{2,1,0:T(8,128)(2,1)S(1)}, u32[]{:S(2)}, u32[]{:S(2)}) collective-permute-start(bf16[2,128,1024]{2,1,0:T(8,128)(2,1)S(1)} %get-tuple-element.56), channel_id=1, source_target_pairs={{0,4},{4,0},{8,12},{12,8},{16,20},{20,16},{24,28},{28,24},{1,5},{5... | collective-permute-start | bytes 1572872 | tf_op jit(solution)/shard_map/ppermute | solution.py:343
  112.0 1.5 %collective-permute-start.19 = (f32[1,128]{1,0:T(1,128)S(1)}, f32[1,128]{1,0:T(1,128)S(1)}, u32[]{:S(2)}, u32[]{:S(2)}) collective-permute-start(f32[1,128]{1,0:T(1,128)S(1)} %get-tuple-element.60), channel_id=1, source_target_pairs={{0,8},{4,12},{8,0},{12,4},{16,24},{20,28},{24,16},{28,20},{1,9},{5... | collective-permute-start | bytes 1544 | tf_op jit(solution)/shard_map/ppermute | solution.py:315
  113.5 2.0 %collective-permute-done.19 = f32[1,128]{1,0:T(1,128)S(1)} collective-permute-done((f32[1,128]{1,0:T(1,128)S(1)}, f32[1,128]{1,0:T(1,128)S(1)}, u32[]{:S(2)}, u32[]{:S(2)}) %collective-permute-start.19) | collective-permute-done | bytes 544 | tf_op jit(solution)/shard_map/ppermute | solution.py:315
  115.5 2.5 %collective-permute-start.20 = (f32[1,128]{1,0:T(1,128)S(1)}, f32[1,128]{1,0:T(1,128)S(1)}, u32[]{:S(2)}, u32[]{:S(2)}) collective-permute-start(f32[1,128]{1,0:T(1,128)S(1)} %add.24), channel_id=1, source_target_pairs={{0,16},{4,20},{8,24},{12,28},{16,0},{20,4},{24,8},{28,12},{1,17},{... | collective-permute-start | bytes 1544 | tf_op jit(solution)/shard_map/ppermute | solution.py:315
  118.1 1.9 %collective-permute-done.20 = f32[1,128]{1,0:T(1,128)S(1)} collective-permute-done((f32[1,128]{1,0:T(1,128)S(1)}, f32[1,128]{1,0:T(1,128)S(1)}, u32[]{:S(2)}, u32[]{:S(2)}) %collective-permute-start.20) | collective-permute-done | bytes 544 | tf_op jit(solution)/shard_map/ppermute | solution.py:315
  120.0 1.1 collective-permute-done.21
  121.1 1.5 %collective-permute-start.22 = (f32[1,128]{1,0:T(1,128)S(1)}, f32[1,128]{1,0:T(1,128)S(1)}, u32[]{:S(2)}, u32[]{:S(2)}) collective-permute-start(f32[1,128]{1,0:T(1,128)S(1)} %add.26), channel_id=1, source_target_pairs={{0,2},{1,3},{2,0},{3,1},{4,6},{5,7},{6,4},{7,5},{8,10},{9,11},{10,... | collective-permute-start | bytes 1544 | tf_op jit(solution)/shard_map/ppermute | solution.py:315
  122.6 2.0 %collective-permute-done.22 = f32[1,128]{1,0:T(1,128)S(1)} collective-permute-done((f32[1,128]{1,0:T(1,128)S(1)}, f32[1,128]{1,0:T(1,128)S(1)}, u32[]{:S(2)}, u32[]{:S(2)}) %collective-permute-start.22) | collective-permute-done | bytes 544 | tf_op jit(solution)/shard_map/ppermute | solution.py:315
  124.6 0.8 collective-permute-start.23
  125.4 1.2 collective-permute-start.16
  126.7 6.8 %collective-permute-done.23 = f32[1,128]{1,0:T(1,128)S(1)} collective-permute-done((f32[1,128]{1,0:T(1,128)S(1)}, f32[1,128]{1,0:T(1,128)S(1)}, u32[]{:S(2)}, u32[]{:S(2)}) %collective-permute-start.23) | collective-permute-done | bytes 544 | tf_op jit(solution)/shard_map/ppermute | solution.py:315
  133.9 1.5 %place_columns.6.refs_0_ = bf16[2,128,8192]{2,1,0:T(8,128)(2,1)} custom-call(s32[3]{0:T(128)S(1)} %pad_add_fusion.info.refs_0_, bf16[2,128,1024]{2,1,0:T(8,128)(2,1)S(1)} %get-tuple-element.55.here, bf16[2,128,1024]{2,1,0:T(8,128)(2,1)S(1)} %collective-permute-done.17.there, bf16[2,128,8192]{2,1,0:T(8,128)(2,1)} %place_columns.5.refs_0_), custom_call_target="tpu_custom_call", output_to_operand_aliasing={{}: (3, {})} | custom-call | tf_op jit(solution)/shard_map/place_columns/pallas_call | solution.py:94
  135.5 1.3 place_columns.7
  136.8 0.9 add_bitcast_fusion
  (38 shorter events, 3.4 us)
Async XLA Ops:
  0.7 2.2 %copy-start = (bf16[1,2,128,8192]{3,2,1,0:T(8,128)(2,1)S(1)}, bf16[1,2,128,8192]{3,2,1,0:T(8,128)(2,1)}, u32[]{:S(2)}) copy-start(bf16[1,2,128,8192]{3,2,1,0:T(8,128)(2,1)} %param.5) | copy-start | bytes 12582916
  3.5 9.7 %copy-start.5 = (s32[128]{0:T(128)S(1)}, s32[128]{0:T(128)}, u32[]{:S(2)}) copy-start(s32[128]{0:T(128)} %param.9) | copy-start | bytes 1540
  3.6 9.7 %copy-start.4 = (s32[128,8]{0,1:T(8,128)S(1)}, s32[128,8]{0,1:T(8,128)}, u32[]{:S(2)}) copy-start(s32[128,8]{0,1:T(8,128)} %param.8) | copy-start | bytes 12292
  3.6 29.6 %copy-start.3 = (bf16[1,2,128,640]{3,2,1,0:T(8,128)(2,1)S(1)}, bf16[1,2,128,640]{3,2,1,0:T(8,128)(2,1)}, u32[]{:S(2)}) copy-start(bf16[1,2,128,640]{3,2,1,0:T(8,128)(2,1)} %param.6) | copy-start | bytes 983044
  3.6 24.2 %collective-permute-start = (bf16[2,128,1792]{2,1,0:T(8,128)(2,1)S(1)}, bf16[2,128,1792]{2,1,0:T(8,128)(2,1)S(1)}, u32[]{:S(2)}, u32[]{:S(2)}) collective-permute-start(bf16[2,128,1792]{2,1,0:T(8,128)(2,1)S(1)} %split_columns.5), channel_id=1, source_target_pairs={{0,4},{4,0},{8,12},{12,8},{16,20},{20,16},{24,28},{28,24},{1,5},{5... | collective-permute-start | bytes 2752520 | tf_op jit(solution)/shard_map/ppermute | solution.py:343
  7.2 33.3 %collective-permute-start.6 = (bf16[2,128,1792]{2,1,0:T(8,128)(2,1)S(1)}, bf16[2,128,1792]{2,1,0:T(8,128)(2,1)S(1)}, u32[]{:S(2)}, u32[]{:S(2)}) collective-permute-start(bf16[2,128,1792]{2,1,0:T(8,128)(2,1)S(1)} %split_columns.7.refs_6_), channel_id=1, source_target_pairs={{0,8},{4,12},{8,16},{12,20},{16,24},{20,28},{1,9},{5,13},{9,17},{1... | collective-permute-start | bytes 2752520 | tf_op jit(solution)/shard_map/ppermute | solution.py:347
  10.8 30.8 %collective-permute-start.8 = (bf16[2,128,1792]{2,1,0:T(8,128)(2,1)S(1)}, bf16[2,128,1792]{2,1,0:T(8,128)(2,1)S(1)}, u32[]{:S(2)}, u32[]{:S(2)}) collective-permute-start(bf16[2,128,1792]{2,1,0:T(8,128)(2,1)S(1)} %split_columns.7.refs_6_), channel_id=1, source_target_pairs={{8,0},{12,4},{16,8},{20,12},{24,16},{28,20},{9,1},{13,5},{17,9},{2... | collective-permute-start | bytes 2752520 | tf_op jit(solution)/shard_map/ppermute | solution.py:347
  12.7 25.5 %collective-permute-start.3 = (bf16[2,128,1024]{2,1,0:T(8,128)(2,1)S(1)}, bf16[2,128,1024]{2,1,0:T(8,128)(2,1)S(1)}, u32[]{:S(2)}, u32[]{:S(2)}) collective-permute-start(bf16[2,128,1024]{2,1,0:T(8,128)(2,1)S(1)} %split_columns.6), channel_id=1, source_target_pairs={{0,4},{4,0},{8,12},{12,8},{16,20},{20,16},{24,28},{28,24},{1,5},{5... | collective-permute-start | bytes 1572872 | tf_op jit(solution)/shard_map/ppermute | solution.py:343
  27.8 24.8 %collective-permute-start.7 = (bf16[2,128,1792]{2,1,0:T(8,128)(2,1)S(1)}, bf16[2,128,1792]{2,1,0:T(8,128)(2,1)S(1)}, u32[]{:S(2)}, u32[]{:S(2)}) collective-permute-start(bf16[2,128,1792]{2,1,0:T(8,128)(2,1)S(1)} %collective-permute-done.refs_7_), channel_id=1, source_target_pairs={{0,8},{4,12},{8,16},{12,20},{16,24},{20,28},{1,9},{5,13},{9,17},{1... | collective-permute-start | bytes 2752520 | tf_op jit(solution)/shard_map/ppermute | solution.py:347
  31.9 25.2 %collective-permute-start.9 = (bf16[2,128,1792]{2,1,0:T(8,128)(2,1)S(1)}, bf16[2,128,1792]{2,1,0:T(8,128)(2,1)S(1)}, u32[]{:S(2)}, u32[]{:S(2)}) collective-permute-start(bf16[2,128,1792]{2,1,0:T(8,128)(2,1)S(1)} %collective-permute-done.refs_7_), channel_id=1, source_target_pairs={{8,0},{12,4},{16,8},{20,12},{24,16},{28,20},{9,1},{13,5},{17,9},{2... | collective-permute-start | bytes 2752520 | tf_op jit(solution)/shard_map/ppermute | solution.py:347
  38.2 11.1 %collective-permute-start.2 = (bf16[272,640]{1,0:T(8,128)(2,1)S(1)}, bf16[272,640]{1,0:T(8,128)(2,1)S(1)}, u32[]{:S(2)}, u32[]{:S(2)}) collective-permute-start(bf16[272,640]{1,0:T(8,128)(2,1)S(1)} %pad_maximum_fusion.own), channel_id=1, source_target_pairs={{0,4},{4,0},{8,12},{12,8},{16,20},{20,16},{24,28},{28,24},{1,5},{5... | collective-permute-start | bytes 1044488 | tf_op jit(solution)/shard_map/ppermute | solution.py:343
  40.5 16.5 %copy-start.2 = (f32[1,2]{1,0:T(1,128)S(1)}, f32[1,2]{1,0:T(1,128)}, u32[]{:S(2)}) copy-start(f32[1,2]{1,0:T(1,128)} %param.7) | copy-start | bytes 28
  40.6 26.0 %collective-permute-start.1 = (bf16[2,128,1280]{2,1,0:T(8,128)(2,1)S(1)}, bf16[2,128,1280]{2,1,0:T(8,128)(2,1)S(1)}, u32[]{:S(2)}, u32[]{:S(2)}) collective-permute-start(bf16[2,128,1280]{2,1,0:T(8,128)(2,1)S(1)} %split_columns.4), channel_id=1, source_target_pairs={{0,4},{4,0},{8,12},{12,8},{16,20},{20,16},{24,28},{28,24},{1,5},{5... | collective-permute-start | bytes 1966088 | tf_op jit(solution)/shard_map/ppermute | solution.py:343
  41.6 25.0 %copy-start.1 = (bf16[1,2,128,8192]{3,2,1,0:T(8,128)(2,1)S(1)}, bf16[1,2,128,8192]{3,2,1,0:T(8,128)(2,1)}, u32[]{:S(2)}) copy-start(bf16[1,2,128,8192]{3,2,1,0:T(8,128)(2,1)} %param.5) | copy-start | bytes 12582916
  41.6 33.5 %collective-permute-start.4 = (bf16[2,2,128,1024]{3,2,1,0:T(8,128)(2,1)S(1)}, bf16[2,2,128,1024]{3,2,1,0:T(8,128)(2,1)S(1)}, u32[]{:S(2)}, u32[]{:S(2)}) collective-permute-start(bf16[2,2,128,1024]{3,2,1,0:T(8,128)(2,1)S(1)} %join_blocks.3.refs_4_), channel_id=1, source_target_pairs={{0,8},{4,12},{8,16},{12,20},{16,24},{20,28},{1,9},{5,13},{9,17},{1... | collective-permute-start | bytes 3145736 | tf_op jit(solution)/shard_map/ppermute | solution.py:347
  49.3 30.3 %collective-permute-start.5 = (bf16[2,2,128,1024]{3,2,1,0:T(8,128)(2,1)S(1)}, bf16[2,2,128,1024]{3,2,1,0:T(8,128)(2,1)S(1)}, u32[]{:S(2)}, u32[]{:S(2)}) collective-permute-start(bf16[2,2,128,1024]{3,2,1,0:T(8,128)(2,1)S(1)} %join_blocks.3.refs_4_), channel_id=1, source_target_pairs={{8,0},{12,4},{16,8},{20,12},{24,16},{28,20},{9,1},{13,5},{17,9},{2... | collective-permute-start | bytes 3145736 | tf_op jit(solution)/shard_map/ppermute | solution.py:347
  66.5 23.0 %collective-permute-start.11 = (bf16[2,128,1792]{2,1,0:T(8,128)(2,1)S(1)}, bf16[2,128,1792]{2,1,0:T(8,128)(2,1)S(1)}, u32[]{:S(2)}, u32[]{:S(2)}) collective-permute-start(bf16[2,128,1792]{2,1,0:T(8,128)(2,1)S(1)} %get-tuple-element.44), channel_id=1, source_target_pairs={{0,4},{4,0},{8,12},{12,8},{16,20},{20,16},{24,28},{28,24},{1,5},{5... | collective-permute-start | bytes 2752520 | tf_op jit(solution)/shard_map/ppermute | solution.py:343
  67.3 30.2 %collective-permute-start.14 = (bf16[2,2,128,1024]{3,2,1,0:T(8,128)(2,1)S(1)}, bf16[2,2,128,1024]{3,2,1,0:T(8,128)(2,1)S(1)}, u32[]{:S(2)}, u32[]{:S(2)}) collective-permute-start(bf16[2,2,128,1024]{3,2,1,0:T(8,128)(2,1)S(1)} %get-tuple-element.33.refs_4_), channel_id=1, source_target_pairs={{0,8},{4,12},{8,16},{12,20},{16,24},{20,28},{1,9},{5,13},{9,17},{1... | collective-permute-start | bytes 3145736 | tf_op jit(solution)/shard_map/ppermute | solution.py:347
  72.2 29.4 %collective-permute-start.15 = (bf16[2,2,128,1024]{3,2,1,0:T(8,128)(2,1)S(1)}, bf16[2,2,128,1024]{3,2,1,0:T(8,128)(2,1)S(1)}, u32[]{:S(2)}, u32[]{:S(2)}) collective-permute-start(bf16[2,2,128,1024]{3,2,1,0:T(8,128)(2,1)S(1)} %get-tuple-element.33.refs_4_), channel_id=1, source_target_pairs={{8,0},{12,4},{16,8},{20,12},{24,16},{28,20},{9,1},{13,5},{17,9},{2... | collective-permute-start | bytes 3145736 | tf_op jit(solution)/shard_map/ppermute | solution.py:347
  85.3 9.2 %collective-permute-start.10 = (bf16[2,128,1024]{2,1,0:T(8,128)(2,1)S(1)}, bf16[2,128,1024]{2,1,0:T(8,128)(2,1)S(1)}, u32[]{:S(2)}, u32[]{:S(2)}) collective-permute-start(bf16[2,128,1024]{2,1,0:T(8,128)(2,1)S(1)} %get-tuple-element.42), channel_id=1, source_target_pairs={{0,4},{4,0},{8,12},{12,8},{16,20},{20,16},{24,28},{28,24},{1,5},{5... | collective-permute-start | bytes 1572872 | tf_op jit(solution)/shard_map/ppermute | solution.py:343
  85.7 21.8 %collective-permute-start.12 = (bf16[2,2,128,256]{3,2,1,0:T(8,128)(2,1)S(1)}, bf16[2,2,128,256]{3,2,1,0:T(8,128)(2,1)S(1)}, u32[]{:S(2)}, u32[]{:S(2)}) collective-permute-start(bf16[2,2,128,256]{3,2,1,0:T(8,128)(2,1)S(1)} %get-tuple-element.45.refs_4_), channel_id=1, source_target_pairs={{0,8},{4,12},{8,16},{12,20},{16,24},{20,28},{1,9},{5,13},{9,17},{1... | collective-permute-start | bytes 786440 | tf_op jit(solution)/shard_map/ppermute | solution.py:347
  89.4 18.0 %collective-permute-start.13 = (bf16[2,2,128,256]{3,2,1,0:T(8,128)(2,1)S(1)}, bf16[2,2,128,256]{3,2,1,0:T(8,128)(2,1)S(1)}, u32[]{:S(2)}, u32[]{:S(2)}) collective-permute-start(bf16[2,2,128,256]{3,2,1,0:T(8,128)(2,1)S(1)} %get-tuple-element.45.refs_4_), channel_id=1, source_target_pairs={{8,0},{12,4},{16,8},{20,12},{24,16},{28,20},{9,1},{13,5},{17,9},{2... | collective-permute-start | bytes 786440 | tf_op jit(solution)/shard_map/ppermute | solution.py:347
  109.9 26.9 %collective-permute-start.18 = (f32[2,128,640]{2,1,0:T(8,128)S(1)}, f32[2,128,640]{2,1,0:T(8,128)S(1)}, u32[]{:S(2)}, u32[]{:S(2)}) collective-permute-start(f32[2,128,640]{2,1,0:T(8,128)S(1)} %get-tuple-element.59), channel_id=1, source_target_pairs={{0,4},{4,0},{8,12},{12,8},{16,20},{20,16},{24,28},{28,24},{1,5},{5... | collective-permute-start | bytes 1966088 | tf_op jit(solution)/shard_map/ppermute | solution.py:343
  110.0 24.0 %collective-permute-start.17 = (bf16[2,128,1024]{2,1,0:T(8,128)(2,1)S(1)}, bf16[2,128,1024]{2,1,0:T(8,128)(2,1)S(1)}, u32[]{:S(2)}, u32[]{:S(2)}) collective-permute-start(bf16[2,128,1024]{2,1,0:T(8,128)(2,1)S(1)} %get-tuple-element.56), channel_id=1, source_target_pairs={{0,4},{4,0},{8,12},{12,8},{16,20},{20,16},{24,28},{28,24},{1,5},{5... | collective-permute-start | bytes 1572872 | tf_op jit(solution)/shard_map/ppermute | solution.py:343
  112.0 3.5 %collective-permute-start.19 = (f32[1,128]{1,0:T(1,128)S(1)}, f32[1,128]{1,0:T(1,128)S(1)}, u32[]{:S(2)}, u32[]{:S(2)}) collective-permute-start(f32[1,128]{1,0:T(1,128)S(1)} %get-tuple-element.60), channel_id=1, source_target_pairs={{0,8},{4,12},{8,0},{12,4},{16,24},{20,28},{24,16},{28,20},{1,9},{5... | collective-permute-start | bytes 1544 | tf_op jit(solution)/shard_map/ppermute | solution.py:315
  115.5 4.4 %collective-permute-start.20 = (f32[1,128]{1,0:T(1,128)S(1)}, f32[1,128]{1,0:T(1,128)S(1)}, u32[]{:S(2)}, u32[]{:S(2)}) collective-permute-start(f32[1,128]{1,0:T(1,128)S(1)} %add.24), channel_id=1, source_target_pairs={{0,16},{4,20},{8,24},{12,28},{16,0},{20,4},{24,8},{28,12},{1,17},{... | collective-permute-start | bytes 1544 | tf_op jit(solution)/shard_map/ppermute | solution.py:315
  120.0 1.1 collective-permute-start.21
  121.1 3.5 %collective-permute-start.22 = (f32[1,128]{1,0:T(1,128)S(1)}, f32[1,128]{1,0:T(1,128)S(1)}, u32[]{:S(2)}, u32[]{:S(2)}) collective-permute-start(f32[1,128]{1,0:T(1,128)S(1)} %add.26), channel_id=1, source_target_pairs={{0,2},{1,3},{2,0},{3,1},{4,6},{5,7},{6,4},{7,5},{8,10},{9,11},{10,... | collective-permute-start | bytes 1544 | tf_op jit(solution)/shard_map/ppermute | solution.py:315
  124.6 8.8 %collective-permute-start.23 = (f32[1,128]{1,0:T(1,128)S(1)}, f32[1,128]{1,0:T(1,128)S(1)}, u32[]{:S(2)}, u32[]{:S(2)}) collective-permute-start(f32[1,128]{1,0:T(1,128)S(1)} %add.27), channel_id=1, source_target_pairs={{0,4},{4,0},{8,12},{12,8},{16,20},{20,16},{24,28},{28,24},{1,5},{5... | collective-permute-start | bytes 1544 | tf_op jit(solution)/shard_map/ppermute | solution.py:315
  125.4 10.0 %collective-permute-start.16 = (bf16[2,128,256]{2,1,0:T(8,128)(2,1)S(1)}, bf16[2,128,256]{2,1,0:T(8,128)(2,1)S(1)}, u32[]{:S(2)}, u32[]{:S(2)}) collective-permute-start(bf16[2,128,256]{2,1,0:T(8,128)(2,1)S(1)} %get-tuple-element.54), channel_id=1, source_target_pairs={{0,4},{4,0},{8,12},{12,8},{16,20},{20,16},{24,28},{28,24},{1,5},{5... | collective-permute-start | bytes 393224 | tf_op jit(solution)/shard_map/ppermute | solution.py:343

commit v6 on v5

--- a/solution.py
+++ b/solution.py
@@ -77,31 +77,33 @@
     )(info, whole, theirs)
 
 
-def place_kernel(half, off, size, info, here, there, *refs):
-    whole, sems = refs[-2:]
+def place_kernel(half, cuts, info, *refs):
+    parts, whole, sems = refs[: 2 * len(cuts)], refs[-2], refs[-1]
     side = info[0]
-    run(
-        [
-            pltpu.make_async_copy(here, columns(whole, side * half + off, size), sems.at[0]),
-            pltpu.make_async_copy(there, columns(whole, (1 - side) * half + off, size), sems.at[1]),
-        ]
-    )
-
-
-def place(info, here, there, whole, half, off):
-    _, rows, size = here.shape
+    copies = []
+    for n, (off, size) in enumerate(cuts):
+        for m, at in ((2 * n, side), (2 * n + 1, 1 - side)):
+            to = columns(whole, at * half + off, size)
+            copies.append(pltpu.make_async_copy(parts[m], to, sems.at[m]))
+    run(copies)
+
+
+def place(info, pieces, whole, half):
+    rows = pieces[0][0].shape[1]
     first = whole is None
+    cuts = [(off, here.shape[2]) for here, _, off in pieces]
+    parts = [part for here, there, _ in pieces for part in (here, there)]
     return pl.pallas_call(
-        functools.partial(place_kernel, half, off, size),
-        out_shape=jax.ShapeDtypeStruct((2, rows, 2 * half), here.dtype),
-        in_specs=[IN_SMEM, IN_VMEM, IN_VMEM] + ([] if first else [IN_HBM]),
+        functools.partial(place_kernel, half, cuts),
+        out_shape=jax.ShapeDtypeStruct((2, rows, 2 * half), parts[0].dtype),
+        in_specs=[IN_SMEM] + [IN_VMEM] * len(parts) + ([] if first else [IN_HBM]),
         out_specs=IN_HBM,
-        scratch_shapes=[pltpu.SemaphoreType.DMA((2,))],
-        input_output_aliases={} if first else {3: 0},
+        scratch_shapes=[pltpu.SemaphoreType.DMA((len(parts),))],
+        input_output_aliases={} if first else {1 + len(parts): 0},
         compiler_params=PARAMS,
         cost_estimate=LIGHT,
         name="place_columns",
-    )(info, here, there, *([] if first else [whole]))
+    )(info, *parts, *([] if first else [whole]))
 
 
 def prepare_kernel(info, own, mate, resp, mask):
@@ -379,8 +381,7 @@
             ahead = neighbours(both[n + 1])
         gate = list(both[n + 1 : n + 2])
         if n >= 2:
-            here, back, at = sent[n - 2]
-            whole = place(info, here, back, whole, half, at)
+            whole = place(info, sent[n - 2 : n - 1], whole, half)
             info_now, whole = lax.optimization_barrier((info, whole, *gate))[:2]
         else:
             info_now = after(info, *gate)
@@ -393,8 +394,7 @@
         if n + 1 < steps:
             arrays = [both[n + 1], *ahead]
             layout = ((1, 0), (1, 1), (0, 0), (0, 1), (2, 0), (2, 1))
-    for here, back, at in sent[-2:]:
-        whole = place(info, here, back, whole, half, at)
+    whole = place(info, sent[-2:], whole, half)
     gradient = grad[0] + swap(grad[1])
     if shots & (shots - 1) or freqs & (freqs - 1):
         total = lax.psum(corr, ("shot", "freq"))

time: 138 us -> 138 us (level)
    pallas_call x4 -> x3, Pallas kernels: 6.11 us -> 4.94 us  [place(): pl.pallas_call(functools.partial(place_kernel, half, cuts), out_shape=jax...]
  transfers between devices with their start and end apart: 24 -> 24, of which waited for: 15 -> 15; matrix products, arithmetic and copies ran while one was open for 0% -> 0% of each run, Pallas kernels for 23% -> 22%
where the time goes in v6:
time: 138 us; the launch traced here: 137 us
  waiting for transfers between devices  56.1 us (41%)
  starting transfers between devices  43.4 us (31%)
  Pallas kernels  33 us (24%)
  local copies, waits for them, and re-layouts  2.22 us (2%)
  other arithmetic  1.6 us (1%)
    ppermute x10, starting transfers between devices, neighbours(): lax.ppermute(a, 'shot', [(s, s + d) for s in range(shots) if 0 <= s + d <...  27.6 us
    ppermute x9, waiting for transfers between devices, swap(): return lax.ppermute(a, 'shot', [(s, s ^ 1) for s in range(shots)])  25.7 us
    pallas_call x4, Pallas kernels, chunk(): pl.pallas_call(functools.partial(chunk_kernel, conf), out_shape=out_shape...  23.5 us
    ppermute x10, waiting for transfers between devices, neighbours(): lax.ppermute(a, 'shot', [(s, s + d) for s in range(shots) if 0 <= s + d <...  16.6 us
    ppermute x5, waiting for transfers between devices, total_over(): lax.ppermute(value, axis, [(i, i ^ step) for i in range(size)])  13.8 us
    ppermute x9, starting transfers between devices, swap(): return lax.ppermute(a, 'shot', [(s, s ^ 1) for s in range(shots)])  9.41 us
    ppermute x5, starting transfers between devices, total_over(): lax.ppermute(value, axis, [(i, i ^ step) for i in range(size)])  6.36 us
    pallas_call x3, Pallas kernels, place(): pl.pallas_call(functools.partial(place_kernel, half, cuts), out_shape=jax...  4.94 us
  transfers between devices with their start and end apart: 24, of which 15 were waited for; matrix products, arithmetic and copies ran while one was open for 0% of the time, Pallas kernels for 22%

profile of v6, /device:TPU:0, one launch (start us, length us, event | category | flops | bytes accessed | tf_op | source)
XLA Modules:
  0.0 137.4 jit_solution(9088505880516192441)
XLA Ops:
  0.7 2.2 %copy-done = bf16[1,2,128,8192]{3,2,1,0:T(8,128)(2,1)S(1)} copy-done((bf16[1,2,128,8192]{3,2,1,0:T(8,128)(2,1)S(1)}, bf16[1,2,128,8192]{3,2,1,0:T(8,128)(2,1)}, u32[]{:S(2)}) %copy-start) | copy-done | bytes 4194328
  2.9 0.6 split_columns.5
  3.6 3.0 %collective-permute-start.1 = (bf16[2,128,1792]{2,1,0:T(8,128)(2,1)S(1)}, bf16[2,128,1792]{2,1,0:T(8,128)(2,1)S(1)}, u32[]{:S(2)}, u32[]{:S(2)}) collective-permute-start(bf16[2,128,1792]{2,1,0:T(8,128)(2,1)S(1)} %split_columns.5), channel_id=1, source_target_pairs={{0,4},{4,0},{8,12},{12,8},{16,20},{20,16},{24,28},{28,24},{1,5},{5... | collective-permute-start | bytes 2752520 | tf_op jit(solution)/shard_map/ppermute | solution.py:345
  6.6 0.6 split_columns.6.refs_6_
  7.2 3.5 %collective-permute-start.3 = (bf16[2,128,1792]{2,1,0:T(8,128)(2,1)S(1)}, bf16[2,128,1792]{2,1,0:T(8,128)(2,1)S(1)}, u32[]{:S(2)}, u32[]{:S(2)}) collective-permute-start(bf16[2,128,1792]{2,1,0:T(8,128)(2,1)S(1)} %split_columns.6.refs_6_), channel_id=1, source_target_pairs={{0,8},{4,12},{8,16},{12,20},{16,24},{20,28},{1,9},{5,13},{9,17},{1... | collective-permute-start | bytes 2752520 | tf_op jit(solution)/shard_map/ppermute | solution.py:349
  10.8 1.3 collective-permute-start.5
  13.3 14.4 %collective-permute-done.1.refs_7_ = bf16[2,128,1792]{2,1,0:T(8,128)(2,1)S(1)} collective-permute-done((bf16[2,128,1792]{2,1,0:T(8,128)(2,1)S(1)}, bf16[2,128,1792]{2,1,0:T(8,128)(2,1)S(1)}, u32[]{:S(2)}, u32[]{:S(2)}) %collective-permute-start.1) | collective-permute-done | bytes 917536 | tf_op jit(solution)/shard_map/ppermute | solution.py:345
  27.8 4.1 %collective-permute-start.4 = (bf16[2,128,1792]{2,1,0:T(8,128)(2,1)S(1)}, bf16[2,128,1792]{2,1,0:T(8,128)(2,1)S(1)}, u32[]{:S(2)}, u32[]{:S(2)}) collective-permute-start(bf16[2,128,1792]{2,1,0:T(8,128)(2,1)S(1)} %collective-permute-done.1.refs_7_), channel_id=1, source_target_pairs={{0,8},{4,12},{8,16},{12,20},{16,24},{20,28},{1,9},{5,13},{9,17},{1... | collective-permute-start | bytes 2752520 | tf_op jit(solution)/shard_map/ppermute | solution.py:349
  31.9 1.3 collective-permute-start.6
  33.2 4.9 %collective-permute-done.theirs = bf16[2,128,1024]{2,1,0:T(8,128)(2,1)S(1)} collective-permute-done((bf16[2,128,1024]{2,1,0:T(8,128)(2,1)S(1)}, bf16[2,128,1024]{2,1,0:T(8,128)(2,1)S(1)}, u32[]{:S(2)}, u32[]{:S(2)}) %collective-permute-start) | collective-permute-done | bytes 524320 | tf_op jit(solution)/shard_map/ppermute | solution.py:345
  38.2 1.7 %collective-permute-start.2 = (bf16[272,640]{1,0:T(8,128)(2,1)S(1)}, bf16[272,640]{1,0:T(8,128)(2,1)S(1)}, u32[]{:S(2)}, u32[]{:S(2)}) collective-permute-start(bf16[272,640]{1,0:T(8,128)(2,1)S(1)} %pad_maximum_fusion.own), channel_id=1, source_target_pairs={{0,4},{4,0},{8,12},{12,8},{16,20},{20,16},{24,28},{28,24},{1,5},{5... | collective-permute-start | bytes 1044488 | tf_op jit(solution)/shard_map/ppermute | solution.py:345
  39.9 0.6 split_columns.7
  40.9 0.6 join_blocks.2.refs_4_
  41.6 4.1 %collective-permute-start.11 = (bf16[2,2,128,1024]{3,2,1,0:T(8,128)(2,1)S(1)}, bf16[2,2,128,1024]{3,2,1,0:T(8,128)(2,1)S(1)}, u32[]{:S(2)}, u32[]{:S(2)}) collective-permute-start(bf16[2,2,128,1024]{3,2,1,0:T(8,128)(2,1)S(1)} %join_blocks.2.refs_4_), channel_id=1, source_target_pairs={{0,8},{4,12},{8,16},{12,20},{16,24},{20,28},{1,9},{5,13},{9,17},{1... | collective-permute-start | bytes 3145736 | tf_op jit(solution)/shard_map/ppermute | solution.py:349
  45.7 3.6 %collective-permute-done.2.mate = bf16[272,640]{1,0:T(8,128)(2,1)S(1)} collective-permute-done((bf16[272,640]{1,0:T(8,128)(2,1)S(1)}, bf16[272,640]{1,0:T(8,128)(2,1)S(1)}, u32[]{:S(2)}, u32[]{:S(2)}) %collective-permute-start.2) | collective-permute-done | bytes 348192 | tf_op jit(solution)/shard_map/ppermute | solution.py:345
  49.3 1.3 collective-permute-start.12
  50.5 0.8 prepare_response.1
  51.3 1.3 collective-permute-done.4.refs_5_
  52.6 4.5 %collective-permute-done.6.refs_9_ = bf16[2,128,1792]{2,1,0:T(8,128)(2,1)S(1)} collective-permute-done((bf16[2,128,1792]{2,1,0:T(8,128)(2,1)S(1)}, bf16[2,128,1792]{2,1,0:T(8,128)(2,1)S(1)}, u32[]{:S(2)}, u32[]{:S(2)}) %collective-permute-start.6) | collective-permute-done | bytes 917536 | tf_op jit(solution)/shard_map/ppermute | solution.py:349
  57.1 9.4 %residual_chunk.4 = (bf16[2,128,1792]{2,1,0:T(8,128)(2,1)S(1)}, bf16[2,128,1792]{2,1,0:T(8,128)(2,1)S(1)}, f32[768,512]{1,0:T(8,128)S(1)}, f32[2,8,128]{2,1,0:T(8,128)S(1)}) custom-call(s32[3]{0:T(128)S(1)} %pad_add_fusion.info.refs_0_, f32[2]{0:T(128)S(1)} %bitcast.18, bf16[512,1536]{1,0:T(8,128)(2,1)S(1)} %get-tuple-element.34.refs_2_, ...), custom_call_target="tpu_custom_call" | custom-call | tf_op jit(solution)/shard_map/residual_chunk/pallas_call | solution.py:296
  66.6 0.7 join_blocks.3
  67.3 1.3 collective-permute-start.10
  68.6 5.6 %collective-permute-start.9 = (bf16[2,2,128,1024]{3,2,1,0:T(8,128)(2,1)S(1)}, bf16[2,2,128,1024]{3,2,1,0:T(8,128)(2,1)S(1)}, u32[]{:S(2)}, u32[]{:S(2)}) collective-permute-start(bf16[2,2,128,1024]{3,2,1,0:T(8,128)(2,1)S(1)} %get-tuple-element.41.refs_4_), channel_id=1, source_target_pairs={{0,8},{4,12},{8,16},{12,20},{16,24},{20,28},{1,9},{5,13},{9,17},{1... | collective-permute-start | bytes 3145736 | tf_op jit(solution)/shard_map/ppermute | solution.py:349
  74.2 0.9 collective-permute-done.11.refs_5_
  75.1 4.5 %collective-permute-done.12.refs_6_ = bf16[2,2,128,1024]{3,2,1,0:T(8,128)(2,1)S(1)} collective-permute-done((bf16[2,2,128,1024]{3,2,1,0:T(8,128)(2,1)S(1)}, bf16[2,2,128,1024]{3,2,1,0:T(8,128)(2,1)S(1)}, u32[]{:S(2)}, u32[]{:S(2)}) %collective-permute-start.12) | collective-permute-done | bytes 1048608 | tf_op jit(solution)/shard_map/ppermute | solution.py:349
  79.5 5.8 %residual_chunk.5 = (bf16[2,128,1024]{2,1,0:T(8,128)(2,1)S(1)}, bf16[2,128,1024]{2,1,0:T(8,128)(2,1)S(1)}, f32[768,512]{1,0:T(8,128)S(1)}, f32[2,8,128]{2,1,0:T(8,128)S(1)}) custom-call(s32[3]{0:T(128)S(1)} %pad_add_fusion.info.refs_0_, f32[2]{0:T(128)S(1)} %bitcast.19, ...), custom_call_target="tpu_custom_call", output_to_operand_aliasing={{2}: (7, {}), {3}: (8, {})} | custom-call | tf_op jit(solution)/shard_map/residual_chunk/pallas_call | solution.py:296
  85.7 3.7 %collective-permute-start.15 = (bf16[2,2,128,256]{3,2,1,0:T(8,128)(2,1)S(1)}, bf16[2,2,128,256]{3,2,1,0:T(8,128)(2,1)S(1)}, u32[]{:S(2)}, u32[]{:S(2)}) collective-permute-start(bf16[2,2,128,256]{3,2,1,0:T(8,128)(2,1)S(1)} %get-tuple-element.39.refs_4_), channel_id=1, source_target_pairs={{0,8},{4,12},{8,16},{12,20},{16,24},{20,28},{1,9},{5,13},{9,17},{1... | collective-permute-start | bytes 786440 | tf_op jit(solution)/shard_map/ppermute | solution.py:349
  89.4 1.5 %collective-permute-start.16 = (bf16[2,2,128,256]{3,2,1,0:T(8,128)(2,1)S(1)}, bf16[2,2,128,256]{3,2,1,0:T(8,128)(2,1)S(1)}, u32[]{:S(2)}, u32[]{:S(2)}) collective-permute-start(bf16[2,2,128,256]{3,2,1,0:T(8,128)(2,1)S(1)} %get-tuple-element.39.refs_4_), channel_id=1, source_target_pairs={{8,0},{12,4},{16,8},{20,12},{24,16},{28,20},{9,1},{13,5},{17,9},{2... | collective-permute-start | bytes 786440 | tf_op jit(solution)/shard_map/ppermute | solution.py:349
  90.9 1.8 %place_columns.3.refs_2_ = bf16[2,128,8192]{2,1,0:T(8,128)(2,1)} custom-call(s32[3]{0:T(128)S(1)} %pad_add_fusion.info.refs_0_, bf16[2,128,1792]{2,1,0:T(8,128)(2,1)S(1)} %get-tuple-element.36.refs_0_, bf16[2,128,1792]{2,1,0:T(8,128)(2,1)S(1)} %collective-permute-done.7.refs_1_), custom_call_target="tpu_custom_call" | custom-call | tf_op jit(solution)/shard_map/place_columns/pallas_call | solution.py:96
  92.7 1.9 %collective-permute-done.14.refs_1_ = bf16[2,128,1024]{2,1,0:T(8,128)(2,1)S(1)} collective-permute-done((bf16[2,128,1024]{2,1,0:T(8,128)(2,1)S(1)}, bf16[2,128,1024]{2,1,0:T(8,128)(2,1)S(1)}, u32[]{:S(2)}, u32[]{:S(2)}) %collective-permute-start.14) | collective-permute-done | bytes 524320 | tf_op jit(solution)/shard_map/ppermute | solution.py:345
  94.6 1.5 %place_columns.4.refs_4_ = bf16[2,128,8192]{2,1,0:T(8,128)(2,1)} custom-call(s32[3]{0:T(128)S(1)} %pad_add_fusion.info.refs_0_, bf16[2,128,1024]{2,1,0:T(8,128)(2,1)S(1)} %get-tuple-element.49.refs_0_, bf16[2,128,1024]{2,1,0:T(8,128)(2,1)S(1)} %collective-permute-done.14.refs_1_, ...), custom_call_target="tpu_custom_call", output_to_operand_aliasing={{}: (3, {})} | custom-call | tf_op jit(solution)/shard_map/place_columns/pallas_call | solution.py:96
  96.1 5.5 %collective-permute-done.10.refs_6_ = bf16[2,2,128,1024]{3,2,1,0:T(8,128)(2,1)S(1)} collective-permute-done((bf16[2,2,128,1024]{3,2,1,0:T(8,128)(2,1)S(1)}, bf16[2,2,128,1024]{3,2,1,0:T(8,128)(2,1)S(1)}, u32[]{:S(2)}, u32[]{:S(2)}) %collective-permute-start.10) | collective-permute-done | bytes 1048608 | tf_op jit(solution)/shard_map/ppermute | solution.py:349
  101.6 5.8 %residual_chunk.6 = (bf16[2,128,1024]{2,1,0:T(8,128)(2,1)S(1)}, bf16[2,128,1024]{2,1,0:T(8,128)(2,1)S(1)}, f32[768,512]{1,0:T(8,128)S(1)}, f32[2,8,128]{2,1,0:T(8,128)S(1)}) custom-call(s32[3]{0:T(128)S(1)} %pad_add_fusion.info.refs_0_, f32[2]{0:T(128)S(1)} %bitcast.20, ...), custom_call_target="tpu_custom_call", output_to_operand_aliasing={{2}: (7, {}), {3}: (8, {})} | custom-call | tf_op jit(solution)/shard_map/residual_chunk/pallas_call | solution.py:296
  107.5 2.4 %residual_chunk.7 = (bf16[2,128,256]{2,1,0:T(8,128)(2,1)S(1)}, bf16[2,128,256]{2,1,0:T(8,128)(2,1)S(1)}, f32[2,128,640]{2,1,0:T(8,128)S(1)}, f32[2,128,640]{2,1,0:T(8,128)S(1)}, f32[1,128]{1,0:T(1,128)S(1)}) custom-call(s32[3]{0:T(128)S(1)} %pad_add_fusion.info.refs_0_, f32[2]{0:T(128)S(1)} %bitcast.21, bf16[512,1536]{1,0:T(8,128)(2,1)S(1)} %get-tuple-element.34.refs_2_, ...), custom_call_target="tpu_custom_call" | custom-call | tf_op jit(solution)/shard_map/residual_chunk/pallas_call | solution.py:296
  110.0 2.0 %collective-permute-start.13 = (bf16[2,128,1024]{2,1,0:T(8,128)(2,1)S(1)}, bf16[2,128,1024]{2,1,0:T(8,128)(2,1)S(1)}, u32[]{:S(2)}, u32[]{:S(2)}) collective-permute-start(bf16[2,128,1024]{2,1,0:T(8,128)(2,1)S(1)} %get-tuple-element.48), channel_id=1, source_target_pairs={{0,4},{4,0},{8,12},{12,8},{16,20},{20,16},{24,28},{28,24},{1,5},{5... | collective-permute-start | bytes 1572872 | tf_op jit(solution)/shard_map/ppermute | solution.py:345
  112.0 1.5 %collective-permute-start.19 = (f32[1,128]{1,0:T(1,128)S(1)}, f32[1,128]{1,0:T(1,128)S(1)}, u32[]{:S(2)}, u32[]{:S(2)}) collective-permute-start(f32[1,128]{1,0:T(1,128)S(1)} %get-tuple-element.60), channel_id=1, source_target_pairs={{0,8},{4,12},{8,0},{12,4},{16,24},{20,28},{24,16},{28,20},{1,9},{5... | collective-permute-start | bytes 1544 | tf_op jit(solution)/shard_map/ppermute | solution.py:317
  113.5 2.0 %collective-permute-done.19 = f32[1,128]{1,0:T(1,128)S(1)} collective-permute-done((f32[1,128]{1,0:T(1,128)S(1)}, f32[1,128]{1,0:T(1,128)S(1)}, u32[]{:S(2)}, u32[]{:S(2)}) %collective-permute-start.19) | collective-permute-done | bytes 544 | tf_op jit(solution)/shard_map/ppermute | solution.py:317
  115.5 2.5 %collective-permute-start.20 = (f32[1,128]{1,0:T(1,128)S(1)}, f32[1,128]{1,0:T(1,128)S(1)}, u32[]{:S(2)}, u32[]{:S(2)}) collective-permute-start(f32[1,128]{1,0:T(1,128)S(1)} %add.24), channel_id=1, source_target_pairs={{0,16},{4,20},{8,24},{12,28},{16,0},{20,4},{24,8},{28,12},{1,17},{... | collective-permute-start | bytes 1544 | tf_op jit(solution)/shard_map/ppermute | solution.py:317
  118.1 1.9 %collective-permute-done.20 = f32[1,128]{1,0:T(1,128)S(1)} collective-permute-done((f32[1,128]{1,0:T(1,128)S(1)}, f32[1,128]{1,0:T(1,128)S(1)}, u32[]{:S(2)}, u32[]{:S(2)}) %collective-permute-start.20) | collective-permute-done | bytes 544 | tf_op jit(solution)/shard_map/ppermute | solution.py:317
  120.0 1.1 collective-permute-done.21
  121.1 1.5 %collective-permute-start.22 = (f32[1,128]{1,0:T(1,128)S(1)}, f32[1,128]{1,0:T(1,128)S(1)}, u32[]{:S(2)}, u32[]{:S(2)}) collective-permute-start(f32[1,128]{1,0:T(1,128)S(1)} %add.26), channel_id=1, source_target_pairs={{0,2},{1,3},{2,0},{3,1},{4,6},{5,7},{6,4},{7,5},{8,10},{9,11},{10,... | collective-permute-start | bytes 1544 | tf_op jit(solution)/shard_map/ppermute | solution.py:317
  122.6 2.0 %collective-permute-done.22 = f32[1,128]{1,0:T(1,128)S(1)} collective-permute-done((f32[1,128]{1,0:T(1,128)S(1)}, f32[1,128]{1,0:T(1,128)S(1)}, u32[]{:S(2)}, u32[]{:S(2)}) %collective-permute-start.22) | collective-permute-done | bytes 544 | tf_op jit(solution)/shard_map/ppermute | solution.py:317
  124.7 0.8 collective-permute-start.23
  125.5 1.2 collective-permute-start.17
  126.7 6.7 %collective-permute-done.23 = f32[1,128]{1,0:T(1,128)S(1)} collective-permute-done((f32[1,128]{1,0:T(1,128)S(1)}, f32[1,128]{1,0:T(1,128)S(1)}, u32[]{:S(2)}, u32[]{:S(2)}) %collective-permute-start.23) | collective-permute-done | bytes 544 | tf_op jit(solution)/shard_map/ppermute | solution.py:317
  133.9 0.8 collective-permute-done.17.refs_3_
  134.8 1.6 %place_columns.5 = bf16[2,128,8192]{2,1,0:T(8,128)(2,1)} custom-call(s32[3]{0:T(128)S(1)} %pad_add_fusion.info.refs_0_, bf16[2,128,1024]{2,1,0:T(8,128)(2,1)S(1)} %get-tuple-element.47.refs_0_, bf16[2,128,1024]{2,1,0:T(8,128)(2,1)S(1)} %collective-permute-done.13.refs_1_, ...), custom_call_target="tpu_custom_call", output_to_operand_aliasing={{}: (5, {})} | custom-call | tf_op jit(solution)/shard_map/place_columns/pallas_call | solution.py:96
  136.4 0.9 add_bitcast_fusion
  (37 shorter events, 2.8 us)
Async XLA Ops:
  0.7 2.2 %copy-start = (bf16[1,2,128,8192]{3,2,1,0:T(8,128)(2,1)S(1)}, bf16[1,2,128,8192]{3,2,1,0:T(8,128)(2,1)}, u32[]{:S(2)}) copy-start(bf16[1,2,128,8192]{3,2,1,0:T(8,128)(2,1)} %param.5) | copy-start | bytes 12582916
  3.5 9.7 %copy-start.5 = (s32[128]{0:T(128)S(1)}, s32[128]{0:T(128)}, u32[]{:S(2)}) copy-start(s32[128]{0:T(128)} %param.9) | copy-start | bytes 1540
  3.6 9.7 %copy-start.4 = (s32[128,8]{0,1:T(8,128)S(1)}, s32[128,8]{0,1:T(8,128)}, u32[]{:S(2)}) copy-start(s32[128,8]{0,1:T(8,128)} %param.8) | copy-start | bytes 12292
  3.6 29.6 %copy-start.3 = (bf16[1,2,128,640]{3,2,1,0:T(8,128)(2,1)S(1)}, bf16[1,2,128,640]{3,2,1,0:T(8,128)(2,1)}, u32[]{:S(2)}) copy-start(bf16[1,2,128,640]{3,2,1,0:T(8,128)(2,1)} %param.6) | copy-start | bytes 983044
  3.6 24.2 %collective-permute-start.1 = (bf16[2,128,1792]{2,1,0:T(8,128)(2,1)S(1)}, bf16[2,128,1792]{2,1,0:T(8,128)(2,1)S(1)}, u32[]{:S(2)}, u32[]{:S(2)}) collective-permute-start(bf16[2,128,1792]{2,1,0:T(8,128)(2,1)S(1)} %split_columns.5), channel_id=1, source_target_pairs={{0,4},{4,0},{8,12},{12,8},{16,20},{20,16},{24,28},{28,24},{1,5},{5... | collective-permute-start | bytes 2752520 | tf_op jit(solution)/shard_map/ppermute | solution.py:345
  7.2 33.3 %collective-permute-start.3 = (bf16[2,128,1792]{2,1,0:T(8,128)(2,1)S(1)}, bf16[2,128,1792]{2,1,0:T(8,128)(2,1)S(1)}, u32[]{:S(2)}, u32[]{:S(2)}) collective-permute-start(bf16[2,128,1792]{2,1,0:T(8,128)(2,1)S(1)} %split_columns.6.refs_6_), channel_id=1, source_target_pairs={{0,8},{4,12},{8,16},{12,20},{16,24},{20,28},{1,9},{5,13},{9,17},{1... | collective-permute-start | bytes 2752520 | tf_op jit(solution)/shard_map/ppermute | solution.py:349
  10.8 30.8 %collective-permute-start.5 = (bf16[2,128,1792]{2,1,0:T(8,128)(2,1)S(1)}, bf16[2,128,1792]{2,1,0:T(8,128)(2,1)S(1)}, u32[]{:S(2)}, u32[]{:S(2)}) collective-permute-start(bf16[2,128,1792]{2,1,0:T(8,128)(2,1)S(1)} %split_columns.6.refs_6_), channel_id=1, source_target_pairs={{8,0},{12,4},{16,8},{20,12},{24,16},{28,20},{9,1},{13,5},{17,9},{2... | collective-permute-start | bytes 2752520 | tf_op jit(solution)/shard_map/ppermute | solution.py:349
  12.7 25.5 %collective-permute-start = (bf16[2,128,1024]{2,1,0:T(8,128)(2,1)S(1)}, bf16[2,128,1024]{2,1,0:T(8,128)(2,1)S(1)}, u32[]{:S(2)}, u32[]{:S(2)}) collective-permute-start(bf16[2,128,1024]{2,1,0:T(8,128)(2,1)S(1)} %split_columns.4), channel_id=1, source_target_pairs={{0,4},{4,0},{8,12},{12,8},{16,20},{20,16},{24,28},{28,24},{1,5},{5... | collective-permute-start | bytes 1572872 | tf_op jit(solution)/shard_map/ppermute | solution.py:345
  27.8 24.8 %collective-permute-start.4 = (bf16[2,128,1792]{2,1,0:T(8,128)(2,1)S(1)}, bf16[2,128,1792]{2,1,0:T(8,128)(2,1)S(1)}, u32[]{:S(2)}, u32[]{:S(2)}) collective-permute-start(bf16[2,128,1792]{2,1,0:T(8,128)(2,1)S(1)} %collective-permute-done.1.refs_7_), channel_id=1, source_target_pairs={{0,8},{4,12},{8,16},{12,20},{16,24},{20,28},{1,9},{5,13},{9,17},{1... | collective-permute-start | bytes 2752520 | tf_op jit(solution)/shard_map/ppermute | solution.py:349
  31.9 25.2 %collective-permute-start.6 = (bf16[2,128,1792]{2,1,0:T(8,128)(2,1)S(1)}, bf16[2,128,1792]{2,1,0:T(8,128)(2,1)S(1)}, u32[]{:S(2)}, u32[]{:S(2)}) collective-permute-start(bf16[2,128,1792]{2,1,0:T(8,128)(2,1)S(1)} %collective-permute-done.1.refs_7_), channel_id=1, source_target_pairs={{8,0},{12,4},{16,8},{20,12},{24,16},{28,20},{9,1},{13,5},{17,9},{2... | collective-permute-start | bytes 2752520 | tf_op jit(solution)/shard_map/ppermute | solution.py:349
  38.2 11.1 %collective-permute-start.2 = (bf16[272,640]{1,0:T(8,128)(2,1)S(1)}, bf16[272,640]{1,0:T(8,128)(2,1)S(1)}, u32[]{:S(2)}, u32[]{:S(2)}) collective-permute-start(bf16[272,640]{1,0:T(8,128)(2,1)S(1)} %pad_maximum_fusion.own), channel_id=1, source_target_pairs={{0,4},{4,0},{8,12},{12,8},{16,20},{20,16},{24,28},{28,24},{1,5},{5... | collective-permute-start | bytes 1044488 | tf_op jit(solution)/shard_map/ppermute | solution.py:345
  40.5 16.5 %copy-start.2 = (f32[1,2]{1,0:T(1,128)S(1)}, f32[1,2]{1,0:T(1,128)}, u32[]{:S(2)}) copy-start(f32[1,2]{1,0:T(1,128)} %param.7) | copy-start | bytes 28
  40.6 26.0 %collective-permute-start.8 = (bf16[2,128,1280]{2,1,0:T(8,128)(2,1)S(1)}, bf16[2,128,1280]{2,1,0:T(8,128)(2,1)S(1)}, u32[]{:S(2)}, u32[]{:S(2)}) collective-permute-start(bf16[2,128,1280]{2,1,0:T(8,128)(2,1)S(1)} %split_columns.7), channel_id=1, source_target_pairs={{0,4},{4,0},{8,12},{12,8},{16,20},{20,16},{24,28},{28,24},{1,5},{5... | collective-permute-start | bytes 1966088 | tf_op jit(solution)/shard_map/ppermute | solution.py:345
  41.6 25.0 %copy-start.1 = (bf16[1,2,128,8192]{3,2,1,0:T(8,128)(2,1)S(1)}, bf16[1,2,128,8192]{3,2,1,0:T(8,128)(2,1)}, u32[]{:S(2)}) copy-start(bf16[1,2,128,8192]{3,2,1,0:T(8,128)(2,1)} %param.5) | copy-start | bytes 12582916
  41.6 33.5 %collective-permute-start.11 = (bf16[2,2,128,1024]{3,2,1,0:T(8,128)(2,1)S(1)}, bf16[2,2,128,1024]{3,2,1,0:T(8,128)(2,1)S(1)}, u32[]{:S(2)}, u32[]{:S(2)}) collective-permute-start(bf16[2,2,128,1024]{3,2,1,0:T(8,128)(2,1)S(1)} %join_blocks.2.refs_4_), channel_id=1, source_target_pairs={{0,8},{4,12},{8,16},{12,20},{16,24},{20,28},{1,9},{5,13},{9,17},{1... | collective-permute-start | bytes 3145736 | tf_op jit(solution)/shard_map/ppermute | solution.py:349
  49.3 30.3 %collective-permute-start.12 = (bf16[2,2,128,1024]{3,2,1,0:T(8,128)(2,1)S(1)}, bf16[2,2,128,1024]{3,2,1,0:T(8,128)(2,1)S(1)}, u32[]{:S(2)}, u32[]{:S(2)}) collective-permute-start(bf16[2,2,128,1024]{3,2,1,0:T(8,128)(2,1)S(1)} %join_blocks.2.refs_4_), channel_id=1, source_target_pairs={{8,0},{12,4},{16,8},{20,12},{24,16},{28,20},{9,1},{13,5},{17,9},{2... | collective-permute-start | bytes 3145736 | tf_op jit(solution)/shard_map/ppermute | solution.py:349
  66.5 23.0 %collective-permute-start.7 = (bf16[2,128,1792]{2,1,0:T(8,128)(2,1)S(1)}, bf16[2,128,1792]{2,1,0:T(8,128)(2,1)S(1)}, u32[]{:S(2)}, u32[]{:S(2)}) collective-permute-start(bf16[2,128,1792]{2,1,0:T(8,128)(2,1)S(1)} %get-tuple-element.37), channel_id=1, source_target_pairs={{0,4},{4,0},{8,12},{12,8},{16,20},{20,16},{24,28},{28,24},{1,5},{5... | collective-permute-start | bytes 2752520 | tf_op jit(solution)/shard_map/ppermute | solution.py:345
  67.3 34.3 %collective-permute-start.10 = (bf16[2,2,128,1024]{3,2,1,0:T(8,128)(2,1)S(1)}, bf16[2,2,128,1024]{3,2,1,0:T(8,128)(2,1)S(1)}, u32[]{:S(2)}, u32[]{:S(2)}) collective-permute-start(bf16[2,2,128,1024]{3,2,1,0:T(8,128)(2,1)S(1)} %get-tuple-element.41.refs_4_), channel_id=1, source_target_pairs={{8,0},{12,4},{16,8},{20,12},{24,16},{28,20},{9,1},{13,5},{17,9},{2... | collective-permute-start | bytes 3145736 | tf_op jit(solution)/shard_map/ppermute | solution.py:349
  68.6 33.1 %collective-permute-start.9 = (bf16[2,2,128,1024]{3,2,1,0:T(8,128)(2,1)S(1)}, bf16[2,2,128,1024]{3,2,1,0:T(8,128)(2,1)S(1)}, u32[]{:S(2)}, u32[]{:S(2)}) collective-permute-start(bf16[2,2,128,1024]{3,2,1,0:T(8,128)(2,1)S(1)} %get-tuple-element.41.refs_4_), channel_id=1, source_target_pairs={{0,8},{4,12},{8,16},{12,20},{16,24},{20,28},{1,9},{5,13},{9,17},{1... | collective-permute-start | bytes 3145736 | tf_op jit(solution)/shard_map/ppermute | solution.py:349
  85.3 9.2 %collective-permute-start.14 = (bf16[2,128,1024]{2,1,0:T(8,128)(2,1)S(1)}, bf16[2,128,1024]{2,1,0:T(8,128)(2,1)S(1)}, u32[]{:S(2)}, u32[]{:S(2)}) collective-permute-start(bf16[2,128,1024]{2,1,0:T(8,128)(2,1)S(1)} %get-tuple-element.50), channel_id=1, source_target_pairs={{0,4},{4,0},{8,12},{12,8},{16,20},{20,16},{24,28},{28,24},{1,5},{5... | collective-permute-start | bytes 1572872 | tf_op jit(solution)/shard_map/ppermute | solution.py:345
  85.7 21.8 %collective-permute-start.15 = (bf16[2,2,128,256]{3,2,1,0:T(8,128)(2,1)S(1)}, bf16[2,2,128,256]{3,2,1,0:T(8,128)(2,1)S(1)}, u32[]{:S(2)}, u32[]{:S(2)}) collective-permute-start(bf16[2,2,128,256]{3,2,1,0:T(8,128)(2,1)S(1)} %get-tuple-element.39.refs_4_), channel_id=1, source_target_pairs={{0,8},{4,12},{8,16},{12,20},{16,24},{20,28},{1,9},{5,13},{9,17},{1... | collective-permute-start | bytes 786440 | tf_op jit(solution)/shard_map/ppermute | solution.py:349
  89.4 18.0 %collective-permute-start.16 = (bf16[2,2,128,256]{3,2,1,0:T(8,128)(2,1)S(1)}, bf16[2,2,128,256]{3,2,1,0:T(8,128)(2,1)S(1)}, u32[]{:S(2)}, u32[]{:S(2)}) collective-permute-start(bf16[2,2,128,256]{3,2,1,0:T(8,128)(2,1)S(1)} %get-tuple-element.39.refs_4_), channel_id=1, source_target_pairs={{8,0},{12,4},{16,8},{20,12},{24,16},{28,20},{9,1},{13,5},{17,9},{2... | collective-permute-start | bytes 786440 | tf_op jit(solution)/shard_map/ppermute | solution.py:349
  109.9 26.5 %collective-permute-start.18 = (f32[2,128,640]{2,1,0:T(8,128)S(1)}, f32[2,128,640]{2,1,0:T(8,128)S(1)}, u32[]{:S(2)}, u32[]{:S(2)}) collective-permute-start(f32[2,128,640]{2,1,0:T(8,128)S(1)} %get-tuple-element.59), channel_id=1, source_target_pairs={{0,4},{4,0},{8,12},{12,8},{16,20},{20,16},{24,28},{28,24},{1,5},{5... | collective-permute-start | bytes 1966088 | tf_op jit(solution)/shard_map/ppermute | solution.py:345
  110.0 24.8 %collective-permute-start.13 = (bf16[2,128,1024]{2,1,0:T(8,128)(2,1)S(1)}, bf16[2,128,1024]{2,1,0:T(8,128)(2,1)S(1)}, u32[]{:S(2)}, u32[]{:S(2)}) collective-permute-start(bf16[2,128,1024]{2,1,0:T(8,128)(2,1)S(1)} %get-tuple-element.48), channel_id=1, source_target_pairs={{0,4},{4,0},{8,12},{12,8},{16,20},{20,16},{24,28},{28,24},{1,5},{5... | collective-permute-start | bytes 1572872 | tf_op jit(solution)/shard_map/ppermute | solution.py:345
  112.0 3.5 %collective-permute-start.19 = (f32[1,128]{1,0:T(1,128)S(1)}, f32[1,128]{1,0:T(1,128)S(1)}, u32[]{:S(2)}, u32[]{:S(2)}) collective-permute-start(f32[1,128]{1,0:T(1,128)S(1)} %get-tuple-element.60), channel_id=1, source_target_pairs={{0,8},{4,12},{8,0},{12,4},{16,24},{20,28},{24,16},{28,20},{1,9},{5... | collective-permute-start | bytes 1544 | tf_op jit(solution)/shard_map/ppermute | solution.py:317
  115.5 4.4 %collective-permute-start.20 = (f32[1,128]{1,0:T(1,128)S(1)}, f32[1,128]{1,0:T(1,128)S(1)}, u32[]{:S(2)}, u32[]{:S(2)}) collective-permute-start(f32[1,128]{1,0:T(1,128)S(1)} %add.24), channel_id=1, source_target_pairs={{0,16},{4,20},{8,24},{12,28},{16,0},{20,4},{24,8},{28,12},{1,17},{... | collective-permute-start | bytes 1544 | tf_op jit(solution)/shard_map/ppermute | solution.py:317
  120.0 1.1 collective-permute-start.21
  121.1 3.5 %collective-permute-start.22 = (f32[1,128]{1,0:T(1,128)S(1)}, f32[1,128]{1,0:T(1,128)S(1)}, u32[]{:S(2)}, u32[]{:S(2)}) collective-permute-start(f32[1,128]{1,0:T(1,128)S(1)} %add.26), channel_id=1, source_target_pairs={{0,2},{1,3},{2,0},{3,1},{4,6},{5,7},{6,4},{7,5},{8,10},{9,11},{10,... | collective-permute-start | bytes 1544 | tf_op jit(solution)/shard_map/ppermute | solution.py:317
  124.7 8.8 %collective-permute-start.23 = (f32[1,128]{1,0:T(1,128)S(1)}, f32[1,128]{1,0:T(1,128)S(1)}, u32[]{:S(2)}, u32[]{:S(2)}) collective-permute-start(f32[1,128]{1,0:T(1,128)S(1)} %add.27), channel_id=1, source_target_pairs={{0,4},{4,0},{8,12},{12,8},{16,20},{20,16},{24,28},{28,24},{1,5},{5... | collective-permute-start | bytes 1544 | tf_op jit(solution)/shard_map/ppermute | solution.py:317
  125.5 9.3 %collective-permute-start.17 = (bf16[2,128,256]{2,1,0:T(8,128)(2,1)S(1)}, bf16[2,128,256]{2,1,0:T(8,128)(2,1)S(1)}, u32[]{:S(2)}, u32[]{:S(2)}) collective-permute-start(bf16[2,128,256]{2,1,0:T(8,128)(2,1)S(1)} %get-tuple-element.56), channel_id=1, source_target_pairs={{0,4},{4,0},{8,12},{12,8},{16,20},{20,16},{24,28},{28,24},{1,5},{5... | collective-permute-start | bytes 393224 | tf_op jit(solution)/shard_map/ppermute | solution.py:345
